TPU v7x, 256 devices: a whole 4x4x8 slice. The times are simulated.
256 devices in a mesh: member: 8 (over z_lo, core), shard: 32 (over x, y, z_hi).
Axes of the slice: x: 4, y: 4, z: 8 (z_hi: 2, z_lo: 4; z = z_hi * 4 + z_lo), core: 2. Of those that a mesh axis runs over, the one named last changes fastest.
Arguments:
- latent: bfloat16 [8, 1024, 1024], P('member', 'shard'), may hold values from -6 to 6
- grid_embed: bfloat16 [8192, 1024], P('shard'), may hold values from -6 to 6
- edge_src: int32 [8192, 3], P('shard'), may hold values from 0 to 1023, as said below
- area: float32 [8192], P('shard'), may hold values from 0.15 to 27
- target: float32 [8192, 100], P('shard'), may hold values from -6 to 6
- w_query: bfloat16 [1024, 1024], replicated, may hold values from -0.1875 to 0.1875
- w_keyval: bfloat16 [1024, 2048], replicated, may hold values from -0.1875 to 0.1875
- w_head: bfloat16 [1024, 100], replicated, may hold values from -0.1875 to 0.1875
Outputs:
- loss: float32 [8], P('member')
- d_latent: float32 [8, 1024, 1024], P('member', 'shard')
- grad_query: float32 [1024, 1024], P('shard')
- grad_keyval: float32 [1024, 2048], P('shard')
- grad_head: float32 [1024, 100], P('shard')
Inputs may be any that keep to these rules, and one draw needn't show every extreme that they name: edge_src[g, k] is a node of the latent block of index g // 256 or of one of the two blocks beside it, cyclically, where block b holds nodes b * 32 to (b + 1) * 32 - 1.
All inputs are finite; a program needn't handle non-finite values.
Results may differ from a plain program's by a relative error of at most 0.035.
Values may be sent and summed in bfloat16 or wider, within the bound.
No kernel may reach another device: no remote copies, remote signals or barrier semaphores. Data moves between devices by JAX's collectives and lax.ppermute only.
A program may use at most 128 MiB of HBM per device.

v0:
```python
import math

import jax
import jax.numpy as jnp
from jax import lax
from jax.sharding import PartitionSpec as P

HEADS = 16
KNB = 3


def padded(cells, sides, width):
    for axis, dim in sides:
        count = lax.axis_size(axis)
        head = lax.slice_in_dim(cells, 0, width, axis=dim)
        tail = lax.slice_in_dim(cells, cells.shape[dim] - width, cells.shape[dim], axis=dim)
        cells = jnp.concatenate(
            [
                lax.ppermute(tail, axis, [(i, (i + 1) % count) for i in range(count)]),
                cells,
                lax.ppermute(head, axis, [((i + 1) % count, i) for i in range(count)]),
            ],
            axis=dim,
        )
    return cells


def from_behind(array, axis, by):
    devices = lax.axis_size(axis)
    return lax.ppermute(array, axis, [(i, (i + by) % devices) for i in range(devices)])


def normalize_heads(values):
    shaped = values.reshape(values.shape[:-1] + (HEADS, values.shape[-1] // HEADS))
    return shaped * lax.rsqrt(jnp.mean(shaped * shaped, -1, keepdims=True) + 1e-06)


def attend(query, table, source):
    width = query.shape[-1]
    size = width // HEADS
    picked = table[source]
    query_norm = normalize_heads(query)
    key_norm = normalize_heads(picked[..., :width])
    values = picked[..., width:].reshape(picked.shape[:2] + (HEADS, size))
    score = jnp.einsum("bhs,bkhs->bhk", query_norm, key_norm) * size ** (-0.5)
    expon = jnp.exp(score)
    weight = expon / jnp.sum(expon, -1, keepdims=True)
    return jnp.einsum("bhk,bkhs->bhs", weight, values).reshape(query.shape)


def layer_norm(hidden):
    center = hidden - jnp.mean(hidden, -1, keepdims=True)
    return center * lax.rsqrt(jnp.mean(center * center, -1, keepdims=True) + 1e-05)


def smooth_abs(delta):
    return jnp.sqrt(delta * delta + 0.0625)


def slope(delta):
    return delta / smooth_abs(delta)


def inner_rows(left, right):
    return lax.dot_general(
        left, right, (((0,), (0,)), ((), ())), preferred_element_type=jnp.float32
    )


def on_device(latent, grid_embed, edge_src, area, target, w_query, w_keyval, w_head):
    rows = grid_embed.shape[0]
    width = grid_embed.shape[1]
    nodes = latent.shape[1]
    shards = lax.axis_size("shard")
    members = lax.axis_size("member")
    own_latent = latent[0]
    here = lax.axis_index("shard")
    source = jnp.mod(edge_src - (here - 1) * nodes, shards * nodes)
    widened = padded(own_latent, (("shard", 0),), nodes)
    table_low = jnp.dot(widened, w_keyval, preferred_element_type=jnp.float32).astype(jnp.bfloat16)
    table = lax.optimization_barrier(table_low).astype(jnp.float32)
    block = math.gcd(rows, 512)
    blocks = rows // block
    query = jnp.dot(grid_embed, w_query, preferred_element_type=jnp.float32)
    query_blocks = query.reshape(blocks, block, width)
    source_blocks = source.reshape(blocks, block, KNB)
    mixed = lax.map(lambda pair: attend(pair[0], table, pair[1]), (query_blocks, source_blocks))
    hidden = grid_embed.astype(jnp.float32) + mixed.reshape(rows, width)
    normed = layer_norm(hidden).astype(jnp.bfloat16)
    preds = jnp.dot(normed, w_head, preferred_element_type=jnp.float32)
    variables = preds.shape[1]
    pair_scale = 1.0 / (members * (members - 1))
    divisor = rows * shards * variables
    empty = jnp.zeros(preds.shape, jnp.float32)
    carry = (empty, empty)
    delta = preds[None] - lax.all_gather(
        preds[None].astype(jnp.bfloat16), "member", axis=0, tiled=True
    ).astype(jnp.float32)
    pair_value = carry[0] + jnp.sum(smooth_abs(delta), 0)
    pair_slope = carry[1] + jnp.sum(slope(delta), 0)
    miss = preds - target
    weights = area[:, None]
    local_loss = jnp.sum(
        weights * (smooth_abs(miss) / members - 0.5 * pair_scale * (pair_value - 0.25))
    )
    loss = lax.psum(local_loss[None], "shard") / divisor
    d_pred = weights * (slope(miss) / members - pair_scale * pair_slope)
    d_outb = d_pred.astype(jnp.bfloat16)
    d_normed = jnp.dot(d_outb, w_head.T, preferred_element_type=jnp.float32)
    ignored, norm_back = jax.vjp(layer_norm, hidden)
    d_hidden = norm_back(d_normed)[0]

    def block_back(carry, items):
        query_part, source_part, d_part = items
        ignored_out, attend_back = jax.vjp(
            lambda qq, tt: attend(qq, tt, source_part), query_part, table
        )
        d_q, d_t = attend_back(d_part)
        return (carry + d_t, d_q)

    d_table, d_query = lax.scan(
        block_back,
        jnp.zeros(table.shape, jnp.float32),
        (query_blocks, source_blocks, d_hidden.reshape(blocks, block, width)),
    )
    d_queryb = d_query.reshape(rows, width).astype(jnp.bfloat16)
    from_upper = from_behind(d_table[:nodes].astype(jnp.bfloat16), "shard", -1).astype(jnp.float32)
    from_lower = from_behind(d_table[2 * nodes :].astype(jnp.bfloat16), "shard", 1).astype(
        jnp.float32
    )
    d_own = d_table[nodes : 2 * nodes] + from_upper + from_lower
    d_ownb = d_own.astype(jnp.bfloat16)
    d_latent = jnp.dot(d_ownb, w_keyval.T, preferred_element_type=jnp.float32)[None]
    scale = (members * rows * shards) ** (-0.5)
    pick = lambda data: data
    parts = [
        inner_rows(pick(grid_embed), d_queryb),
        inner_rows(pick(own_latent), d_ownb),
        inner_rows(pick(normed), d_outb),
    ]
    portion = lax.psum_scatter(
        (jnp.concatenate(parts, axis=1) * scale).astype(jnp.bfloat16),
        "shard",
        scatter_dimension=0,
        tiled=True,
    )
    total = lax.psum(portion, "member").astype(jnp.float32)
    return (loss, d_latent, total[:, :width], total[:, width : 3 * width], total[:, 3 * width :])


def solution(mesh):
    placed = (
        P("member", "shard", None),
        P("shard", None),
        P("shard", None),
        P("shard"),
        P("shard", None),
        P(),
        P(),
        P(),
    )
    return jax.shard_map(
        on_device,
        mesh=mesh,
        in_specs=placed,
        out_specs=(
            P("member"),
            P("member", "shard", None),
            P("shard", None),
            P("shard", None),
            P("shard", None),
        ),
        check_vma=False,
    )
```

profile of v0, /device:TPU:1, one launch (start us, length us, event | category | flops | bytes accessed | tf_op | source)
XLA Modules:
  0.0 572.5 jit_solution(10662145856981593402)
XLA Ops:
  7.2 12.5 %collective-permute-start.1 = (bf16[32,1024]{1,0:T(8,128)(2,1)}, bf16[32,1024]{1,0:T(8,128)(2,1)S(1)}, u32[]{:S(2)}, u32[]{:S(2)}) collective-permute-start(bf16[32,1024]{1,0:T(8,128)(2,1)} %bitcast.80), channel_id=1, source_target_pairs={{1,0},{2,1},{3,2},{4,3},{5,4},{6,5},{7,6},{8,7},{9,8},{10,9},{11,1... | collective-permute-start | bytes 196616 | tf_op jit(solution)/shard_map/ppermute | solution.py:21
  24.1 7.5 %collective-permute-done = bf16[32,1024]{1,0:T(8,128)(2,1)S(1)} collective-permute-done((bf16[32,1024]{1,0:T(8,128)(2,1)}, bf16[32,1024]{1,0:T(8,128)(2,1)S(1)}, u32[]{:S(2)}, u32[]{:S(2)}) %collective-permute-start) | collective-permute-done | bytes 65568 | tf_op jit(solution)/shard_map/ppermute | solution.py:19
  32.5 4.3 gather_fusion.1
  36.8 5.0 gather_fusion
  41.8 10.5 %reshape.145 = f32[256,3,2048]{2,1,0:T(4,128)} reshape(f32[768,2048]{1,0:T(8,128)} %gather_fusion) | data formatting | bytes 12582912 | tf_op jit(solution)/shard_map/while/body/eval_jaxpr/gather | solution.py:41
  52.3 5.1 slice.44
  57.4 3.4 copy.28
  62.9 9.1 %reshape.153 = bf16[256,3,2048]{2,1,0:T(4,128)(2,1)} reshape(bf16[768,2048]{1,0:T(8,128)(2,1)} %gather_fusion.1) | data formatting | bytes 6291456 | tf_op jit(solution)/shard_map/while/body/eval_jaxpr/gather | solution.py:41
  72.0 3.6 slice.45
  75.6 4.1 copy.59
  79.7 2.9 multiply_reduce_fusion.2
  89.1 16.8 %all-gather = bf16[2048,100]{0,1:T(8,128)(2,1)S(1)} all-gather(bf16[256,100]{0,1:T(8,128)(2,1)S(1)} %get-tuple-element.68), channel_id=2, replica_groups=mesh['member'=8,'shard'=32] {'member'}, dimensions={0}, use_global_device_ids=true | all-gather | bytes 460800 | tf_op jit(solution)/shard_map/all_gather | solution.py:96
  117.9 3.1 pad_add_fusion
  121.0 9.6 %copy.32 = f32[256,3,2048]{2,1,0:T(4,128)} copy(f32[256,3,2048]{0,2,1:T(8,128)} %pad_add_fusion) | data formatting | bytes 12582912 | tf_op jit(solution)/shard_map/while/body/eval_jaxpr/transpose(jvp())/add_any | solution.py:43
  130.7 10.8 %reshape.164 = f32[768,2048]{1,0:T(8,128)} reshape(f32[256,3,2048]{2,1,0:T(4,128)} %copy.32) | data formatting | bytes 12582912 | tf_op jit(solution)/shard_map/while/body/eval_jaxpr/transpose(jvp())/add_any | solution.py:43
  141.5 14.9 %scatter_custom_fusion = f32[96,2048]{1,0:T(8,128)S(1)} fusion(s32[768]{0:T(1024)S(1)} %reshape.146, f32[768,2048]{1,0:T(8,128)} %reshape.164, f32[]{:T(128)} %constant.61.clone.1), kind=kCustom, calls=%fused_computation.36 | custom fusion | flops 1572864 | bytes 786944 | tf_op jit(solution)/shard_map/while/body/eval_jaxpr/transpose(jvp())/scatter-add | solution.py:41
  157.8 4.2 collective-permute-start.3
  163.2 6.6 %collective-permute-done.2 = bf16[32,2048]{1,0:T(8,128)(2,1)S(1)} collective-permute-done((bf16[32,2048]{1,0:T(8,128)(2,1)S(1)}, bf16[32,2048]{1,0:T(8,128)(2,1)S(1)}, u32[]{:S(2)}, u32[]{:S(2)}) %collective-permute-start.2) | collective-permute-done | bytes 131104 | tf_op jit(solution)/shard_map/ppermute | solution.py:30
  172.8 4.2 fusion
  177.0 9.3 %copy.61 = bf16[1024,3172]{1,0:T(8,128)(2,1)} copy(bf16[1024,3172]{0,1:T(8,128)(2,1)} %fusion) | data formatting | bytes 12992512
  186.3 112.3 %psum.14 = f32[1]{0:T(128)} all-reduce(f32[1]{0:T(128)} %bitcast.11), channel_id=1, replica_groups=mesh['member'=8,'shard'=32] {'shard'}, use_global_device_ids=true, to_apply=%region_7.8 | all-reduce | flops 1 | bytes 8 | tf_op jit(solution)/shard_map/psum | solution.py:106
  299.3 183.2 %reduce-scatter.4.cloned.1.call-done = bf16[32,3172]{1,0:T(8,128)(2,1)} async-done(((bf16[1024,3172]{1,0:T(8,128)(2,1)}), bf16[32,3172]{1,0:T(8,128)(2,1)}) %reduce-scatter.4.cloned.1.call-update) | async-done | bytes 203024
  484.6 4.3 convolution_bitcast_fusion.2
  489.0 70.2 %all-reduce.4.cloned.1.call-done = bf16[32,3172]{0,1:T(8,128)(2,1)} async-done(((bf16[32,3172]{0,1:T(8,128)(2,1)}), bf16[32,3172]{0,1:T(8,128)(2,1)}) %all-reduce.4.cloned.1.call-update) | async-done | bytes 203024 | tf_op jit(solution)/shard_map/psum | solution.py:147
  (96 shorter events, 38.8 us)
Async XLA Ops:
  7.2 13.6 %copy-start = (bf16[1024,1024]{1,0:T(8,128)(2,1)S(1)}, bf16[1024,1024]{1,0:T(8,128)(2,1)}, u32[]{:S(2)}) copy-start(bf16[1024,1024]{1,0:T(8,128)(2,1)} %param.13) | copy-start | bytes 6291460
  7.2 24.4 %copy-start.13 = (bf16[1,32,1024]{2,1,0:T(8,128)(2,1)S(1)}, bf16[1,32,1024]{2,1,0:T(8,128)(2,1)}, u32[]{:S(2)}) copy-start(bf16[1,32,1024]{2,1,0:T(8,128)(2,1)} %param.8) | copy-start | bytes 196612
  7.2 475.3 %reduce-scatter.4.cloned.1.call-start = ((), (), s32[]{:S(2)}) async-start(), calls=%async_computation.2 | async-start | bytes 6758400
  7.2 16.9 %collective-permute-start.1 = (bf16[32,1024]{1,0:T(8,128)(2,1)}, bf16[32,1024]{1,0:T(8,128)(2,1)S(1)}, u32[]{:S(2)}, u32[]{:S(2)}) collective-permute-start(bf16[32,1024]{1,0:T(8,128)(2,1)} %bitcast.80), channel_id=1, source_target_pairs={{1,0},{2,1},{3,2},{4,3},{5,4},{6,5},{7,6},{8,7},{9,8},{10,9},{11,1... | collective-permute-start | bytes 196616 | tf_op jit(solution)/shard_map/ppermute | solution.py:21
  19.7 11.9 %collective-permute-start = (bf16[32,1024]{1,0:T(8,128)(2,1)}, bf16[32,1024]{1,0:T(8,128)(2,1)S(1)}, u32[]{:S(2)}, u32[]{:S(2)}) collective-permute-start(bf16[32,1024]{1,0:T(8,128)(2,1)} %bitcast.81), channel_id=1, source_target_pairs={{0,1},{1,2},{2,3},{3,4},{4,5},{5,6},{6,7},{7,8},{8,9},{9,10},{10,1... | collective-permute-start | bytes 196616 | tf_op jit(solution)/shard_map/ppermute | solution.py:19
  20.8 10.9 %copy-start.5 = (bf16[1024,2048]{1,0:T(8,128)(2,1)S(1)}, bf16[1024,2048]{1,0:T(8,128)(2,1)}, u32[]{:S(2)}) copy-start(bf16[1024,2048]{1,0:T(8,128)(2,1)} %param.14) | copy-start | bytes 12582916
  22.9 9.5 %copy-start.6 = (f32[256,1024]{0,1:T(8,128)}, f32[256,1024]{0,1:T(8,128)S(1)}, u32[]{:S(2)}) copy-start(f32[256,1024]{0,1:T(8,128)S(1)} %get-tuple-element.67) | copy-start | bytes 3145732
  60.9 1.2 copy-start.8
  85.2 3.3 copy-start.2
  85.2 3.3 copy-start.3
  85.2 3.5 copy-start.12
  88.7 19.5 %copy-start.10 = (bf16[256,1024]{1,0:T(8,128)(2,1)}, bf16[256,1024]{1,0:T(8,128)(2,1)S(1)}, u32[]{:S(2)}) copy-start(bf16[256,1024]{1,0:T(8,128)(2,1)S(1)} %multiply_convert_fusion) | copy-start | bytes 1572868
  88.7 18.3 %copy-start.14 = (f32[256,100]{0,1:T(8,128)S(1)}, f32[256,100]{0,1:T(8,128)}, u32[]{:S(2)}) copy-start(f32[256,100]{0,1:T(8,128)} %param.12) | copy-start | bytes 307204
  88.7 18.3 %copy-start.15 = (f32[256]{0:T(256)S(1)}, f32[256]{0:T(256)}, u32[]{:S(2)}) copy-start(f32[256]{0:T(256)} %param.11) | copy-start | bytes 3076
  112.3 2.6 copy-start.9
  116.3 1.2 copy-start.7
  130.7 31.2 %copy-start.4 = (bf16[256,1024]{1,0:T(8,128)(2,1)S(1)}, bf16[256,1024]{1,0:T(8,128)(2,1)}, u32[]{:S(2)}) copy-start(bf16[256,1024]{1,0:T(8,128)(2,1)} %param.9) | copy-start | bytes 1572868
  156.5 13.3 %collective-permute-start.2 = (bf16[32,2048]{1,0:T(8,128)(2,1)S(1)}, bf16[32,2048]{1,0:T(8,128)(2,1)S(1)}, u32[]{:S(2)}, u32[]{:S(2)}) collective-permute-start(bf16[32,2048]{1,0:T(8,128)(2,1)S(1)} %get-tuple-element.62), channel_id=1, source_target_pairs={{0,31},{1,0},{2,1},{3,2},{4,3},{5,4},{6,5},{7,6},{8,7},{9,8},{10,9... | collective-permute-start | bytes 393224 | tf_op jit(solution)/shard_map/ppermute | solution.py:30
  157.8 13.7 %collective-permute-start.3 = (bf16[32,2048]{1,0:T(8,128)(2,1)S(1)}, bf16[32,2048]{1,0:T(8,128)(2,1)S(1)}, u32[]{:S(2)}, u32[]{:S(2)}) collective-permute-start(bf16[32,2048]{1,0:T(8,128)(2,1)S(1)} %get-tuple-element.63), channel_id=1, source_target_pairs={{0,1},{1,2},{2,3},{3,4},{4,5},{5,6},{6,7},{7,8},{8,9},{9,10},{10,1... | collective-permute-start | bytes 393224 | tf_op jit(solution)/shard_map/ppermute | solution.py:30
  161.9 1.0 copy-start.11
  186.3 372.8 %all-reduce.4.cloned.1.call-start = ((), (), s32[]{:S(2)}) async-start(), calls=%async_computation.1 | async-start | bytes 1626112 | tf_op jit(solution)/shard_map/psum | solution.py:147
  484.6 79.9 %copy-start.1 = (bf16[1024,1024]{1,0:T(8,128)(2,1)S(1)}, bf16[1024,1024]{1,0:T(8,128)(2,1)}, u32[]{:S(2)}) copy-start(bf16[1024,1024]{1,0:T(8,128)(2,1)} %param.13) | copy-start | bytes 6291460
Sparse Core Ops, SparseCore 0:
  186.4 296.0 reduce-scatter.3
  485.1 73.9 all-reduce.3
where the time goes:
time: 576 us; the launch traced here: 572 us
  waiting for transfers between devices  269 us (47%)
  blocking collectives  129 us (22%)
  local copies, waits for them, and re-layouts  89.5 us (16%)
  other arithmetic  40.2 us (7%)
  starting transfers between devices  18 us (3%)
  between operations  16.2 us (3%)
  matrix products  10.3 us (2%)
    unnamed x3, waiting for transfers between devices  183 us
    psum x1, blocking collectives, on_device(): loss = lax.psum(local_loss[None], 'shard') / divisor  112 us
    psum x1, waiting for transfers between devices, on_device(): total = lax.psum(portion, 'member').astype(jnp.float32)  70.2 us
    gather x4, local copies, waits for them, and re-layouts, attend(): picked = table[source]  28.9 us
    add_any x2, local copies, waits for them, and re-layouts, attend(): key_norm = normalize_heads(picked[..., :width])  20.4 us
    unnamed x39, local copies, waits for them, and re-layouts  19.7 us
    all_gather x1, blocking collectives, on_device(): lax.all_gather(preds[None].astype(jnp.bfloat16), 'member', axis=0, tiled=...  16.8 us
    scatter-add x1, other arithmetic, attend(): picked = table[source]  14.9 us
  transfers between devices with their start and end apart: 6, of which 5 were waited for; matrix products, arithmetic and copies ran while one was open for 2% of the time, Pallas kernels for 0%

commit v1 on v0

v1 whole, which is shorter than its diff:
```python
import jax
import jax.numpy as jnp
from jax import lax
from jax.experimental import pallas as pl
from jax.experimental.pallas import tpu as pltpu
from jax.sharding import PartitionSpec as P

F32 = jnp.float32
BF16 = jnp.bfloat16
TILE = 128
SIZE = 64
MEMBERS = 8
SHARDS = 32
NODES = 32
WIDE = 96
ROWS = 256
WIDTH = 1024
VARS = 100
PAIR = 1.0 / (MEMBERS * (MEMBERS - 1))
SCALE = (MEMBERS * ROWS * SHARDS) ** (-0.5)
VMEM = pl.BlockSpec(memory_space=pltpu.VMEM)
SMEM = pl.BlockSpec(memory_space=pltpu.SMEM)


def dot(left, right, over=((1,), (0,))):
    return lax.dot_general(left, right, (over, ((), ())), preferred_element_type=F32)


def call(body, outs, specs, scratch=(), flops=0, size=0):
    return pl.pallas_call(
        body,
        out_shape=outs,
        in_specs=specs,
        out_specs=[VMEM] * len(outs),
        scratch_shapes=list(scratch),
        compiler_params=pltpu.CompilerParams(vmem_limit_bytes=48 * 1024 * 1024),
        cost_estimate=pl.CostEstimate(flops=flops, bytes_accessed=size, transcendentals=0),
    )


def lanes(shape):
    return lax.broadcasted_iota(jnp.int32, shape, len(shape) - 1)


def averager():
    row = lax.broadcasted_iota(jnp.int32, (TILE, TILE), 0) // SIZE
    return jnp.where(row == lanes((TILE, TILE)) // SIZE, 1.0 / SIZE, 0.0).astype(BF16)


def head_mean(values, average):
    high = values.astype(BF16)
    low = (values - high.astype(F32)).astype(BF16)
    return dot(high, average) + dot(low, average)


def counts_of(index):
    lane = lanes((ROWS, TILE))
    total = jnp.zeros((ROWS, TILE), F32)
    for k in range(3):
        total = total + jnp.where(index[:, k : k + 1] == lane, 1.0, 0.0)
    return total


def both_heads(tile):
    first = lanes(tile.shape) < SIZE
    zero = jnp.zeros_like(tile)
    return jnp.concatenate([jnp.where(first, tile, zero), jnp.where(first, zero, tile)], 0)


def pad_rows(tile):
    return jnp.concatenate([tile, jnp.zeros((TILE - tile.shape[0], tile.shape[1]), tile.dtype)], 0)


def per_head(first, second, shape):
    return jnp.where(lanes(shape) < SIZE, first, second)


def halves(values):
    return (
        jnp.sum(values[:, :TILE], -1, keepdims=True),
        jnp.sum(values[:, TILE:], -1, keepdims=True),
    )


def query_kernel(me, embed, w_query, normal, tile, inverse):
    average = averager()
    value = dot(embed[...], w_query[...])
    here = me[0]
    held = jnp.zeros((ROWS, TILE), F32)
    for t in range(WIDTH // TILE):
        part = value[:, t * TILE : (t + 1) * TILE]
        root = lax.rsqrt(head_mean(part * part, average) + 1e-06)
        normal[:, t * TILE : (t + 1) * TILE] = (part * root).astype(BF16)
        held = jnp.where(here == t, root, held)
    inverse[...] = held
    tile[...] = normal[:, pl.ds(pl.multiple_of(here * TILE, TILE), TILE)]


def forward_kernel(wide, w_keyval, normal, embed, index, w_head, payload, hidden):
    average = averager()
    count = counts_of(index[...])
    count = jnp.concatenate([count, count], 1)
    table = dot(wide[...], w_keyval[...]).astype(BF16)
    for t in range(WIDTH // TILE):
        at = slice(t * TILE, (t + 1) * TILE)
        key = table[:, at].astype(F32)
        key = (key * lax.rsqrt(head_mean(key * key, average) + 1e-06)).astype(BF16)
        key = both_heads(pad_rows(key))
        value = both_heads(pad_rows(table[:, WIDTH + t * TILE : WIDTH + (t + 1) * TILE]))
        score = dot(normal[:, at], key, ((1,), (1,)))
        expon = count * jnp.exp(score * SIZE**-0.5)
        first, second = halves(expon)
        mixed = dot(expon.astype(BF16), value)
        mixed = mixed * per_head(1.0 / first, 1.0 / second, mixed.shape)
        hidden[:, at] = embed[:, at].astype(F32) + mixed
    whole = hidden[...]
    mean = jnp.mean(whole, -1, keepdims=True)
    center = whole - mean
    inverse = lax.rsqrt(jnp.mean(center * center, -1, keepdims=True) + 1e-05)
    pred = dot((center * inverse).astype(BF16), w_head[...])
    lane = lanes(pred.shape)
    for at, stat in ((VARS, mean), (VARS + 2, inverse)):
        high = stat.astype(BF16).astype(F32)
        pred = jnp.where(lane == at, high, pred)
        pred = jnp.where(lane == at + 1, stat - high, pred)
    payload[...] = pred.astype(BF16)


def crps(preds, target, area, d_pred, lost):
    size = 32

    @pl.loop(0, ROWS // size)
    def _(step):
        rows = pl.ds(pl.multiple_of(step * size, size), size)
        value = [preds[k][rows, :].astype(F32) for k in range(MEMBERS)]
        slope = [jnp.zeros((size, TILE), F32) for _ in range(MEMBERS)]
        weight = jnp.where(lanes((size, TILE)) < VARS, area[rows, :], 0.0)
        aim = target[rows, :]
        pair = jnp.zeros((size, TILE), F32)
        for i in range(MEMBERS):
            for j in range(i + 1, MEMBERS):
                delta = value[i] - value[j]
                square = delta * delta + 0.0625
                root = lax.rsqrt(square)
                if i == 0:
                    pair = pair + square * root
                part = delta * root
                slope[i] = slope[i] + part
                slope[j] = slope[j] - part
        for i in range(MEMBERS):
            delta = value[i] - aim
            square = delta * delta + 0.0625
            root = lax.rsqrt(square)
            if i == 0:
                lost[rows, :] = weight * (square * root / MEMBERS - 0.5 * PAIR * pair)
            d_pred[i, rows, :] = (weight * (delta * root / MEMBERS - PAIR * slope[i])).astype(BF16)


def backward_kernel(
    me, latents, w_keyval, normal, inverse, embed, embed_tile, index, head_rows, head_sum,
    target, area, p0, p1, p2, p3, p4, p5, p6, p7,
    payload, t0, t1, t2, t3, t4, t5, t6, t7, d_pred, lost, d_table,
):
    preds = (p0, p1, p2, p3, p4, p5, p6, p7)
    tables = (t0, t1, t2, t3, t4, t5, t6, t7)
    here = me[0]
    crps(preds, target, area, d_pred, lost)
    average = averager()
    count = counts_of(index[...])
    count = jnp.concatenate([count, count], 1)
    query = normal[...]
    base = embed_tile[...].astype(F32)
    d_query = jnp.zeros((ROWS, TILE), F32)
    d_head = jnp.zeros((TILE, TILE), F32)
    shape = (ROWS, TILE)
    first_head = lanes((TILE, TILE)) < SIZE
    for k in range(MEMBERS):
        who = jnp.bitwise_xor(here, k)
        latent = latents[who]
        table = dot(latent, w_keyval[...]).astype(BF16)
        key_raw = pad_rows(table[:, :TILE]).astype(F32)
        key_root = lax.rsqrt(head_mean(key_raw * key_raw, average) + 1e-06)
        key_norm = key_raw * key_root
        key = both_heads(key_norm.astype(BF16))
        value = both_heads(pad_rows(table[:, TILE:]))
        score = dot(query, key, ((1,), (1,)))
        expon = count * jnp.exp(score * SIZE**-0.5)
        first, second = halves(expon)
        weight = jnp.concatenate([expon[:, :TILE] / first, expon[:, TILE:] / second], 1)
        weight_low = weight.astype(BF16)
        mixed = dot(weight_low, value)
        pred = preds[k][...].astype(F32)
        mean = pred[:, VARS : VARS + 1] + pred[:, VARS + 1 : VARS + 2]
        scale = pred[:, VARS + 2 : VARS + 3] + pred[:, VARS + 3 : VARS + 4]
        normed = (base + mixed - mean) * scale
        out = d_pred[k]
        out_wide = out.astype(F32)
        d_head = d_head + dot(normed.astype(BF16), out, ((0,), (0,)))
        d_normed = dot(out, head_rows[...], ((1,), (1,)))
        level = jnp.sum(out_wide * head_sum[...], -1, keepdims=True) / WIDTH
        along = jnp.sum(out_wide * pred, -1, keepdims=True) / WIDTH
        d_mixed = (scale * (d_normed - level - normed * along)).astype(BF16)
        d_weight = dot(d_mixed, value, ((1,), (1,)))
        first, second = halves(weight * d_weight)
        d_score = jnp.concatenate(
            [
                weight[:, :TILE] * (d_weight[:, :TILE] - first),
                weight[:, TILE:] * (d_weight[:, TILE:] - second),
            ],
            1,
        )
        d_score = (d_score * SIZE**-0.5).astype(BF16)
        d_value = dot(weight_low, d_mixed, ((0,), (0,)))
        d_value = jnp.where(first_head, d_value[:TILE], d_value[TILE:])
        d_query = d_query + dot(d_score, key)
        d_key = dot(d_score, query, ((0,), (0,)))
        d_key = jnp.where(first_head, d_key[:TILE], d_key[TILE:])
        d_key = key_root * (d_key - key_norm * head_mean(d_key * key_norm, average))
        both = jnp.concatenate([d_key[:WIDE], d_value[:WIDE]], 1).astype(BF16)
        tables[k][...] = both
        d_table[pl.ds(pl.multiple_of(who * WIDE, WIDE), WIDE), :] = both
    wide_query = query.astype(F32)
    d_query = inverse[...] * (d_query - wide_query * head_mean(d_query * wide_query, average))
    grad = dot(embed[...], d_query.astype(BF16), ((0,), (0,)))
    payload[:, :TILE] = (grad * SCALE).astype(BF16)
    flat = latents[...].reshape(MEMBERS * WIDE, WIDTH)
    grad = dot(flat, d_table[...], ((0,), (0,)))
    payload[:, TILE : 3 * TILE] = (grad * SCALE).astype(BF16)
    loss = jnp.sum(lost[...], axis=(0, 1), keepdims=True) / (ROWS * SHARDS * VARS)
    high = loss.astype(BF16).astype(F32)
    lane = lanes((WIDTH, TILE))
    side = jnp.where(lane == VARS, high, jnp.where(lane == VARS + 1, loss - high, 0.0))
    payload[:, 3 * TILE :] = side.astype(BF16)
    rows = pl.ds(pl.multiple_of(here * TILE, TILE), TILE)
    lane = lanes((TILE, TILE))
    payload[rows, 3 * TILE :] = jnp.where(
        lane < VARS, d_head * SCALE, side[:TILE]
    ).astype(BF16)


def sum_kernel(pieces, total, loss):
    value = jnp.sum(pieces[...].astype(F32), 0)
    total[...] = value.astype(BF16)
    loss[...] = value[0:1, 3 * TILE + VARS : 3 * TILE + VARS + 1] + value[
        0:1, 3 * TILE + VARS + 1 : 3 * TILE + VARS + 2
    ]


def place_kernel(me, g0, g1, g2, g3, g4, g5, g6, g7, query, keyval, head):
    here = me[0]
    total = jnp.zeros((NODES, TILE), F32)
    for k, part in enumerate((g0, g1, g2, g3, g4, g5, g6, g7)):
        at = pl.multiple_of(jnp.bitwise_xor(here, k) * TILE, TILE)
        query[:, pl.ds(at, TILE)] = part[:, :TILE].astype(F32)
        keyval[:, pl.ds(at, TILE)] = part[:, TILE : 2 * TILE].astype(F32)
        keyval[:, pl.ds(pl.multiple_of(WIDTH + at, TILE), TILE)] = part[
            :, 2 * TILE : 3 * TILE
        ].astype(F32)
        total = total + part[:, 3 * TILE :].astype(F32)
    head[...] = total[:, :VARS]


def latent_kernel(me, t0, t1, t2, t3, t4, t5, t6, t7, w_keyval, own, partner, other):
    here = me[0]
    total = jnp.zeros((WIDE, WIDTH), F32)
    for k, part in enumerate((t0, t1, t2, t3, t4, t5, t6, t7)):
        at = pl.multiple_of(jnp.bitwise_xor(here, k) * TILE, TILE)
        total = total + dot(part[:, :TILE], w_keyval[:, pl.ds(at, TILE)], ((1,), (1,)))
        at = pl.multiple_of(WIDTH + at, TILE)
        total = total + dot(part[:, TILE:], w_keyval[:, pl.ds(at, TILE)], ((1,), (1,)))
    own[...] = total[:NODES]
    partner[...] = total[NODES : 2 * NODES]
    other[...] = total[2 * NODES :].astype(BF16)


def swap(array, axis, bits):
    count = lax.axis_size(axis)
    return lax.ppermute(array, axis, [(i, i ^ bits) for i in range(count)])


def outward(sign):
    step = lambda i: 2 * sign if i % 2 == 0 else -2 * sign
    return [(i, (i + step(i)) % SHARDS) for i in range(SHARDS)]


def spread(array):
    slots = {0: array}
    for k in (6, 4, 2):
        slots[k] = swap(array, "member", k)
    for k in (0, 2, 4, 6):
        slots[k + 1] = swap(slots[k], "member", 1)
    return [slots[k] for k in range(MEMBERS)]


def shape(*dims, kind=BF16):
    return jax.ShapeDtypeStruct(dims, kind)


def on_device(latent, grid_embed, edge_src, area, target, w_query, w_keyval, w_head):
    member = lax.axis_index("member").astype(jnp.int32)
    shard = lax.axis_index("shard").astype(jnp.int32)
    me = member.reshape(1)
    own = latent[0]
    partner = swap(own, "shard", 1)
    other = lax.ppermute(partner, "shard", outward(1))
    wide = jnp.concatenate([own, partner, other], 0)
    offset = jnp.mod(edge_src // NODES - shard, SHARDS)
    toward = jnp.where(shard % 2 == 0, 1, SHARDS - 1)
    slot = jnp.where(offset == 0, 0, jnp.where(offset == toward, 1, 2))
    index = slot * NODES + edge_src % NODES
    head_wide = jnp.pad(w_head, ((0, 0), (0, TILE - VARS)))
    head_rows = lax.dynamic_slice_in_dim(head_wide, member * TILE, TILE, 0)
    head_sum = jnp.sum(head_wide.astype(F32), 0, keepdims=True)
    target_wide = jnp.pad(target, ((0, 0), (0, TILE - VARS)))
    area_wide = area[:, None]
    embed_tile = lax.dynamic_slice_in_dim(grid_embed, member * TILE, TILE, 1)
    keyval_tile = jnp.concatenate(
        [
            lax.dynamic_slice_in_dim(w_keyval, member * TILE, TILE, 1),
            lax.dynamic_slice_in_dim(w_keyval, WIDTH + member * TILE, TILE, 1),
        ],
        1,
    )
    normal, normal_tile, inverse = call(
        query_kernel,
        [shape(ROWS, WIDTH), shape(ROWS, TILE), shape(ROWS, TILE, kind=F32)],
        [SMEM, VMEM, VMEM],
        flops=2 * ROWS * WIDTH * WIDTH,
        size=4 << 20,
    )(me, grid_embed, w_query)
    (payload,) = call(
        forward_kernel,
        [shape(ROWS, TILE)],
        [VMEM] * 6,
        [pltpu.VMEM((ROWS, WIDTH), F32)],
        flops=4 << 30,
        size=8 << 20,
    )(wide, w_keyval, normal, grid_embed, index, head_wide)
    latents = lax.all_gather(wide, "member", axis=0, tiled=False)
    preds = spread(payload)
    results = call(
        backward_kernel,
        [shape(WIDTH, 4 * TILE)] + [shape(WIDE, 2 * TILE)] * MEMBERS,
        [SMEM] + [VMEM] * 19,
        [
            pltpu.VMEM((MEMBERS, ROWS, TILE), BF16),
            pltpu.VMEM((ROWS, TILE), F32),
            pltpu.VMEM((MEMBERS * WIDE, 2 * TILE), BF16),
        ],
        flops=8 << 30,
        size=16 << 20,
    )(
        me, latents, keyval_tile, normal_tile, inverse, grid_embed, embed_tile, index,
        head_rows, head_sum, target_wide, area_wide, *preds,
    )
    grads, d_tables = results[0], results[1:]
    d_tables = [d_tables[0]] + [swap(d_tables[k], "member", k) for k in range(1, MEMBERS)]
    pieces = lax.all_to_all(
        grads.reshape(SHARDS, NODES, 4 * TILE), "shard", 0, 0, tiled=False
    )
    total, loss = call(
        sum_kernel,
        [shape(NODES, 4 * TILE), shape(1, 1, kind=F32)],
        [VMEM],
        flops=1 << 20,
        size=1 << 20,
    )(pieces)
    parts = spread(total)
    grad_query, grad_keyval, grad_head = call(
        place_kernel,
        [
            shape(NODES, WIDTH, kind=F32),
            shape(NODES, 2 * WIDTH, kind=F32),
            shape(NODES, VARS, kind=F32),
        ],
        [SMEM] + [VMEM] * MEMBERS,
        size=1 << 20,
    )(me, *parts)
    mine, near, far = call(
        latent_kernel,
        [
            shape(NODES, WIDTH, kind=F32),
            shape(NODES, WIDTH, kind=F32),
            shape(NODES, WIDTH),
        ],
        [SMEM] + [VMEM] * 9,
        flops=2 * WIDE * WIDTH * 2 * WIDTH,
        size=5 << 20,
    )(me, *d_tables, w_keyval)
    near = near + lax.ppermute(far, "shard", outward(-1)).astype(F32)
    d_latent = mine + swap(near.astype(BF16), "shard", 1).astype(F32)
    return (loss.reshape(1), d_latent[None], grad_query, grad_keyval, grad_head)


def solution(mesh):
    placed = (
        P("member", "shard", None),
        P("shard", None),
        P("shard", None),
        P("shard"),
        P("shard", None),
        P(),
        P(),
        P(),
    )
    return jax.shard_map(
        on_device,
        mesh=mesh,
        in_specs=placed,
        out_specs=(
            P("member"),
            P("member", "shard", None),
            P("shard", None),
            P("shard", None),
            P("shard", None),
        ),
        check_vma=False,
    )
```

time: 576 us -> 161 us (0.28)
  waiting for transfers between devices: 269 us -> 40.6 us
  blocking collectives: 129 us -> 0 us
  local copies, waits for them, and re-layouts: 89.5 us -> 11.5 us
  starting transfers between devices: 18 us -> 68.2 us
  other arithmetic: 40.2 us -> 3.35 us
  Pallas kernels: 0 us -> 22.6 us
  matrix products: 10.3 us -> 0 us
    unnamed x3 -> x1, waiting for transfers between devices: 183 us -> 0.02 us
    psum x1 -> x0, blocking collectives: 112 us -> none  [on_device(): loss = lax.psum(local_loss[None], 'shard') / divisor]
    psum x1 -> x0, waiting for transfers between devices: 70.2 us -> none  [on_device(): total = lax.psum(portion, 'member').astype(jnp.float32)]
    ppermute x4 -> x25, starting transfers between devices: 17.9 us -> 57.7 us  [the longest x23 51.4 us: swap(): return lax.ppermute(array, axis, [(i, i ^ bits) for i in range(count)])]
    gather x4 -> x0, local copies, waits for them, and re-layouts: 28.9 us -> none  [attend(): picked = table[source]]
    add_any x3 -> x0, local copies, waits for them, and re-layouts: 23 us -> none  [the longest x2 20.4 us: attend(): key_norm = normalize_heads(picked[..., :width])]
    pallas_call x0 -> x6, Pallas kernels: none -> 22.6 us  [the longest x1 15 us: on_device(): call(backward_kernel, [shape(WIDTH, 4 * TILE)] + [shape(WIDE, 2 * TILE)]...]
    all_gather x1 -> x0, blocking collectives: 16.8 us -> none  [on_device(): lax.all_gather(preds[None].astype(jnp.bfloat16), 'member', axis=0, tiled=...]
  transfers between devices with their start and end apart: 6 -> 27, of which waited for: 5 -> 10; matrix products, arithmetic and copies ran while one was open for 2% -> 4% of each run, Pallas kernels for 0% -> 4%
where the time goes in v1:
time: 161 us
  starting transfers between devices  68.2 us (42%)
  waiting for transfers between devices  40.6 us (25%)
  Pallas kernels  22.6 us (14%)
  between operations  14.2 us (9%)
  local copies, waits for them, and re-layouts  11.5 us (7%)
  other arithmetic  3.35 us (2%)
    ppermute x23, starting transfers between devices, swap(): return lax.ppermute(array, axis, [(i, i ^ bits) for i in range(count)])  51.4 us
    ppermute x23, waiting for transfers between devices, swap(): return lax.ppermute(array, axis, [(i, i ^ bits) for i in range(count)])  22 us
    pallas_call x1, Pallas kernels, on_device(): call(backward_kernel, [shape(WIDTH, 4 * TILE)] + [shape(WIDE, 2 * TILE)]...  15 us
    all_gather x1, waiting for transfers between devices, on_device(): latents = lax.all_gather(wide, 'member', axis=0, tiled=False)  12 us
    all_to_all x1, starting transfers between devices, on_device(): lax.all_to_all(grads.reshape(SHARDS, NODES, 4 * TILE), 'shard', 0, 0, til...  10.5 us
    unnamed x17, local copies, waits for them, and re-layouts  9.38 us
    ppermute x1, waiting for transfers between devices, on_device(): other = lax.ppermute(partner, 'shard', outward(1))  5.29 us
    ppermute x1, starting transfers between devices, on_device(): near = near + lax.ppermute(far, 'shard', outward(-1)).astype(F32)  4.98 us
  transfers between devices with their start and end apart: 27, of which 10 were waited for; matrix products, arithmetic and copies ran while one was open for 4% of the time, Pallas kernels for 4%

profile of v1, /device:TPU:1, one launch (start us, length us, event | category | flops | bytes accessed | tf_op | source)
XLA Modules:
  0.0 160.6 jit_solution(11903762388491922330)
XLA Ops:
  7.2 7.8 %collective-permute-start = (bf16[32,1024]{1,0:T(8,128)(2,1)}, bf16[32,1024]{1,0:T(8,128)(2,1)S(1)}, u32[]{:S(2)}, u32[]{:S(2)}) collective-permute-start(bf16[32,1024]{1,0:T(8,128)(2,1)} %bitcast.11), channel_id=1, source_target_pairs={{0,1},{1,0},{2,3},{3,2},{4,5},{5,4},{6,7},{7,6},{8,9},{9,8},{10,11... | collective-permute-start | bytes 196616 | tf_op jit(solution)/shard_map/ppermute | solution.py:278
  15.0 2.0 %collective-permute-done = bf16[32,1024]{1,0:T(8,128)(2,1)S(1)} collective-permute-done((bf16[32,1024]{1,0:T(8,128)(2,1)}, bf16[32,1024]{1,0:T(8,128)(2,1)S(1)}, u32[]{:S(2)}, u32[]{:S(2)}) %collective-permute-start) | collective-permute-done | bytes 65568 | tf_op jit(solution)/shard_map/ppermute | solution.py:278
  18.3 5.3 %collective-permute-done.1 = bf16[32,1024]{1,0:T(8,128)(2,1)S(1)} collective-permute-done((bf16[32,1024]{1,0:T(8,128)(2,1)S(1)}, bf16[32,1024]{1,0:T(8,128)(2,1)S(1)}, u32[]{:S(2)}, u32[]{:S(2)}) %collective-permute-start.1) | collective-permute-done | bytes 65568 | tf_op jit(solution)/shard_map/ppermute | solution.py:305
  23.6 1.5 pad_maximum_fusion.1.wide
  30.1 1.7 %copy-done.2 = bf16[1024,1024]{1,0:T(8,128)(2,1)S(1)} copy-done((bf16[1024,1024]{1,0:T(8,128)(2,1)S(1)}, bf16[1024,1024]{1,0:T(8,128)(2,1)}, u32[]{:S(2)}) %copy-start.2) | copy-done | bytes 2097176
  35.4 3.6 %shard_map.120.p0 = bf16[256,128]{1,0:T(8,128)(2,1)S(1)} custom-call(bf16[96,1024]{1,0:T(8,128)(2,1)S(1)} %copy-done.3, bf16[1024,2048]{1,0:T(8,128)(2,1)S(1)} %copy-done, bf16[256,1024]{1,0:T(8,128)(2,1)S(1)} %get-tuple-element.27.normal, bf16[256,1024]{1,0:T(8,128)(2,1)S(1)} %copy-done.4, s32[256,3]{1,0:T(8,128)S(1)} %fusion.2.index, ...), custom_call_target="tpu_custom_call" | custom-call | flops 4294967296 | bytes 8388608 | tf_op jit(solution)/shard_map/pallas_call | solution.py:331
  39.0 2.8 %collective-permute-start.7 = (bf16[256,128]{1,0:T(8,128)(2,1)S(1)}, bf16[256,128]{1,0:T(8,128)(2,1)S(1)}, u32[]{:S(2)}, u32[]{:S(2)}) collective-permute-start(bf16[256,128]{1,0:T(8,128)(2,1)S(1)} %shard_map.120.p0), channel_id=1, source_target_pairs={{0,192},{32,224},{64,128},{96,160},{128,64},{160,96},{192,0},{224,... | collective-permute-start | bytes 196616 | tf_op jit(solution)/shard_map/ppermute | solution.py:278
  42.7 4.0 %collective-permute-start.2 = (bf16[256,128]{1,0:T(8,128)(2,1)S(1)}, bf16[256,128]{1,0:T(8,128)(2,1)S(1)}, u32[]{:S(2)}, u32[]{:S(2)}) collective-permute-start(bf16[256,128]{1,0:T(8,128)(2,1)S(1)} %shard_map.120.p0), channel_id=1, source_target_pairs={{0,32},{32,0},{64,96},{96,64},{128,160},{160,128},{192,224},{224,1... | collective-permute-start | bytes 196616 | tf_op jit(solution)/shard_map/ppermute | solution.py:278
  46.6 3.4 %collective-permute-start.8 = (bf16[256,128]{1,0:T(8,128)(2,1)S(1)}, bf16[256,128]{1,0:T(8,128)(2,1)S(1)}, u32[]{:S(2)}, u32[]{:S(2)}) collective-permute-start(bf16[256,128]{1,0:T(8,128)(2,1)S(1)} %collective-permute-done.7.p6), channel_id=1, source_target_pairs={{0,32},{32,0},{64,96},{96,64},{128,160},{160,128},{192,224},{224,1... | collective-permute-start | bytes 196616 | tf_op jit(solution)/shard_map/ppermute | solution.py:278
  50.1 3.0 %collective-permute-start.6 = (bf16[256,128]{1,0:T(8,128)(2,1)S(1)}, bf16[256,128]{1,0:T(8,128)(2,1)S(1)}, u32[]{:S(2)}, u32[]{:S(2)}) collective-permute-start(bf16[256,128]{1,0:T(8,128)(2,1)S(1)} %collective-permute-done.5.p4), channel_id=1, source_target_pairs={{0,32},{32,0},{64,96},{96,64},{128,160},{160,128},{192,224},{224,1... | collective-permute-start | bytes 196616 | tf_op jit(solution)/shard_map/ppermute | solution.py:278
  54.4 12.0 %all-gather.3.cloned.1.call-done = bf16[768,1024]{1,0:T(8,128)(2,1)} async-done(((bf16[96,1024]{1,0:T(8,128)(2,1)}), bf16[768,1024]{1,0:T(8,128)(2,1)}) %all-gather.3.cloned.1.call-update) | async-done | bytes 1572880 | tf_op jit(solution)/shard_map/all_gather | solution.py:339
  67.8 15.0 %shard_map.121 = (bf16[1024,512]{1,0:T(8,128)(2,1)}, bf16[96,256]{1,0:T(8,128)(2,1)S(1)}, bf16[96,256]{1,0:T(8,128)(2,1)S(1)}, bf16[96,256]{1,0:T(8,128)(2,1)S(1...) custom-call(s32[1]{0:T(128)} %bitcast.me, ...), custom_call_target="tpu_custom_call" | custom-call | flops 8589934592 | bytes 16777216 | tf_op jit(solution)/shard_map/pallas_call | solution.py:341
  82.7 10.5 %all-to-all-start = ((bf16[32,32,512]{2,1,0:T(8,128)(2,1)}), bf16[32,32,512]{2,1,0:T(8,128)(2,1)S(1)}, u32[]{:S(2)}, u32[]{:S(2)}) async-start(bf16[32,32,512]{2,1,0:T(8,128)(2,1)} %bitcast.5), calls=%async_computation | async-start | bytes 2097152 | tf_op jit(solution)/shard_map/all_to_all | solution.py:358
  93.2 2.7 %collective-permute-start.9 = (bf16[96,256]{1,0:T(8,128)(2,1)S(1)}, bf16[96,256]{1,0:T(8,128)(2,1)S(1)}, u32[]{:S(2)}, u32[]{:S(2)}) collective-permute-start(bf16[96,256]{1,0:T(8,128)(2,1)S(1)} %get-tuple-element.31), channel_id=1, source_target_pairs={{0,32},{32,0},{64,96},{96,64},{128,160},{160,128},{192,224},{224,1... | collective-permute-start | bytes 147464 | tf_op jit(solution)/shard_map/ppermute | solution.py:278
  95.9 1.7 %collective-permute-start.11 = (bf16[96,256]{1,0:T(8,128)(2,1)S(1)}, bf16[96,256]{1,0:T(8,128)(2,1)S(1)}, u32[]{:S(2)}, u32[]{:S(2)}) collective-permute-start(bf16[96,256]{1,0:T(8,128)(2,1)S(1)} %get-tuple-element.33), channel_id=1, source_target_pairs={{0,96},{32,64},{64,32},{96,0},{128,224},{160,192},{192,160},{224,1... | collective-permute-start | bytes 147464 | tf_op jit(solution)/shard_map/ppermute | solution.py:278
  98.0 2.3 %collective-permute-start.13 = (bf16[96,256]{1,0:T(8,128)(2,1)S(1)}, bf16[96,256]{1,0:T(8,128)(2,1)S(1)}, u32[]{:S(2)}, u32[]{:S(2)}) collective-permute-start(bf16[96,256]{1,0:T(8,128)(2,1)S(1)} %get-tuple-element.35), channel_id=1, source_target_pairs={{0,160},{32,128},{64,224},{96,192},{128,32},{160,0},{192,96},{224,... | collective-permute-start | bytes 147464 | tf_op jit(solution)/shard_map/ppermute | solution.py:278
  101.8 15.4 %collective-permute-done.10.t2 = bf16[96,256]{1,0:T(8,128)(2,1)S(1)} collective-permute-done((bf16[96,256]{1,0:T(8,128)(2,1)S(1)}, bf16[96,256]{1,0:T(8,128)(2,1)S(1)}, u32[]{:S(2)}, u32[]{:S(2)}) %collective-permute-start.10) | collective-permute-done | bytes 49184 | tf_op jit(solution)/shard_map/ppermute | solution.py:278
  117.1 6.4 %collective-permute-start.15 = (bf16[96,256]{1,0:T(8,128)(2,1)S(1)}, bf16[96,256]{1,0:T(8,128)(2,1)S(1)}, u32[]{:S(2)}, u32[]{:S(2)}) collective-permute-start(bf16[96,256]{1,0:T(8,128)(2,1)S(1)} %get-tuple-element.37), channel_id=1, source_target_pairs={{0,224},{32,192},{64,160},{96,128},{128,96},{160,64},{192,32},{224... | collective-permute-start | bytes 147464 | tf_op jit(solution)/shard_map/ppermute | solution.py:278
  123.5 2.9 %collective-permute-done.13.t5 = bf16[96,256]{1,0:T(8,128)(2,1)S(1)} collective-permute-done((bf16[96,256]{1,0:T(8,128)(2,1)S(1)}, bf16[96,256]{1,0:T(8,128)(2,1)S(1)}, u32[]{:S(2)}, u32[]{:S(2)}) %collective-permute-start.13) | collective-permute-done | bytes 49184 | tf_op jit(solution)/shard_map/ppermute | solution.py:278
  126.4 2.2 %copy-done.1 = bf16[1024,2048]{1,0:T(8,128)(2,1)S(1)} copy-done((bf16[1024,2048]{1,0:T(8,128)(2,1)S(1)}, bf16[1024,2048]{1,0:T(8,128)(2,1)}, u32[]{:S(2)}) %copy-start.1) | copy-done | bytes 4194328
  130.1 5.0 %collective-permute-start.16 = (bf16[32,1024]{1,0:T(8,128)(2,1)S(1)}, bf16[32,1024]{1,0:T(8,128)(2,1)S(1)}, u32[]{:S(2)}, u32[]{:S(2)}) collective-permute-start(bf16[32,1024]{1,0:T(8,128)(2,1)S(1)} %get-tuple-element.40), channel_id=1, source_target_pairs={{0,30},{1,3},{2,0},{3,5},{4,2},{5,7},{6,4},{7,9},{8,6},{9,11},{10,... | collective-permute-start | bytes 196616 | tf_op jit(solution)/shard_map/ppermute | solution.py:390
  136.4 4.6 %collective-permute-start.17 = (bf16[32,1024]{1,0:T(8,128)(2,1)S(1)}, bf16[32,1024]{1,0:T(8,128)(2,1)S(1)}, u32[]{:S(2)}, u32[]{:S(2)}) collective-permute-start(bf16[32,1024]{1,0:T(8,128)(2,1)S(1)} %add_convert_fusion), channel_id=1, source_target_pairs={{0,1},{1,0},{2,3},{3,2},{4,5},{5,4},{6,7},{7,6},{8,9},{9,8},{10,11... | collective-permute-start | bytes 196616 | tf_op jit(solution)/shard_map/ppermute | solution.py:278
  143.6 1.6 collective-permute-start.19
  145.2 3.8 %collective-permute-start.18 = (bf16[32,512]{1,0:T(8,128)(2,1)S(1)}, bf16[32,512]{1,0:T(8,128)(2,1)S(1)}, u32[]{:S(2)}, u32[]{:S(2)}) collective-permute-start(bf16[32,512]{1,0:T(8,128)(2,1)S(1)} %get-tuple-element.41.g0), channel_id=1, source_target_pairs={{0,32},{32,0},{64,96},{96,64},{128,160},{160,128},{192,224},{224,1... | collective-permute-start | bytes 98312 | tf_op jit(solution)/shard_map/ppermute | solution.py:278
  (68 shorter events, 25.3 us)
Async XLA Ops:
  7.2 59.2 %all-gather.3.cloned.1.call-start = ((), (), s32[]{:S(2)}) async-start(), calls=%async_computation.1 | async-start | bytes 1769472 | tf_op jit(solution)/shard_map/all_gather | solution.py:339
  7.2 9.8 %collective-permute-start = (bf16[32,1024]{1,0:T(8,128)(2,1)}, bf16[32,1024]{1,0:T(8,128)(2,1)S(1)}, u32[]{:S(2)}, u32[]{:S(2)}) collective-permute-start(bf16[32,1024]{1,0:T(8,128)(2,1)} %bitcast.11), channel_id=1, source_target_pairs={{0,1},{1,0},{2,3},{3,2},{4,5},{5,4},{6,7},{7,6},{8,9},{9,8},{10,11... | collective-permute-start | bytes 196616 | tf_op jit(solution)/shard_map/ppermute | solution.py:278
  17.0 6.6 %collective-permute-start.1 = (bf16[32,1024]{1,0:T(8,128)(2,1)S(1)}, bf16[32,1024]{1,0:T(8,128)(2,1)S(1)}, u32[]{:S(2)}, u32[]{:S(2)}) collective-permute-start(bf16[32,1024]{1,0:T(8,128)(2,1)S(1)} %collective-permute-done), channel_id=1, source_target_pairs={{0,2},{1,31},{2,4},{3,1},{4,6},{5,3},{6,8},{7,5},{8,10},{9,7},{10,... | collective-permute-start | bytes 196616 | tf_op jit(solution)/shard_map/ppermute | solution.py:305
  39.0 7.6 %collective-permute-start.7 = (bf16[256,128]{1,0:T(8,128)(2,1)S(1)}, bf16[256,128]{1,0:T(8,128)(2,1)S(1)}, u32[]{:S(2)}, u32[]{:S(2)}) collective-permute-start(bf16[256,128]{1,0:T(8,128)(2,1)S(1)} %shard_map.120.p0), channel_id=1, source_target_pairs={{0,192},{32,224},{64,128},{96,160},{128,64},{160,96},{192,0},{224,... | collective-permute-start | bytes 196616 | tf_op jit(solution)/shard_map/ppermute | solution.py:278
  41.8 8.2 %collective-permute-start.5 = (bf16[256,128]{1,0:T(8,128)(2,1)S(1)}, bf16[256,128]{1,0:T(8,128)(2,1)S(1)}, u32[]{:S(2)}, u32[]{:S(2)}) collective-permute-start(bf16[256,128]{1,0:T(8,128)(2,1)S(1)} %shard_map.120.p0), channel_id=1, source_target_pairs={{0,128},{32,160},{64,192},{96,224},{128,0},{160,32},{192,64},{224,... | collective-permute-start | bytes 196616 | tf_op jit(solution)/shard_map/ppermute | solution.py:278
  41.8 11.3 %collective-permute-start.3 = (bf16[256,128]{1,0:T(8,128)(2,1)S(1)}, bf16[256,128]{1,0:T(8,128)(2,1)S(1)}, u32[]{:S(2)}, u32[]{:S(2)}) collective-permute-start(bf16[256,128]{1,0:T(8,128)(2,1)S(1)} %shard_map.120.p0), channel_id=1, source_target_pairs={{0,64},{32,96},{64,0},{96,32},{128,192},{160,224},{192,128},{224,1... | collective-permute-start | bytes 196616 | tf_op jit(solution)/shard_map/ppermute | solution.py:278
  42.7 10.4 %collective-permute-start.2 = (bf16[256,128]{1,0:T(8,128)(2,1)S(1)}, bf16[256,128]{1,0:T(8,128)(2,1)S(1)}, u32[]{:S(2)}, u32[]{:S(2)}) collective-permute-start(bf16[256,128]{1,0:T(8,128)(2,1)S(1)} %shard_map.120.p0), channel_id=1, source_target_pairs={{0,32},{32,0},{64,96},{96,64},{128,160},{160,128},{192,224},{224,1... | collective-permute-start | bytes 196616 | tf_op jit(solution)/shard_map/ppermute | solution.py:278
  46.6 6.5 %collective-permute-start.8 = (bf16[256,128]{1,0:T(8,128)(2,1)S(1)}, bf16[256,128]{1,0:T(8,128)(2,1)S(1)}, u32[]{:S(2)}, u32[]{:S(2)}) collective-permute-start(bf16[256,128]{1,0:T(8,128)(2,1)S(1)} %collective-permute-done.7.p6), channel_id=1, source_target_pairs={{0,32},{32,0},{64,96},{96,64},{128,160},{160,128},{192,224},{224,1... | collective-permute-start | bytes 196616 | tf_op jit(solution)/shard_map/ppermute | solution.py:278
  50.1 3.9 %collective-permute-start.6 = (bf16[256,128]{1,0:T(8,128)(2,1)S(1)}, bf16[256,128]{1,0:T(8,128)(2,1)S(1)}, u32[]{:S(2)}, u32[]{:S(2)}) collective-permute-start(bf16[256,128]{1,0:T(8,128)(2,1)S(1)} %collective-permute-done.5.p4), channel_id=1, source_target_pairs={{0,32},{32,0},{64,96},{96,64},{128,160},{160,128},{192,224},{224,1... | collective-permute-start | bytes 196616 | tf_op jit(solution)/shard_map/ppermute | solution.py:278
  82.7 58.3 %all-to-all-start = ((bf16[32,32,512]{2,1,0:T(8,128)(2,1)}), bf16[32,32,512]{2,1,0:T(8,128)(2,1)S(1)}, u32[]{:S(2)}, u32[]{:S(2)}) async-start(bf16[32,32,512]{2,1,0:T(8,128)(2,1)} %bitcast.5), calls=%async_computation | async-start | bytes 2097152 | tf_op jit(solution)/shard_map/all_to_all | solution.py:358
  93.2 7.1 %collective-permute-start.9 = (bf16[96,256]{1,0:T(8,128)(2,1)S(1)}, bf16[96,256]{1,0:T(8,128)(2,1)S(1)}, u32[]{:S(2)}, u32[]{:S(2)}) collective-permute-start(bf16[96,256]{1,0:T(8,128)(2,1)S(1)} %get-tuple-element.31), channel_id=1, source_target_pairs={{0,32},{32,0},{64,96},{96,64},{128,160},{160,128},{192,224},{224,1... | collective-permute-start | bytes 147464 | tf_op jit(solution)/shard_map/ppermute | solution.py:278
  95.9 21.2 %collective-permute-start.10 = (bf16[96,256]{1,0:T(8,128)(2,1)S(1)}, bf16[96,256]{1,0:T(8,128)(2,1)S(1)}, u32[]{:S(2)}, u32[]{:S(2)}) collective-permute-start(bf16[96,256]{1,0:T(8,128)(2,1)S(1)} %get-tuple-element.32), channel_id=1, source_target_pairs={{0,64},{32,96},{64,0},{96,32},{128,192},{160,224},{192,128},{224,1... | collective-permute-start | bytes 147464 | tf_op jit(solution)/shard_map/ppermute | solution.py:278
  95.9 27.6 %collective-permute-start.11 = (bf16[96,256]{1,0:T(8,128)(2,1)S(1)}, bf16[96,256]{1,0:T(8,128)(2,1)S(1)}, u32[]{:S(2)}, u32[]{:S(2)}) collective-permute-start(bf16[96,256]{1,0:T(8,128)(2,1)S(1)} %get-tuple-element.33), channel_id=1, source_target_pairs={{0,96},{32,64},{64,32},{96,0},{128,224},{160,192},{192,160},{224,1... | collective-permute-start | bytes 147464 | tf_op jit(solution)/shard_map/ppermute | solution.py:278
  97.6 25.9 %collective-permute-start.12 = (bf16[96,256]{1,0:T(8,128)(2,1)S(1)}, bf16[96,256]{1,0:T(8,128)(2,1)S(1)}, u32[]{:S(2)}, u32[]{:S(2)}) collective-permute-start(bf16[96,256]{1,0:T(8,128)(2,1)S(1)} %get-tuple-element.34), channel_id=1, source_target_pairs={{0,128},{32,160},{64,192},{96,224},{128,0},{160,32},{192,64},{224,... | collective-permute-start | bytes 147464 | tf_op jit(solution)/shard_map/ppermute | solution.py:278
  98.0 28.4 %collective-permute-start.13 = (bf16[96,256]{1,0:T(8,128)(2,1)S(1)}, bf16[96,256]{1,0:T(8,128)(2,1)S(1)}, u32[]{:S(2)}, u32[]{:S(2)}) collective-permute-start(bf16[96,256]{1,0:T(8,128)(2,1)S(1)} %get-tuple-element.35), channel_id=1, source_target_pairs={{0,160},{32,128},{64,224},{96,192},{128,32},{160,0},{192,96},{224,... | collective-permute-start | bytes 147464 | tf_op jit(solution)/shard_map/ppermute | solution.py:278
  100.3 26.1 %collective-permute-start.14 = (bf16[96,256]{1,0:T(8,128)(2,1)S(1)}, bf16[96,256]{1,0:T(8,128)(2,1)S(1)}, u32[]{:S(2)}, u32[]{:S(2)}) collective-permute-start(bf16[96,256]{1,0:T(8,128)(2,1)S(1)} %get-tuple-element.36), channel_id=1, source_target_pairs={{0,192},{32,224},{64,128},{96,160},{128,64},{160,96},{192,0},{224,... | collective-permute-start | bytes 147464 | tf_op jit(solution)/shard_map/ppermute | solution.py:278
  117.1 9.3 %collective-permute-start.15 = (bf16[96,256]{1,0:T(8,128)(2,1)S(1)}, bf16[96,256]{1,0:T(8,128)(2,1)S(1)}, u32[]{:S(2)}, u32[]{:S(2)}) collective-permute-start(bf16[96,256]{1,0:T(8,128)(2,1)S(1)} %get-tuple-element.37), channel_id=1, source_target_pairs={{0,224},{32,192},{64,160},{96,128},{128,96},{160,64},{192,32},{224... | collective-permute-start | bytes 147464 | tf_op jit(solution)/shard_map/ppermute | solution.py:278
  130.1 6.3 %collective-permute-start.16 = (bf16[32,1024]{1,0:T(8,128)(2,1)S(1)}, bf16[32,1024]{1,0:T(8,128)(2,1)S(1)}, u32[]{:S(2)}, u32[]{:S(2)}) collective-permute-start(bf16[32,1024]{1,0:T(8,128)(2,1)S(1)} %get-tuple-element.40), channel_id=1, source_target_pairs={{0,30},{1,3},{2,0},{3,5},{4,2},{5,7},{6,4},{7,9},{8,6},{9,11},{10,... | collective-permute-start | bytes 196616 | tf_op jit(solution)/shard_map/ppermute | solution.py:390
  136.4 15.3 %collective-permute-start.17 = (bf16[32,1024]{1,0:T(8,128)(2,1)S(1)}, bf16[32,1024]{1,0:T(8,128)(2,1)S(1)}, u32[]{:S(2)}, u32[]{:S(2)}) collective-permute-start(bf16[32,1024]{1,0:T(8,128)(2,1)S(1)} %add_convert_fusion), channel_id=1, source_target_pairs={{0,1},{1,0},{2,3},{3,2},{4,5},{5,4},{6,7},{7,6},{8,9},{9,8},{10,11... | collective-permute-start | bytes 196616 | tf_op jit(solution)/shard_map/ppermute | solution.py:278
  141.7 7.3 %collective-permute-start.23 = (bf16[32,512]{1,0:T(8,128)(2,1)S(1)}, bf16[32,512]{1,0:T(8,128)(2,1)S(1)}, u32[]{:S(2)}, u32[]{:S(2)}) collective-permute-start(bf16[32,512]{1,0:T(8,128)(2,1)S(1)} %get-tuple-element.41.g0), channel_id=1, source_target_pairs={{0,192},{32,224},{64,128},{96,160},{128,64},{160,96},{192,0},{224,... | collective-permute-start | bytes 98312 | tf_op jit(solution)/shard_map/ppermute | solution.py:278
  142.9 7.4 %collective-permute-start.21 = (bf16[32,512]{1,0:T(8,128)(2,1)S(1)}, bf16[32,512]{1,0:T(8,128)(2,1)S(1)}, u32[]{:S(2)}, u32[]{:S(2)}) collective-permute-start(bf16[32,512]{1,0:T(8,128)(2,1)S(1)} %get-tuple-element.41.g0), channel_id=1, source_target_pairs={{0,128},{32,160},{64,192},{96,224},{128,0},{160,32},{192,64},{224,... | collective-permute-start | bytes 98312 | tf_op jit(solution)/shard_map/ppermute | solution.py:278
  143.6 8.1 %collective-permute-start.19 = (bf16[32,512]{1,0:T(8,128)(2,1)S(1)}, bf16[32,512]{1,0:T(8,128)(2,1)S(1)}, u32[]{:S(2)}, u32[]{:S(2)}) collective-permute-start(bf16[32,512]{1,0:T(8,128)(2,1)S(1)} %get-tuple-element.41.g0), channel_id=1, source_target_pairs={{0,64},{32,96},{64,0},{96,32},{128,192},{160,224},{192,128},{224,1... | collective-permute-start | bytes 98312 | tf_op jit(solution)/shard_map/ppermute | solution.py:278
  145.2 7.2 %collective-permute-start.18 = (bf16[32,512]{1,0:T(8,128)(2,1)S(1)}, bf16[32,512]{1,0:T(8,128)(2,1)S(1)}, u32[]{:S(2)}, u32[]{:S(2)}) collective-permute-start(bf16[32,512]{1,0:T(8,128)(2,1)S(1)} %get-tuple-element.41.g0), channel_id=1, source_target_pairs={{0,32},{32,0},{64,96},{96,64},{128,160},{160,128},{192,224},{224,1... | collective-permute-start | bytes 98312 | tf_op jit(solution)/shard_map/ppermute | solution.py:278
  149.0 3.4 %collective-permute-start.24 = (bf16[32,512]{1,0:T(8,128)(2,1)S(1)}, bf16[32,512]{1,0:T(8,128)(2,1)S(1)}, u32[]{:S(2)}, u32[]{:S(2)}) collective-permute-start(bf16[32,512]{1,0:T(8,128)(2,1)S(1)} %collective-permute-done.23.g6), channel_id=1, source_target_pairs={{0,32},{32,0},{64,96},{96,64},{128,160},{160,128},{192,224},{224,1... | collective-permute-start | bytes 98312 | tf_op jit(solution)/shard_map/ppermute | solution.py:278
  (10 other events, 57.9 us)
Sparse Core Ops, SparseCore 0:
  25.3 41.0 all-gather.2

commit v2 on v1

v2 whole, which is shorter than its diff:
```python
import jax
import jax.numpy as jnp
from jax import lax
from jax.experimental import pallas as pl
from jax.experimental.pallas import tpu as pltpu
from jax.sharding import PartitionSpec as P

F32 = jnp.float32
BF16 = jnp.bfloat16
TILE = 128
SIZE = 64
TILES = 8
MEMBERS = 8
SHARDS = 32
NODES = 32
WIDE = 96
BOTH = 2 * WIDE
ROWS = 256
WIDTH = 1024
VARS = 100
CARRY = 112
PAIR = 1.0 / (MEMBERS * (MEMBERS - 1))
SCALE = (MEMBERS * ROWS * SHARDS) ** (-0.5)
VMEM = pl.BlockSpec(memory_space=pltpu.VMEM)
SMEM = pl.BlockSpec(memory_space=pltpu.SMEM)


def dot(left, right):
    return lax.dot_general(left, right, (((1,), (0,)), ((), ())), preferred_element_type=F32)


def dot_nt(left, right):
    return lax.dot_general(left, right, (((1,), (1,)), ((), ())), preferred_element_type=F32)


def dot_tn(left, right):
    return lax.dot_general(left, right, (((0,), (0,)), ((), ())), preferred_element_type=F32)


def call(body, outs, specs, scratch=(), flops=0, size=0):
    return pl.pallas_call(
        body,
        out_shape=outs,
        in_specs=specs,
        out_specs=[VMEM] * len(outs),
        scratch_shapes=list(scratch),
        compiler_params=pltpu.CompilerParams(vmem_limit_bytes=40 * 1024 * 1024),
        cost_estimate=pl.CostEstimate(flops=flops, bytes_accessed=size, transcendentals=0),
    )


def iota(shape, dim):
    return lax.broadcasted_iota(jnp.int32, shape, dim)


def lane_mean(values):
    average = jnp.where(
        iota((TILE, TILE), 0) // SIZE == iota((TILE, TILE), 1) // SIZE, 1.0 / SIZE, 0.0
    ).astype(BF16)
    high = values.astype(BF16)
    low = (values - high.astype(F32)).astype(BF16)
    return dot(high, average) + dot(low, average)


def stack_heads(tile):
    first = iota(tile.shape, 1) < SIZE
    zero = jnp.zeros_like(tile)
    return jnp.concatenate([jnp.where(first, tile, zero), jnp.where(first, zero, tile)], 0)


def unstack_heads(both):
    first = iota((WIDE, TILE), 1) < SIZE
    return jnp.where(first, both[:WIDE], both[WIDE:])


def per_half(values, size, first, second):
    return jnp.concatenate([values[:size] * first, values[size:] * second], 0)


def half_sums(values):
    return (
        jnp.sum(values[:WIDE], 0, keepdims=True),
        jnp.sum(values[WIDE:], 0, keepdims=True),
    )


def key_parts(raw):
    root = lax.rsqrt(lane_mean(raw * raw) + 1e-06)
    return raw * root, root


def attention(query, key, value, count):
    score = dot(key, query)
    expon = jnp.exp(score * SIZE**-0.5)
    expon = jnp.concatenate([expon[:WIDE] * count, expon[WIDE:] * count], 0)
    first, second = half_sums(expon)
    weight = per_half(expon, WIDE, 1.0 / first, 1.0 / second).astype(BF16)
    return weight, dot_tn(value, weight)


def attention_back(weight, value, query, d_mixed):
    d_weight = dot(value, d_mixed)
    wide = weight.astype(F32)
    first, second = half_sums(wide * d_weight)
    d_score = jnp.concatenate([d_weight[:WIDE] - first, d_weight[WIDE:] - second], 0)
    d_score = (wide * d_score * SIZE**-0.5).astype(BF16)
    return d_score, unstack_heads(dot_nt(weight, d_mixed)), unstack_heads(dot_nt(d_score, query))


def key_back(d_key, normal, root):
    return root * (d_key - normal * lane_mean(d_key * normal))


def norm_back(d_normed, normed, d_pred, pred, head_sum, scale):
    wide = d_pred.astype(F32)
    level = jnp.sum(wide * head_sum, 0, keepdims=True) / WIDTH
    along = jnp.sum(wide * pred, 0, keepdims=True) / WIDTH
    return (scale * (d_normed - level - normed * along)).astype(BF16)


def stats_of(payload):
    pred = payload.astype(F32)
    mean = pred[VARS : VARS + 1] + pred[VARS + 1 : VARS + 2]
    scale = pred[VARS + 2 : VARS + 3] + pred[VARS + 3 : VARS + 4]
    return pred, mean, scale


def prepare_kernel(
    me, embed, w_query, w_keyval, w_head, edges, target,
    normal, normal_tile, inverse, embed_turned, embed_tile, keyval_tile,
    head_turned, head, head_tile, head_sum, count, aim,
):
    here = me[0]
    shard = me[1]
    at = pl.multiple_of(here * TILE, TILE)
    embed_turned[...] = embed[...].T
    embed_tile[...] = embed_turned[pl.ds(at, TILE), :]
    value = dot(embed[...], w_query[...]).T
    held = jnp.zeros((TILE, ROWS), F32)
    for t in range(TILES):
        roots = []
        for h in (2 * t, 2 * t + 1):
            part = value[h * SIZE : (h + 1) * SIZE]
            root = lax.rsqrt(jnp.mean(part * part, 0, keepdims=True) + 1e-06)
            normal[h * SIZE : (h + 1) * SIZE, :] = (part * root).astype(BF16)
            roots.append(jnp.broadcast_to(root, (SIZE, ROWS)))
        held = jnp.where(here == t, jnp.concatenate(roots, 0), held)
    inverse[...] = held
    normal_tile[...] = normal[pl.ds(at, TILE), :]
    keyval_tile[:, :TILE] = w_keyval[:, pl.ds(at, TILE)]
    keyval_tile[:, TILE:] = w_keyval[:, pl.ds(pl.multiple_of(WIDTH + at, TILE), TILE)]
    rows = jnp.concatenate([w_head[...], jnp.zeros((TILE - VARS, WIDTH), BF16)], 0)
    head_turned[...] = rows[:CARRY]
    head[...] = rows.T
    head_tile[...] = head[pl.ds(at, TILE), :]
    head_sum[...] = jnp.sum(rows.astype(F32), 1, keepdims=True)
    source = edges[...]
    offset = jnp.bitwise_and(jnp.right_shift(source, 5) - shard + SHARDS, SHARDS - 1)
    toward = jnp.where(jnp.bitwise_and(shard, 1) == 0, 1, SHARDS - 1)
    slot = jnp.where(offset == 0, 0, jnp.where(offset == toward, 1, 2))
    index = slot * NODES + jnp.bitwise_and(source, NODES - 1)
    node = iota((WIDE, ROWS), 0)
    total = jnp.zeros((WIDE, ROWS), F32)
    for k in range(3):
        total = total + jnp.where(index[k : k + 1] == node, 1.0, 0.0)
    count[...] = total
    aim[...] = jnp.concatenate([target[...], jnp.zeros((CARRY - VARS, ROWS), F32)], 0)


def forward_kernel(
    own, partner, other, w_keyval, normal, embed, count, head_turned,
    payload, weights, normed, keys, key_roots, values, hidden,
):
    counts = count[...]
    wide = jnp.concatenate([own[...], partner[...], other[...]], 0)
    table = dot(wide, w_keyval[...]).astype(BF16)
    for t in range(TILES):
        at = slice(t * TILE, (t + 1) * TILE)
        key, root = key_parts(table[:, at].astype(F32))
        value = table[:, WIDTH + t * TILE : WIDTH + (t + 1) * TILE]
        keys[:, at] = key.astype(BF16)
        key_roots[:, at] = root
        values[:, at] = value
        weight, mixed = attention(
            normal[at, :], stack_heads(key.astype(BF16)), stack_heads(value), counts
        )
        weights[t] = weight
        hidden[at, :] = embed[at, :].astype(F32) + mixed
    whole = hidden[...]
    mean = jnp.mean(whole, 0, keepdims=True)
    center = whole - mean
    scale = lax.rsqrt(jnp.mean(center * center, 0, keepdims=True) + 1e-05)
    result = (center * scale).astype(BF16)
    normed[...] = result
    pred = dot(head_turned[...], result)
    row = iota(pred.shape, 0)
    for at, stat in ((VARS, mean), (VARS + 2, scale)):
        high = stat.astype(BF16).astype(F32)
        pred = jnp.where(row == at, high, pred)
        pred = jnp.where(row == at + 1, stat - high, pred)
    payload[...] = pred.astype(BF16)


def tables_kernel(*refs):
    latents = refs[: 3 * MEMBERS]
    keyval_tile, normal_tile, embed_tile, count = refs[3 * MEMBERS : 3 * MEMBERS + 4]
    turned, weights, keys, key_roots, values, hidden, flat = refs[3 * MEMBERS + 4 :]
    for i, latent in enumerate(latents):
        flat[i * NODES : (i + 1) * NODES, :] = latent[...]
    turned[...] = flat[...].T
    table = dot(flat[...], keyval_tile[...]).astype(BF16)
    counts = count[...]
    query = normal_tile[...]
    base = embed_tile[...].astype(F32)
    for k in range(MEMBERS):
        part = table[k * WIDE : (k + 1) * WIDE]
        key, root = key_parts(part[:, :TILE].astype(F32))
        keys[k] = key.astype(BF16)
        key_roots[k] = root
        values[k] = part[:, TILE:]
        weight, mixed = attention(
            query, stack_heads(key.astype(BF16)), stack_heads(part[:, TILE:]), counts
        )
        weights[k] = weight
        hidden[k] = base + mixed


def crps(preds, target, area, d_pred, lost):
    size = 16
    d_pred[:, CARRY:, :] = jnp.zeros((MEMBERS, TILE - CARRY, ROWS), BF16)

    @pl.loop(0, CARRY // size)
    def _(step):
        start = pl.multiple_of(step * size, size)
        rows = pl.ds(start, size)
        for side in range(0, ROWS, TILE):
            cols = slice(side, side + TILE)
            value = [preds[k][rows, cols].astype(F32) for k in range(MEMBERS)]
            slope = [jnp.zeros((size, TILE), F32) for _ in range(MEMBERS)]
            weight = jnp.where(iota((size, TILE), 0) + start < VARS, area[:, cols], 0.0)
            aim = target[rows, cols]
            pair = jnp.zeros((size, TILE), F32)
            for i in range(MEMBERS):
                for j in range(i + 1, MEMBERS):
                    delta = value[i] - value[j]
                    square = delta * delta + 0.0625
                    root = lax.rsqrt(square)
                    if i == 0:
                        pair = pair + square * root
                    part = delta * root
                    slope[i] = slope[i] + part
                    slope[j] = slope[j] - part
            for i in range(MEMBERS):
                delta = value[i] - aim
                square = delta * delta + 0.0625
                root = lax.rsqrt(square)
                if i == 0:
                    lost[rows, cols] = weight * (square * root / MEMBERS - 0.5 * PAIR * pair)
                d_pred[i, rows, cols] = (
                    weight * (delta * root / MEMBERS - PAIR * slope[i])
                ).astype(BF16)


def backward_kernel(
    me, turned, weights, keys, key_roots, values, hidden, normal_tile, inverse, embed_turned,
    head_tile, head_sum, target, area, p0, p1, p2, p3, p4, p5, p6, p7,
    payload, d_own, d_pred, lost, d_table,
):
    preds = (p0, p1, p2, p3, p4, p5, p6, p7)
    here = me[0]
    crps(preds, target, area, d_pred, lost)
    d_own[...] = d_pred[0]
    query = normal_tile[...]
    sums = head_sum[...]
    d_query = jnp.zeros((TILE, ROWS), F32)
    d_head = jnp.zeros((TILE, TILE), F32)
    for k in range(MEMBERS):
        pred, mean, scale = stats_of(preds[k][...])
        normed = (hidden[k] - mean) * scale
        out = d_pred[k]
        d_head = d_head + dot_nt(normed.astype(BF16), out)
        d_mixed = norm_back(
            dot(head_tile[...], out), normed, out[:CARRY], pred, sums[:CARRY], scale
        )
        key = keys[k]
        value = stack_heads(values[k])
        d_score, d_value, d_key = attention_back(weights[k], value, query, d_mixed)
        d_query = d_query + dot_tn(stack_heads(key), d_score)
        d_key = key_back(d_key, key.astype(F32), key_roots[k])
        rows = slice(k * WIDE, (k + 1) * WIDE)
        d_table[rows, :TILE] = d_key.astype(BF16)
        d_table[rows, TILE:] = d_value.astype(BF16)
    wide_query = query.astype(F32)
    along = d_query * wide_query
    along = jnp.concatenate(
        [
            jnp.broadcast_to(jnp.mean(along[:SIZE], 0, keepdims=True), (SIZE, ROWS)),
            jnp.broadcast_to(jnp.mean(along[SIZE:], 0, keepdims=True), (SIZE, ROWS)),
        ],
        0,
    )
    d_query = inverse[...] * (d_query - wide_query * along)
    grad = dot_nt(embed_turned[...], d_query.astype(BF16))
    payload[:, :TILE] = (grad * SCALE).astype(BF16)
    grad = dot(turned[...], d_table[...])
    payload[:, TILE : 3 * TILE] = (grad * SCALE).astype(BF16)
    loss = jnp.sum(lost[...], axis=(0, 1), keepdims=True) / (ROWS * SHARDS * VARS)
    high = loss.astype(BF16).astype(F32)
    lane = iota((WIDTH, TILE), 1)
    side = jnp.where(lane == VARS, high, jnp.where(lane == VARS + 1, loss - high, 0.0))
    payload[:, 3 * TILE :] = side.astype(BF16)
    rows = pl.ds(pl.multiple_of(here * TILE, TILE), TILE)
    payload[rows, 3 * TILE :] = jnp.where(
        iota((TILE, TILE), 1) < VARS, d_head * SCALE, side[:TILE]
    ).astype(BF16)


def latent_kernel(
    d_own, payload, weights, normed, keys, key_roots, values, normal, head, head_sum, w_keyval,
    own, partner, other, d_table,
):
    out = d_own[...]
    pred, mean, scale = stats_of(payload[...])
    d_normed = dot(head[...], out)
    d_mixed = norm_back(
        d_normed, normed[...].astype(F32), out[:CARRY], pred, head_sum[:CARRY], scale
    )
    for t in range(TILES):
        at = slice(t * TILE, (t + 1) * TILE)
        key = keys[:, at]
        d_score, d_value, d_key = attention_back(
            weights[t], stack_heads(values[:, at]), normal[at, :], d_mixed[at]
        )
        d_key = key_back(d_key, key.astype(F32), key_roots[:, at])
        d_table[:, at] = d_key.astype(BF16)
        d_table[:, WIDTH + t * TILE : WIDTH + (t + 1) * TILE] = d_value.astype(BF16)
    total = dot_nt(d_table[...], w_keyval[...])
    own[...] = total[:NODES]
    partner[...] = total[NODES : 2 * NODES]
    other[...] = total[2 * NODES :].astype(BF16)


def sum_kernel(pieces, total, loss):
    value = jnp.sum(pieces[...].astype(F32), 0)
    total[...] = value.astype(BF16)
    at = 3 * TILE + VARS
    loss[...] = value[0:1, at : at + 1] + value[0:1, at + 1 : at + 2]


def place_kernel(me, g0, g1, g2, g3, g4, g5, g6, g7, query, keyval, head):
    here = me[0]
    total = jnp.zeros((NODES, TILE), F32)
    for k, part in enumerate((g0, g1, g2, g3, g4, g5, g6, g7)):
        at = pl.multiple_of(jnp.bitwise_xor(here, k) * TILE, TILE)
        query[:, pl.ds(at, TILE)] = part[:, :TILE].astype(F32)
        keyval[:, pl.ds(at, TILE)] = part[:, TILE : 2 * TILE].astype(F32)
        keyval[:, pl.ds(pl.multiple_of(WIDTH + at, TILE), TILE)] = part[
            :, 2 * TILE : 3 * TILE
        ].astype(F32)
        total = total + part[:, 3 * TILE :].astype(F32)
    head[...] = total[:, :VARS]


def swap(array, axis, bits):
    count = lax.axis_size(axis)
    return lax.ppermute(array, axis, [(i, i ^ bits) for i in range(count)])


def outward(sign):
    step = lambda i: 2 * sign if i % 2 == 0 else -2 * sign
    return [(i, (i + step(i)) % SHARDS) for i in range(SHARDS)]


def spread(array):
    slots = {0: array}
    for k in (6, 4, 2):
        slots[k] = swap(array, "member", k)
    for k in (0, 2, 4, 6):
        slots[k + 1] = swap(slots[k], "member", 1)
    return [slots[k] for k in range(MEMBERS)]


def shape(*dims, kind=BF16):
    return jax.ShapeDtypeStruct(dims, kind)


def on_device(latent, grid_embed, edge_src, area, target, w_query, w_keyval, w_head):
    member = lax.axis_index("member").astype(jnp.int32)
    shard = lax.axis_index("shard").astype(jnp.int32)
    me = jnp.stack([member, shard])
    own = latent[0]
    partner = swap(own, "shard", 1)
    other = lax.ppermute(partner, "shard", outward(1))
    (
        normal, normal_tile, inverse, embed_turned, embed_tile, keyval_tile,
        head_turned, head, head_tile, head_sum, count, aim,
    ) = call(
        prepare_kernel,
        [
            shape(WIDTH, ROWS),
            shape(TILE, ROWS),
            shape(TILE, ROWS, kind=F32),
            shape(WIDTH, ROWS),
            shape(TILE, ROWS),
            shape(WIDTH, 2 * TILE),
            shape(CARRY, WIDTH),
            shape(WIDTH, TILE),
            shape(TILE, TILE),
            shape(TILE, 1, kind=F32),
            shape(WIDE, ROWS, kind=F32),
            shape(CARRY, ROWS, kind=F32),
        ],
        [SMEM] + [VMEM] * 6,
        flops=2 * ROWS * WIDTH * WIDTH,
        size=8 << 20,
    )(me, grid_embed, w_query, w_keyval, w_head.T, edge_src.T, target.T)
    payload, weights, normed, keys, key_roots, values = call(
        forward_kernel,
        [
            shape(CARRY, ROWS),
            shape(TILES, BOTH, ROWS),
            shape(WIDTH, ROWS),
            shape(WIDE, WIDTH),
            shape(WIDE, WIDTH, kind=F32),
            shape(WIDE, WIDTH),
        ],
        [VMEM] * 8,
        [pltpu.VMEM((WIDTH, ROWS), F32)],
        flops=1 << 30,
        size=8 << 20,
    )(own, partner, other, w_keyval, normal, embed_turned, count, head_turned)
    preds = spread(payload)
    blocks = [spread(part) for part in (own, partner, other)]
    latents = [blocks[i][k] for k in range(MEMBERS) for i in range(3)]
    member_parts = call(
        tables_kernel,
        [
            shape(WIDTH, MEMBERS * WIDE),
            shape(MEMBERS, BOTH, ROWS),
            shape(MEMBERS, WIDE, TILE),
            shape(MEMBERS, WIDE, TILE, kind=F32),
            shape(MEMBERS, WIDE, TILE),
            shape(MEMBERS, TILE, ROWS, kind=F32),
        ],
        [VMEM] * (3 * MEMBERS + 4),
        [pltpu.VMEM((MEMBERS * WIDE, WIDTH), BF16)],
        flops=2 << 30,
        size=8 << 20,
    )(*latents, keyval_tile, normal_tile, embed_tile, count)
    grads, d_own = call(
        backward_kernel,
        [shape(WIDTH, 4 * TILE), shape(TILE, ROWS)],
        [SMEM] + [VMEM] * 21,
        [
            pltpu.VMEM((MEMBERS, TILE, ROWS), BF16),
            pltpu.VMEM((CARRY, ROWS), F32),
            pltpu.VMEM((MEMBERS * WIDE, 2 * TILE), BF16),
        ],
        flops=2 << 30,
        size=8 << 20,
    )(
        me, *member_parts, normal_tile, inverse, embed_turned, head_tile, head_sum, aim,
        area.reshape(1, ROWS), *preds,
    )
    pieces = lax.all_to_all(
        grads.reshape(SHARDS, NODES, 4 * TILE), "shard", 0, 0, tiled=False
    )
    total, loss = call(
        sum_kernel,
        [shape(NODES, 4 * TILE), shape(1, 1, kind=F32)],
        [VMEM],
        flops=1 << 20,
        size=1 << 20,
    )(pieces)
    parts = spread(total)
    grad_query, grad_keyval, grad_head = call(
        place_kernel,
        [
            shape(NODES, WIDTH, kind=F32),
            shape(NODES, 2 * WIDTH, kind=F32),
            shape(NODES, VARS, kind=F32),
        ],
        [SMEM] + [VMEM] * MEMBERS,
        size=1 << 20,
    )(me, *parts)
    mine, near, far = call(
        latent_kernel,
        [
            shape(NODES, WIDTH, kind=F32),
            shape(NODES, WIDTH, kind=F32),
            shape(NODES, WIDTH),
        ],
        [VMEM] * 11,
        [pltpu.VMEM((WIDE, 2 * WIDTH), BF16)],
        flops=1 << 30,
        size=8 << 20,
    )(
        d_own, payload, weights, normed, keys, key_roots, values, normal, head, head_sum,
        w_keyval,
    )
    near = near + lax.ppermute(far, "shard", outward(-1)).astype(F32)
    d_latent = mine + swap(near.astype(BF16), "shard", 1).astype(F32)
    return (loss.reshape(1), d_latent[None], grad_query, grad_keyval, grad_head)


def solution(mesh):
    placed = (
        P("member", "shard", None),
        P("shard", None),
        P("shard", None),
        P("shard"),
        P("shard", None),
        P(),
        P(),
        P(),
    )
    return jax.shard_map(
        on_device,
        mesh=mesh,
        in_specs=placed,
        out_specs=(
            P("member"),
            P("member", "shard", None),
            P("shard", None),
            P("shard", None),
            P("shard", None),
        ),
        check_vma=False,
    )
```

time: 161 us -> 119 us (0.74)
  waiting for transfers between devices: 40.6 us -> 6.93 us
  between operations: 14.2 us -> 0.84 us
  local copies, waits for them, and re-layouts: 11.5 us -> 15.9 us
  starting transfers between devices: 68.2 us -> 71.5 us
  other arithmetic: 3.35 us -> 1.67 us
    ppermute x23 -> x37, waiting for transfers between devices: 22 us -> 4.89 us  [swap(): return lax.ppermute(array, axis, [(i, i ^ bits) for i in range(count)])]
    all_gather x1 -> x0, waiting for transfers between devices: 12 us -> none  [on_device(): latents = lax.all_gather(wide, 'member', axis=0, tiled=False)]
    unnamed x17 -> x42, local copies, waits for them, and re-layouts: 9.38 us -> 15.9 us
    ppermute x1, waiting for transfers between devices: 5.29 us -> 0.01 us  [on_device(): other = lax.ppermute(partner, 'shard', outward(1))]
    ppermute x23 -> x37, starting transfers between devices: 51.4 us -> 56.4 us  [swap(): return lax.ppermute(array, axis, [(i, i ^ bits) for i in range(count)])]
    pallas_call x3 -> x4, Pallas kernels: 19.7 us -> 16.2 us  [the longest x1 7.49 us: on_device(): call(backward_kernel, [shape(WIDTH, 4 * TILE), shape(TILE, ROWS)], [SMEM]...]
    pallas_call x1, Pallas kernels: 1.49 us -> 3.67 us  [on_device(): call(latent_kernel, [shape(NODES, WIDTH, kind=F32), shape(NODES, WIDTH, k...]
  transfers between devices with their start and end apart: 27 -> 40, of which waited for: 10 -> 4; matrix products, arithmetic and copies ran while one was open for 4% -> 1% of each run, Pallas kernels for 4% -> 11%
where the time goes in v2:
time: 119 us
  starting transfers between devices  71.5 us (60%)
  Pallas kernels  21.9 us (18%)
  local copies, waits for them, and re-layouts  15.9 us (13%)
  waiting for transfers between devices  6.93 us (6%)
  other arithmetic  1.67 us (1%)
    ppermute x37, starting transfers between devices, swap(): return lax.ppermute(array, axis, [(i, i ^ bits) for i in range(count)])  56.4 us
    unnamed x42, local copies, waits for them, and re-layouts  15.9 us
    all_to_all x1, starting transfers between devices, on_device(): lax.all_to_all(grads.reshape(SHARDS, NODES, 4 * TILE), 'shard', 0, 0, til...  9.13 us
    pallas_call x1, Pallas kernels, on_device(): call(backward_kernel, [shape(WIDTH, 4 * TILE), shape(TILE, ROWS)], [SMEM]...  7.49 us
    ppermute x37, waiting for transfers between devices, swap(): return lax.ppermute(array, axis, [(i, i ^ bits) for i in range(count)])  4.89 us
    ppermute x1, starting transfers between devices, on_device(): near = near + lax.ppermute(far, 'shard', outward(-1)).astype(F32)  4.71 us
    pallas_call x1, Pallas kernels, on_device(): call(tables_kernel, [shape(WIDTH, MEMBERS * WIDE), shape(MEMBERS, BOTH, R...  3.78 us
    pallas_call x1, Pallas kernels, on_device(): call(latent_kernel, [shape(NODES, WIDTH, kind=F32), shape(NODES, WIDTH, k...  3.67 us
  transfers between devices with their start and end apart: 40, of which 4 were waited for; matrix products, arithmetic and copies ran while one was open for 1% of the time, Pallas kernels for 11%

profile of v2, /device:TPU:1, one launch (start us, length us, event | category | flops | bytes accessed | tf_op | source)
XLA Modules:
  0.0 118.7 jit_solution(11287109975365845732)
XLA Ops:
  0.6 7.8 %collective-permute-start = (bf16[32,1024]{1,0:T(8,128)(2,1)}, bf16[32,1024]{1,0:T(8,128)(2,1)S(1)}, u32[]{:S(2)}, u32[]{:S(2)}) collective-permute-start(bf16[32,1024]{1,0:T(8,128)(2,1)} %bitcast.13), channel_id=1, source_target_pairs={{0,1},{1,0},{2,3},{3,2},{4,5},{5,4},{6,7},{7,6},{8,9},{9,8},{10,11... | collective-permute-start | bytes 196616 | tf_op jit(solution)/shard_map/ppermute | solution.py:366
  9.6 1.6 %collective-permute-start.17 = (bf16[32,1024]{1,0:T(8,128)(2,1)}, bf16[32,1024]{1,0:T(8,128)(2,1)S(1)}, u32[]{:S(2)}, u32[]{:S(2)}) collective-permute-start(bf16[32,1024]{1,0:T(8,128)(2,1)} %bitcast.15), channel_id=1, source_target_pairs={{0,192},{32,224},{64,128},{96,160},{128,64},{160,96},{192,0},{224,... | collective-permute-start | bytes 196616 | tf_op jit(solution)/shard_map/ppermute | solution.py:366
  11.3 1.6 %collective-permute-start.2 = (bf16[32,1024]{1,0:T(8,128)(2,1)}, bf16[32,1024]{1,0:T(8,128)(2,1)S(1)}, u32[]{:S(2)}, u32[]{:S(2)}) collective-permute-start(bf16[32,1024]{1,0:T(8,128)(2,1)} %bitcast.17), channel_id=1, source_target_pairs={{0,32},{32,0},{64,96},{96,64},{128,160},{160,128},{192,224},{224,1... | collective-permute-start | bytes 196616 | tf_op jit(solution)/shard_map/ppermute | solution.py:366
  14.2 3.2 %collective-permute-done.11.refs_12_ = bf16[32,1024]{1,0:T(8,128)(2,1)S(1)} collective-permute-done((bf16[32,1024]{1,0:T(8,128)(2,1)}, bf16[32,1024]{1,0:T(8,128)(2,1)S(1)}, u32[]{:S(2)}, u32[]{:S(2)}) %collective-permute-start.11) | collective-permute-done | bytes 65568 | tf_op jit(solution)/shard_map/ppermute | solution.py:366
  17.5 1.9 %collective-permute-start.18 = (bf16[32,1024]{1,0:T(8,128)(2,1)S(1)}, bf16[32,1024]{1,0:T(8,128)(2,1)S(1)}, u32[]{:S(2)}, u32[]{:S(2)}) collective-permute-start(bf16[32,1024]{1,0:T(8,128)(2,1)S(1)} %collective-permute-done.refs_1_.partner), channel_id=1, source_target_pairs={{0,192},{32,224},{64,128},{96,160},{128,64},{160,96},{192,0},{224,... | collective-permute-start | bytes 196616 | tf_op jit(solution)/shard_map/ppermute | solution.py:366
  19.5 2.2 %copy-done = bf16[1024,2048]{1,0:T(8,128)(2,1)S(1)} copy-done((bf16[1024,2048]{1,0:T(8,128)(2,1)S(1)}, bf16[1024,2048]{1,0:T(8,128)(2,1)}, u32[]{:S(2)}) %copy-start) | copy-done | bytes 4194328
  21.7 1.6 %copy-done.3 = bf16[1024,1024]{1,0:T(8,128)(2,1)S(1)} copy-done((bf16[1024,1024]{1,0:T(8,128)(2,1)S(1)}, bf16[1024,1024]{1,0:T(8,128)(2,1)}, u32[]{:S(2)}) %copy-start.3) | copy-done | bytes 2097176
  26.8 1.6 %shard_map.119 = (bf16[1024,256]{1,0:T(8,128)(2,1)S(1)}, bf16[128,256]{1,0:T(8,128)(2,1)S(1)}, f32[128,256]{1,0:T(8,128)S(1)}, bf16[1024,256]{1,0:T(8,128)(2,1)S...) custom-call(s32[2]{0:T(128)S(1)} %pad_add_fusion.me, ...), custom_call_target="tpu_custom_call" | custom-call | flops 536870912 | bytes 8388608 | tf_op jit(solution)/shard_map/pallas_call | solution.py:397
  31.3 3.4 %shard_map.121 = (bf16[112,256]{1,0:T(8,128)(2,1)S(1)}, bf16[8,192,256]{2,1,0:T(8,128)(2,1)S(1)}, bf16[1024,256]{1,0:T(8,128)(2,1)S(1)}, bf16[96,1024]{1,0:T(8,1...) custom-call(bf16[32,1024]{1,0:T(8,128)(2,1)S(1)} %bitcast.18, ...), custom_call_target="tpu_custom_call" | custom-call | flops 1073741824 | bytes 8388608 | tf_op jit(solution)/shard_map/pallas_call | solution.py:417
  36.5 1.7 %collective-permute-start.26 = (bf16[112,256]{1,0:T(8,128)(2,1)S(1)}, bf16[112,256]{1,0:T(8,128)(2,1)S(1)}, u32[]{:S(2)}, u32[]{:S(2)}) collective-permute-start(bf16[112,256]{1,0:T(8,128)(2,1)S(1)} %get-tuple-element.56.p0.payload), channel_id=1, source_target_pairs={{0,128},{32,160},{64,192},{96,224},{128,0},{160,32},{192,64},{224,... | collective-permute-start | bytes 172040 | tf_op jit(solution)/shard_map/ppermute | solution.py:366
  39.6 2.2 %collective-permute-start.13 = (bf16[32,1024]{1,0:T(8,128)(2,1)S(1)}, bf16[32,1024]{1,0:T(8,128)(2,1)S(1)}, u32[]{:S(2)}, u32[]{:S(2)}) collective-permute-start(bf16[32,1024]{1,0:T(8,128)(2,1)S(1)} %collective-permute-done.1.refs_2_.other), channel_id=1, source_target_pairs={{0,128},{32,160},{64,192},{96,224},{128,0},{160,32},{192,64},{224,... | collective-permute-start | bytes 196616 | tf_op jit(solution)/shard_map/ppermute | solution.py:366
  43.1 2.1 %collective-permute-start.4 = (bf16[32,1024]{1,0:T(8,128)(2,1)S(1)}, bf16[32,1024]{1,0:T(8,128)(2,1)S(1)}, u32[]{:S(2)}, u32[]{:S(2)}) collective-permute-start(bf16[32,1024]{1,0:T(8,128)(2,1)S(1)} %collective-permute-done.1.refs_2_.other), channel_id=1, source_target_pairs={{0,32},{32,0},{64,96},{96,64},{128,160},{160,128},{192,224},{224,1... | collective-permute-start | bytes 196616 | tf_op jit(solution)/shard_map/ppermute | solution.py:366
  47.5 2.8 %collective-permute-start.9 = (bf16[32,1024]{1,0:T(8,128)(2,1)S(1)}, bf16[32,1024]{1,0:T(8,128)(2,1)S(1)}, u32[]{:S(2)}, u32[]{:S(2)}) collective-permute-start(bf16[32,1024]{1,0:T(8,128)(2,1)S(1)} %collective-permute-done.6.refs_7_), channel_id=1, source_target_pairs={{0,32},{32,0},{64,96},{96,64},{128,160},{160,128},{192,224},{224,1... | collective-permute-start | bytes 196616 | tf_op jit(solution)/shard_map/ppermute | solution.py:366
  52.3 3.8 %shard_map.120 = (bf16[1024,768]{1,0:T(8,128)(2,1)S(1)}, bf16[8,192,256]{2,1,0:T(8,128)(2,1)S(1)}, bf16[8,96,128]{2,1,0:T(8,128)(2,1)S(1)}, f32[8,96,128]{2,1,0:...) custom-call(bf16[32,1024]{1,0:T(8,128)(2,1)S(1)} %bitcast.19, ...), custom_call_target="tpu_custom_call" | custom-call | flops 2147483648 | bytes 8388608 | tf_op jit(solution)/shard_map/pallas_call | solution.py:435
  56.1 7.5 %shard_map.122 = (bf16[1024,512]{1,0:T(8,128)(2,1)}, bf16[128,256]{1,0:T(8,128)(2,1)S(1)}) custom-call(s32[2]{0:T(128)S(1)} %pad_add_fusion.me, bf16[1024,768]{1,0:T(8,128)(2,1)S(1)} %get-tuple-element.43.turned, bf16[8,192,256]{2,1,0:T(8,128)(2,1)S(1)} %get-tuple-element.44.weights, bf16[8,96,128]{2,1,0:T(8,128)(2,1)S(1)} %get-tuple-element.45.keys, ...), custom_call_target="tpu_custom_call" | custom-call | flops 2147483648 | bytes 8388608 | tf_op jit(solution)/shard_map/pallas_call | solution.py:450
  64.2 9.1 %all-to-all-start = ((bf16[32,32,512]{2,1,0:T(8,128)(2,1)}), bf16[32,32,512]{2,1,0:T(8,128)(2,1)S(1)}, u32[]{:S(2)}, u32[]{:S(2)}) async-start(bf16[32,32,512]{2,1,0:T(8,128)(2,1)} %bitcast.7), calls=%async_computation | async-start | bytes 2097152 | tf_op jit(solution)/shard_map/all_to_all | solution.py:465
  73.4 2.2 %copy-done.2 = bf16[1024,2048]{1,0:T(8,128)(2,1)S(1)} copy-done((bf16[1024,2048]{1,0:T(8,128)(2,1)S(1)}, bf16[1024,2048]{1,0:T(8,128)(2,1)}, u32[]{:S(2)}) %copy-start.2) | copy-done | bytes 4194328
  79.9 3.7 %shard_map.124 = (f32[32,1024]{1,0:T(8,128)S(1)}, f32[32,1024]{1,0:T(8,128)S(1)}, bf16[32,1024]{1,0:T(8,128)(2,1)S(1)}) custom-call(bf16[128,256]{1,0:T(8,128)(2,1)S(1)} %copy-done.16, bf16[112,256]{1,0:T(8,128)(2,1)S(1)} %copy-done.18, bf16[8,192,256]{2,1,0:T(8,128)(2,1)S(1)} %get-tuple-element.60.weights, bf16[1024,256]{1,0:T(8,128)(2,1)S(1)} %get-tuple-element.61.normed, ...), custom_call_target="tpu_custom_call" | custom-call | flops 1073741824 | bytes 8388608 | tf_op jit(solution)/shard_map/pallas_call | solution.py:486
  83.6 4.7 %collective-permute-start.30 = (bf16[32,1024]{1,0:T(8,128)(2,1)S(1)}, bf16[32,1024]{1,0:T(8,128)(2,1)S(1)}, u32[]{:S(2)}, u32[]{:S(2)}) collective-permute-start(bf16[32,1024]{1,0:T(8,128)(2,1)S(1)} %get-tuple-element.68), channel_id=1, source_target_pairs={{0,30},{1,3},{2,0},{3,5},{4,2},{5,7},{6,4},{7,9},{8,6},{9,11},{10,... | collective-permute-start | bytes 196616 | tf_op jit(solution)/shard_map/ppermute | solution.py:501
  89.7 6.9 %collective-permute-start.31 = (bf16[32,1024]{1,0:T(8,128)(2,1)S(1)}, bf16[32,1024]{1,0:T(8,128)(2,1)S(1)}, u32[]{:S(2)}, u32[]{:S(2)}) collective-permute-start(bf16[32,1024]{1,0:T(8,128)(2,1)S(1)} %add_convert_fusion), channel_id=1, source_target_pairs={{0,1},{1,0},{2,3},{3,2},{4,5},{5,4},{6,7},{7,6},{8,9},{9,8},{10,11... | collective-permute-start | bytes 196616 | tf_op jit(solution)/shard_map/ppermute | solution.py:366
  98.0 9.5 %collective-permute-start.33 = (bf16[32,512]{1,0:T(8,128)(2,1)S(1)}, bf16[32,512]{1,0:T(8,128)(2,1)S(1)}, u32[]{:S(2)}, u32[]{:S(2)}) collective-permute-start(bf16[32,512]{1,0:T(8,128)(2,1)S(1)} %get-tuple-element.69.g0), channel_id=1, source_target_pairs={{0,64},{32,96},{64,0},{96,32},{128,192},{160,224},{192,128},{224,1... | collective-permute-start | bytes 98312 | tf_op jit(solution)/shard_map/ppermute | solution.py:366
  107.5 2.1 %collective-permute-start.37 = (bf16[32,512]{1,0:T(8,128)(2,1)S(1)}, bf16[32,512]{1,0:T(8,128)(2,1)S(1)}, u32[]{:S(2)}, u32[]{:S(2)}) collective-permute-start(bf16[32,512]{1,0:T(8,128)(2,1)S(1)} %get-tuple-element.69.g0), channel_id=1, source_target_pairs={{0,192},{32,224},{64,128},{96,160},{128,64},{160,96},{192,0},{224,... | collective-permute-start | bytes 98312 | tf_op jit(solution)/shard_map/ppermute | solution.py:366
  109.6 2.7 %collective-permute-start.32 = (bf16[32,512]{1,0:T(8,128)(2,1)S(1)}, bf16[32,512]{1,0:T(8,128)(2,1)S(1)}, u32[]{:S(2)}, u32[]{:S(2)}) collective-permute-start(bf16[32,512]{1,0:T(8,128)(2,1)S(1)} %get-tuple-element.69.g0), channel_id=1, source_target_pairs={{0,32},{32,0},{64,96},{96,64},{128,160},{160,128},{192,224},{224,1... | collective-permute-start | bytes 98312 | tf_op jit(solution)/shard_map/ppermute | solution.py:366
  112.3 2.4 %collective-permute-start.36 = (bf16[32,512]{1,0:T(8,128)(2,1)S(1)}, bf16[32,512]{1,0:T(8,128)(2,1)S(1)}, u32[]{:S(2)}, u32[]{:S(2)}) collective-permute-start(bf16[32,512]{1,0:T(8,128)(2,1)S(1)} %collective-permute-done.35.g4), channel_id=1, source_target_pairs={{0,32},{32,0},{64,96},{96,64},{128,160},{160,128},{192,224},{224,1... | collective-permute-start | bytes 98312 | tf_op jit(solution)/shard_map/ppermute | solution.py:366
  (108 shorter events, 29.4 us)
Async XLA Ops:
  0.6 12.3 %collective-permute-start = (bf16[32,1024]{1,0:T(8,128)(2,1)}, bf16[32,1024]{1,0:T(8,128)(2,1)S(1)}, u32[]{:S(2)}, u32[]{:S(2)}) collective-permute-start(bf16[32,1024]{1,0:T(8,128)(2,1)} %bitcast.13), channel_id=1, source_target_pairs={{0,1},{1,0},{2,3},{3,2},{4,5},{5,4},{6,7},{7,6},{8,9},{9,8},{10,11... | collective-permute-start | bytes 196616 | tf_op jit(solution)/shard_map/ppermute | solution.py:366
  8.5 9.0 %collective-permute-start.11 = (bf16[32,1024]{1,0:T(8,128)(2,1)}, bf16[32,1024]{1,0:T(8,128)(2,1)S(1)}, u32[]{:S(2)}, u32[]{:S(2)}) collective-permute-start(bf16[32,1024]{1,0:T(8,128)(2,1)} %bitcast.14), channel_id=1, source_target_pairs={{0,128},{32,160},{64,192},{96,224},{128,0},{160,32},{192,64},{224,... | collective-permute-start | bytes 196616 | tf_op jit(solution)/shard_map/ppermute | solution.py:366
  9.6 7.8 %collective-permute-start.17 = (bf16[32,1024]{1,0:T(8,128)(2,1)}, bf16[32,1024]{1,0:T(8,128)(2,1)S(1)}, u32[]{:S(2)}, u32[]{:S(2)}) collective-permute-start(bf16[32,1024]{1,0:T(8,128)(2,1)} %bitcast.15), channel_id=1, source_target_pairs={{0,192},{32,224},{64,128},{96,160},{128,64},{160,96},{192,0},{224,... | collective-permute-start | bytes 196616 | tf_op jit(solution)/shard_map/ppermute | solution.py:366
  11.3 17.1 %collective-permute-start.5 = (bf16[32,1024]{1,0:T(8,128)(2,1)}, bf16[32,1024]{1,0:T(8,128)(2,1)S(1)}, u32[]{:S(2)}, u32[]{:S(2)}) collective-permute-start(bf16[32,1024]{1,0:T(8,128)(2,1)} %bitcast.16), channel_id=1, source_target_pairs={{0,64},{32,96},{64,0},{96,32},{128,192},{160,224},{192,128},{224,1... | collective-permute-start | bytes 196616 | tf_op jit(solution)/shard_map/ppermute | solution.py:366
  11.3 18.0 %collective-permute-start.2 = (bf16[32,1024]{1,0:T(8,128)(2,1)}, bf16[32,1024]{1,0:T(8,128)(2,1)S(1)}, u32[]{:S(2)}, u32[]{:S(2)}) collective-permute-start(bf16[32,1024]{1,0:T(8,128)(2,1)} %bitcast.17), channel_id=1, source_target_pairs={{0,32},{32,0},{64,96},{96,64},{128,160},{160,128},{192,224},{224,1... | collective-permute-start | bytes 196616 | tf_op jit(solution)/shard_map/ppermute | solution.py:366
  12.9 17.8 %collective-permute-start.1 = (bf16[32,1024]{1,0:T(8,128)(2,1)S(1)}, bf16[32,1024]{1,0:T(8,128)(2,1)S(1)}, u32[]{:S(2)}, u32[]{:S(2)}) collective-permute-start(bf16[32,1024]{1,0:T(8,128)(2,1)S(1)} %collective-permute-done.refs_1_.partner), channel_id=1, source_target_pairs={{0,2},{1,31},{2,4},{3,1},{4,6},{5,3},{6,8},{7,5},{8,10},{9,7},{10,... | collective-permute-start | bytes 196616 | tf_op jit(solution)/shard_map/ppermute | solution.py:393
  17.4 13.3 %collective-permute-start.12 = (bf16[32,1024]{1,0:T(8,128)(2,1)S(1)}, bf16[32,1024]{1,0:T(8,128)(2,1)S(1)}, u32[]{:S(2)}, u32[]{:S(2)}) collective-permute-start(bf16[32,1024]{1,0:T(8,128)(2,1)S(1)} %collective-permute-done.refs_1_.partner), channel_id=1, source_target_pairs={{0,128},{32,160},{64,192},{96,224},{128,0},{160,32},{192,64},{224,... | collective-permute-start | bytes 196616 | tf_op jit(solution)/shard_map/ppermute | solution.py:366
  17.5 13.7 %collective-permute-start.18 = (bf16[32,1024]{1,0:T(8,128)(2,1)S(1)}, bf16[32,1024]{1,0:T(8,128)(2,1)S(1)}, u32[]{:S(2)}, u32[]{:S(2)}) collective-permute-start(bf16[32,1024]{1,0:T(8,128)(2,1)S(1)} %collective-permute-done.refs_1_.partner), channel_id=1, source_target_pairs={{0,192},{32,224},{64,128},{96,160},{128,64},{160,96},{192,0},{224,... | collective-permute-start | bytes 196616 | tf_op jit(solution)/shard_map/ppermute | solution.py:366
  28.4 7.6 %collective-permute-start.6 = (bf16[32,1024]{1,0:T(8,128)(2,1)S(1)}, bf16[32,1024]{1,0:T(8,128)(2,1)S(1)}, u32[]{:S(2)}, u32[]{:S(2)}) collective-permute-start(bf16[32,1024]{1,0:T(8,128)(2,1)S(1)} %collective-permute-done.refs_1_.partner), channel_id=1, source_target_pairs={{0,64},{32,96},{64,0},{96,32},{128,192},{160,224},{192,128},{224,1... | collective-permute-start | bytes 196616 | tf_op jit(solution)/shard_map/ppermute | solution.py:366
  29.3 7.2 %collective-permute-start.3 = (bf16[32,1024]{1,0:T(8,128)(2,1)S(1)}, bf16[32,1024]{1,0:T(8,128)(2,1)S(1)}, u32[]{:S(2)}, u32[]{:S(2)}) collective-permute-start(bf16[32,1024]{1,0:T(8,128)(2,1)S(1)} %collective-permute-done.refs_1_.partner), channel_id=1, source_target_pairs={{0,32},{32,0},{64,96},{96,64},{128,160},{160,128},{192,224},{224,1... | collective-permute-start | bytes 196616 | tf_op jit(solution)/shard_map/ppermute | solution.py:366
  30.7 7.6 %collective-permute-start.14 = (bf16[32,1024]{1,0:T(8,128)(2,1)S(1)}, bf16[32,1024]{1,0:T(8,128)(2,1)S(1)}, u32[]{:S(2)}, u32[]{:S(2)}) collective-permute-start(bf16[32,1024]{1,0:T(8,128)(2,1)S(1)} %collective-permute-done.11.refs_12_), channel_id=1, source_target_pairs={{0,32},{32,0},{64,96},{96,64},{128,160},{160,128},{192,224},{224,1... | collective-permute-start | bytes 196616 | tf_op jit(solution)/shard_map/ppermute | solution.py:366
  30.8 8.8 %collective-permute-start.20 = (bf16[32,1024]{1,0:T(8,128)(2,1)S(1)}, bf16[32,1024]{1,0:T(8,128)(2,1)S(1)}, u32[]{:S(2)}, u32[]{:S(2)}) collective-permute-start(bf16[32,1024]{1,0:T(8,128)(2,1)S(1)} %collective-permute-done.17.refs_18_), channel_id=1, source_target_pairs={{0,32},{32,0},{64,96},{96,64},{128,160},{160,128},{192,224},{224,1... | collective-permute-start | bytes 196616 | tf_op jit(solution)/shard_map/ppermute | solution.py:366
  31.2 8.4 %collective-permute-start.8 = (bf16[32,1024]{1,0:T(8,128)(2,1)S(1)}, bf16[32,1024]{1,0:T(8,128)(2,1)S(1)}, u32[]{:S(2)}, u32[]{:S(2)}) collective-permute-start(bf16[32,1024]{1,0:T(8,128)(2,1)S(1)} %collective-permute-done.5.refs_6_), channel_id=1, source_target_pairs={{0,32},{32,0},{64,96},{96,64},{128,160},{160,128},{192,224},{224,1... | collective-permute-start | bytes 196616 | tf_op jit(solution)/shard_map/ppermute | solution.py:366
  36.5 6.6 %collective-permute-start.26 = (bf16[112,256]{1,0:T(8,128)(2,1)S(1)}, bf16[112,256]{1,0:T(8,128)(2,1)S(1)}, u32[]{:S(2)}, u32[]{:S(2)}) collective-permute-start(bf16[112,256]{1,0:T(8,128)(2,1)S(1)} %get-tuple-element.56.p0.payload), channel_id=1, source_target_pairs={{0,128},{32,160},{64,192},{96,224},{128,0},{160,32},{192,64},{224,... | collective-permute-start | bytes 172040 | tf_op jit(solution)/shard_map/ppermute | solution.py:366
  38.3 7.0 %collective-permute-start.28 = (bf16[112,256]{1,0:T(8,128)(2,1)S(1)}, bf16[112,256]{1,0:T(8,128)(2,1)S(1)}, u32[]{:S(2)}, u32[]{:S(2)}) collective-permute-start(bf16[112,256]{1,0:T(8,128)(2,1)S(1)} %get-tuple-element.56.p0.payload), channel_id=1, source_target_pairs={{0,192},{32,224},{64,128},{96,160},{128,64},{160,96},{192,0},{224,... | collective-permute-start | bytes 172040 | tf_op jit(solution)/shard_map/ppermute | solution.py:366
  39.6 6.2 %collective-permute-start.7 = (bf16[32,1024]{1,0:T(8,128)(2,1)S(1)}, bf16[32,1024]{1,0:T(8,128)(2,1)S(1)}, u32[]{:S(2)}, u32[]{:S(2)}) collective-permute-start(bf16[32,1024]{1,0:T(8,128)(2,1)S(1)} %collective-permute-done.1.refs_2_.other), channel_id=1, source_target_pairs={{0,64},{32,96},{64,0},{96,32},{128,192},{160,224},{192,128},{224,1... | collective-permute-start | bytes 196616 | tf_op jit(solution)/shard_map/ppermute | solution.py:366
  39.6 8.0 %collective-permute-start.13 = (bf16[32,1024]{1,0:T(8,128)(2,1)S(1)}, bf16[32,1024]{1,0:T(8,128)(2,1)S(1)}, u32[]{:S(2)}, u32[]{:S(2)}) collective-permute-start(bf16[32,1024]{1,0:T(8,128)(2,1)S(1)} %collective-permute-done.1.refs_2_.other), channel_id=1, source_target_pairs={{0,128},{32,160},{64,192},{96,224},{128,0},{160,32},{192,64},{224,... | collective-permute-start | bytes 196616 | tf_op jit(solution)/shard_map/ppermute | solution.py:366
  41.8 8.6 %collective-permute-start.19 = (bf16[32,1024]{1,0:T(8,128)(2,1)S(1)}, bf16[32,1024]{1,0:T(8,128)(2,1)S(1)}, u32[]{:S(2)}, u32[]{:S(2)}) collective-permute-start(bf16[32,1024]{1,0:T(8,128)(2,1)S(1)} %collective-permute-done.1.refs_2_.other), channel_id=1, source_target_pairs={{0,192},{32,224},{64,128},{96,160},{128,64},{160,96},{192,0},{224,... | collective-permute-start | bytes 196616 | tf_op jit(solution)/shard_map/ppermute | solution.py:366
  43.1 7.3 %collective-permute-start.4 = (bf16[32,1024]{1,0:T(8,128)(2,1)S(1)}, bf16[32,1024]{1,0:T(8,128)(2,1)S(1)}, u32[]{:S(2)}, u32[]{:S(2)}) collective-permute-start(bf16[32,1024]{1,0:T(8,128)(2,1)S(1)} %collective-permute-done.1.refs_2_.other), channel_id=1, source_target_pairs={{0,32},{32,0},{64,96},{96,64},{128,160},{160,128},{192,224},{224,1... | collective-permute-start | bytes 196616 | tf_op jit(solution)/shard_map/ppermute | solution.py:366
  64.2 33.1 %all-to-all-start = ((bf16[32,32,512]{2,1,0:T(8,128)(2,1)}), bf16[32,32,512]{2,1,0:T(8,128)(2,1)S(1)}, u32[]{:S(2)}, u32[]{:S(2)}) async-start(bf16[32,32,512]{2,1,0:T(8,128)(2,1)} %bitcast.7), calls=%async_computation | async-start | bytes 2097152 | tf_op jit(solution)/shard_map/all_to_all | solution.py:465
  89.7 26.1 %collective-permute-start.31 = (bf16[32,1024]{1,0:T(8,128)(2,1)S(1)}, bf16[32,1024]{1,0:T(8,128)(2,1)S(1)}, u32[]{:S(2)}, u32[]{:S(2)}) collective-permute-start(bf16[32,1024]{1,0:T(8,128)(2,1)S(1)} %add_convert_fusion), channel_id=1, source_target_pairs={{0,1},{1,0},{2,3},{3,2},{4,5},{5,4},{6,7},{7,6},{8,9},{9,8},{10,11... | collective-permute-start | bytes 196616 | tf_op jit(solution)/shard_map/ppermute | solution.py:366
  98.0 14.3 %collective-permute-start.33 = (bf16[32,512]{1,0:T(8,128)(2,1)S(1)}, bf16[32,512]{1,0:T(8,128)(2,1)S(1)}, u32[]{:S(2)}, u32[]{:S(2)}) collective-permute-start(bf16[32,512]{1,0:T(8,128)(2,1)S(1)} %get-tuple-element.69.g0), channel_id=1, source_target_pairs={{0,64},{32,96},{64,0},{96,32},{128,192},{160,224},{192,128},{224,1... | collective-permute-start | bytes 98312 | tf_op jit(solution)/shard_map/ppermute | solution.py:366
  107.5 7.2 %collective-permute-start.37 = (bf16[32,512]{1,0:T(8,128)(2,1)S(1)}, bf16[32,512]{1,0:T(8,128)(2,1)S(1)}, u32[]{:S(2)}, u32[]{:S(2)}) collective-permute-start(bf16[32,512]{1,0:T(8,128)(2,1)S(1)} %get-tuple-element.69.g0), channel_id=1, source_target_pairs={{0,192},{32,224},{64,128},{96,160},{128,64},{160,96},{192,0},{224,... | collective-permute-start | bytes 98312 | tf_op jit(solution)/shard_map/ppermute | solution.py:366
  109.6 7.8 %collective-permute-start.32 = (bf16[32,512]{1,0:T(8,128)(2,1)S(1)}, bf16[32,512]{1,0:T(8,128)(2,1)S(1)}, u32[]{:S(2)}, u32[]{:S(2)}) collective-permute-start(bf16[32,512]{1,0:T(8,128)(2,1)S(1)} %get-tuple-element.69.g0), channel_id=1, source_target_pairs={{0,32},{32,0},{64,96},{96,64},{128,160},{160,128},{192,224},{224,1... | collective-permute-start | bytes 98312 | tf_op jit(solution)/shard_map/ppermute | solution.py:366
  (37 other events, 149.2 us)

commit v3 on v2

v3 whole, which is shorter than its diff:
```python
import jax
import jax.numpy as jnp
from jax import lax
from jax.experimental import pallas as pl
from jax.experimental.pallas import tpu as pltpu
from jax.sharding import PartitionSpec as P

F32 = jnp.float32
BF16 = jnp.bfloat16
TILE = 128
SIZE = 64
TILES = 8
MEMBERS = 8
HALF = 4
SHARDS = 32
NODES = 32
WIDE = 96
BOTH = 2 * WIDE
ROWS = 256
WIDTH = 1024
VARS = 100
KNB = 3
CARRY = 112
EDGE = 96
FOLDS = 4
PAIR = 1.0 / (MEMBERS * (MEMBERS - 1))
SCALE = (MEMBERS * ROWS * SHARDS) ** (-0.5)
VMEM = pl.BlockSpec(memory_space=pltpu.VMEM)
SMEM = pl.BlockSpec(memory_space=pltpu.SMEM)


def dot(left, right):
    return lax.dot_general(left, right, (((1,), (0,)), ((), ())), preferred_element_type=F32)


def dot_nt(left, right):
    return lax.dot_general(left, right, (((1,), (1,)), ((), ())), preferred_element_type=F32)


def dot_tn(left, right):
    return lax.dot_general(left, right, (((0,), (0,)), ((), ())), preferred_element_type=F32)


def call(body, outs, specs, scratch=(), flops=0, size=0, limit=12):
    return pl.pallas_call(
        body,
        out_shape=outs,
        in_specs=specs,
        out_specs=[VMEM] * len(outs),
        scratch_shapes=list(scratch),
        compiler_params=pltpu.CompilerParams(vmem_limit_bytes=limit << 20),
        cost_estimate=pl.CostEstimate(flops=flops, bytes_accessed=size, transcendentals=0),
    )


def iota(shape, dim):
    return lax.broadcasted_iota(jnp.int32, shape, dim)


def lane_mean(values):
    average = jnp.where(
        iota((TILE, TILE), 0) // SIZE == iota((TILE, TILE), 1) // SIZE, 1.0 / SIZE, 0.0
    ).astype(BF16)
    high = values.astype(BF16)
    low = (values - high.astype(F32)).astype(BF16)
    return dot(high, average) + dot(low, average)


def stack_heads(tile):
    first = iota(tile.shape, 1) < SIZE
    zero = jnp.zeros_like(tile)
    return jnp.concatenate([jnp.where(first, tile, zero), jnp.where(first, zero, tile)], 0)


def unstack_heads(both):
    first = iota((WIDE, TILE), 1) < SIZE
    return jnp.where(first, both[:WIDE], both[WIDE:])


def half_sums(values):
    return (
        jnp.sum(values[:WIDE], 0, keepdims=True),
        jnp.sum(values[WIDE:], 0, keepdims=True),
    )


def key_parts(raw):
    root = lax.rsqrt(lane_mean(raw * raw) + 1e-06)
    return raw * root, root


def attention_back(weight, value, query, d_mixed):
    d_weight = dot(value, d_mixed)
    wide = weight.astype(F32)
    first, second = half_sums(wide * d_weight)
    d_score = jnp.concatenate([d_weight[:WIDE] - first, d_weight[WIDE:] - second], 0)
    d_score = (wide * d_score * SIZE**-0.5).astype(BF16)
    return d_score, unstack_heads(dot_nt(weight, d_mixed)), unstack_heads(dot_nt(d_score, query))


def key_back(d_key, normal, root):
    return root * (d_key - normal * lane_mean(d_key * normal))


def counts_of(edges, shard):
    source = edges[...]
    offset = jnp.bitwise_and(jnp.right_shift(source, 5) - shard + SHARDS, SHARDS - 1)
    toward = jnp.where(jnp.bitwise_and(shard, 1) == 0, 1, SHARDS - 1)
    slot = jnp.where(offset == 0, 0, jnp.where(offset == toward, 1, 2))
    index = slot * NODES + jnp.bitwise_and(source, NODES - 1)
    node = iota((WIDE, ROWS), 0)
    total = jnp.zeros((WIDE, ROWS), F32)
    for k in range(KNB):
        total = total + jnp.where(index[k : k + 1] == node, 1.0, 0.0)
    return total


def prepare_kernel(
    me, embed, w_query, normal, normal_tile, inverse, embed_turned, embed_tile
):
    here = me[0]
    at = pl.multiple_of(here * TILE, TILE)
    embed_turned[...] = embed[...].T
    embed_tile[...] = embed_turned[pl.ds(at, TILE), :]
    value = dot(embed[...], w_query[...]).T
    held = jnp.zeros((TILE, ROWS), F32)
    for t in range(TILES):
        roots = []
        for h in (2 * t, 2 * t + 1):
            part = value[h * SIZE : (h + 1) * SIZE]
            root = lax.rsqrt(jnp.mean(part * part, 0, keepdims=True) + 1e-06)
            normal[h * SIZE : (h + 1) * SIZE, :] = (part * root).astype(BF16)
            roots.append(jnp.broadcast_to(root, (SIZE, ROWS)))
        held = jnp.where(here == t, jnp.concatenate(roots, 0), held)
    inverse[...] = held
    normal_tile[...] = normal[pl.ds(at, TILE), :]


def weigh(scores, count):
    groups = scores.shape[0] // WIDE
    expon = jnp.exp(scores * SIZE**-0.5).reshape(groups, WIDE, ROWS) * count[None]
    weight = expon * (1.0 / jnp.sum(expon, 1, keepdims=True))
    return weight.astype(BF16).reshape(groups * WIDE, ROWS)


def forward_kernel(
    me, own, partner, other, w_keyval, normal, embed, edges, w_head,
    bundle, weights, normed, table, hidden,
):
    bundle[:NODES, :] = other[...]
    counts = counts_of(edges, me[1])
    wide = jnp.concatenate([own[...], partner[...], other[...]], 0)
    low = dot(wide, w_keyval[...]).astype(BF16)
    table[...] = low
    tiles = [slice(t * TILE, (t + 1) * TILE) for t in range(TILES)]
    raw = jnp.concatenate([low[:, at] for at in tiles], 0).astype(F32)
    keys = key_parts(raw)[0].astype(BF16)
    scores = [
        dot(stack_heads(keys[t * WIDE : (t + 1) * WIDE]), normal[at, :])
        for t, at in enumerate(tiles)
    ]
    shares = [weigh(score, counts) for score in scores]
    for t, at in enumerate(tiles):
        weights[t] = shares[t]
        value = stack_heads(low[:, WIDTH + t * TILE : WIDTH + (t + 1) * TILE])
        hidden[at, :] = embed[at, :].astype(F32) + dot_tn(value, shares[t])
    whole = hidden[...]
    mean = jnp.mean(whole, 0, keepdims=True)
    center = whole - mean
    scale = lax.rsqrt(jnp.mean(center * center, 0, keepdims=True) + 1e-05)
    result = (center * scale).astype(BF16)
    normed[...] = result
    pred = dot(w_head[...], result)
    pred = jnp.concatenate([pred, jnp.zeros((TILE - VARS, ROWS), F32)], 0)
    row = iota(pred.shape, 0)
    for at, stat in ((VARS, mean), (VARS + 2, scale)):
        high = stat.astype(BF16).astype(F32)
        pred = jnp.where(row == at, high, pred)
        pred = jnp.where(row == at + 1, stat - high, pred)
    pred = pred.astype(BF16)
    for q in range(FOLDS):
        bundle[NODES:, q * ROWS : (q + 1) * ROWS] = pred[q * NODES : (q + 1) * NODES]


def stack_kernel(*refs):
    parts, out = refs[:-1], refs[-1]
    at = 0
    for b in range(len(parts) // HALF):
        rows = parts[b * HALF].shape[0]
        for i in range(HALF):
            out[i, at : at + rows, :] = parts[b * HALF + i][...]
        at += rows


def tables_kernel(
    me, stack, w_keyval, normal_tile, embed_tile, edges,
    turned, weights, keys, key_roots, values, hidden,
):
    at = pl.multiple_of(me[0] * TILE, TILE)
    flat = jnp.concatenate([stack[i, :WIDE, :] for i in range(HALF)], 0)
    turned[...] = flat.T
    key, root = key_parts(dot(flat, w_keyval[:, pl.ds(at, TILE)]).astype(BF16).astype(F32))
    at = pl.multiple_of(WIDTH + at, TILE)
    value = dot(flat, w_keyval[:, pl.ds(at, TILE)]).astype(BF16)
    key_roots[...] = root
    key = key.astype(BF16)
    members = [slice(i * WIDE, (i + 1) * WIDE) for i in range(HALF)]
    key = jnp.concatenate([stack_heads(key[rows]) for rows in members], 0)
    value = jnp.concatenate([stack_heads(value[rows]) for rows in members], 0)
    keys[...] = key
    values[...] = value
    weight = weigh(dot(key, normal_tile[...]), counts_of(edges, me[1]))
    weights[...] = weight
    base = embed_tile[...].astype(F32)
    for i in range(HALF):
        rows = slice(i * BOTH, (i + 1) * BOTH)
        hidden[i] = base + dot_tn(value[rows], weight[rows])


def head_kernel(me, w_head, head, head_tile, head_sum):
    at = pl.multiple_of(me[0] * TILE, TILE)
    rows = jnp.concatenate([w_head[...], jnp.zeros((TILE - VARS, WIDTH), BF16)], 0)
    head[...] = rows.T
    head_tile[...] = head[pl.ds(at, TILE), :]
    head_sum[...] = jnp.sum(rows.astype(F32), 1, keepdims=True)


def payload_rows(stack, i, start, size):
    fold, row = start // NODES, WIDE + start % NODES
    return stack[i, row : row + size, fold * ROWS : (fold + 1) * ROWS]


def stats_of(stack, i):
    rows = payload_rows(stack, i, EDGE, 16).astype(F32)
    at = VARS - EDGE
    mean = rows[at : at + 1] + rows[at + 1 : at + 2]
    return mean, rows[at + 2 : at + 3] + rows[at + 3 : at + 4]


def crps_kernel(mine, theirs, target, area, d_pred, d_own, loss):
    size = 16
    stacks = (mine, theirs)
    lost = jnp.zeros((size, ROWS), F32)
    weight = area[...]
    for start in range(0, CARRY, size):
        rows = slice(start, start + size)
        value = [
            payload_rows(stacks[k % 2], k // 2, start, size).astype(F32)
            for k in range(MEMBERS)
        ]
        slope = [jnp.zeros((size, ROWS), F32) for _ in range(MEMBERS)]
        pair = jnp.zeros((size, ROWS), F32)
        if start + size <= VARS:
            aim, share = target[rows, :], jnp.broadcast_to(weight, (size, ROWS))
        else:
            short = jnp.zeros((start + size - VARS, ROWS), F32)
            aim = jnp.concatenate([target[start:VARS, :], short], 0)
            share = jnp.where(iota((size, ROWS), 0) + start < VARS, weight, 0.0)
        for i in range(MEMBERS):
            for j in range(i + 1, MEMBERS):
                delta = value[i] - value[j]
                square = delta * delta + 0.0625
                root = lax.rsqrt(square)
                if i == 0:
                    pair = pair + square * root
                part = delta * root
                slope[i] = slope[i] + part
                slope[j] = slope[j] - part
        for i in range(MEMBERS):
            delta = value[i] - aim
            square = delta * delta + 0.0625
            root = lax.rsqrt(square)
            if i == 0:
                lost = lost + share * (square * root / MEMBERS - 0.5 * PAIR * pair)
            out = (share * (delta * root / MEMBERS - PAIR * slope[i])).astype(BF16)
            d_pred[rows, i * ROWS : (i + 1) * ROWS] = out
            if i == 0:
                d_own[rows, :] = out
    d_pred[CARRY:, :] = jnp.zeros((TILE - CARRY, MEMBERS * ROWS), BF16)
    d_own[CARRY:, :] = payload_rows(mine, 0, EDGE, 16)
    loss[...] = jnp.sum(lost, axis=(0, 1), keepdims=True) / (ROWS * SHARDS * VARS)


def backward_kernel(*refs):
    me = refs[0]
    sets = (refs[1:7], refs[7:13])
    (
        normal_tile, inverse, embed_turned, head_tile, head_sum, d_pred, loss, mine, theirs,
        payload, d_table, normed_all, d_mixed_all, d_score_all,
    ) = refs[13:]
    stacks = (mine, theirs)
    here = me[0]
    query = normal_tile[...]
    sums = head_sum[...]
    out = d_pred[...]
    wide = out.astype(F32)
    d_normed = dot(head_tile[...], out)
    levels = jnp.sum(wide * sums, 0, keepdims=True) / WIDTH
    for k in range(MEMBERS):
        side, i = k % 2, k // 2
        cols = slice(k * ROWS, (k + 1) * ROWS)
        mean, scale = stats_of(stacks[side], i)
        normed = (sets[side][5][i] - mean) * scale
        along = jnp.zeros((1, ROWS), F32)
        for start in range(0, VARS + NODES - VARS % NODES, NODES):
            pred = payload_rows(stacks[side], i, start, NODES).astype(F32)
            along = along + jnp.sum(pred * wide[start : start + NODES, cols], 0, keepdims=True)
        normed_all[:, cols] = normed.astype(BF16)
        d_mixed_all[:, cols] = (
            scale * (d_normed[:, cols] - levels[:, cols] - normed * (along / WIDTH))
        ).astype(BF16)
    d_head = dot_nt(normed_all[...], out)
    for k in range(MEMBERS):
        side, i = k % 2, k // 2
        rows = slice(i * BOTH, (i + 1) * BOTH)
        d_weight = dot(sets[side][4][rows, :], d_mixed_all[:, k * ROWS : (k + 1) * ROWS])
        weight = sets[side][1][rows, :].astype(F32).reshape(2, WIDE, ROWS)
        d_weight = d_weight.reshape(2, WIDE, ROWS)
        d_score = weight * (d_weight - jnp.sum(weight * d_weight, 1, keepdims=True))
        d_score_all[side, rows, :] = (
            (d_score * SIZE**-0.5).astype(BF16).reshape(BOTH, ROWS)
        )
    d_query = jnp.zeros((TILE, ROWS), F32)
    for side in range(2):
        turned, weights, keys, key_roots, values, hidden = sets[side]
        d_score = d_score_all[side]
        d_query = d_query + dot_tn(keys[...], d_score)
        d_both = dot_nt(d_score, query)
        parts = [slice(i * BOTH, (i + 1) * BOTH) for i in range(HALF)]
        d_key = jnp.concatenate([unstack_heads(d_both[rows]) for rows in parts], 0)
        key = jnp.concatenate([unstack_heads(keys[rows, :]) for rows in parts], 0).astype(F32)
        d_table[side, :, :TILE] = key_back(d_key, key, key_roots[...]).astype(BF16)
        for i, rows in enumerate(parts):
            k = 2 * i + side
            d_value = dot_nt(weights[rows, :], d_mixed_all[:, k * ROWS : (k + 1) * ROWS])
            d_table[side, i * WIDE : (i + 1) * WIDE, TILE:] = unstack_heads(d_value).astype(BF16)
    wide_query = query.astype(F32)
    along = d_query * wide_query
    along = jnp.concatenate(
        [
            jnp.broadcast_to(jnp.mean(along[:SIZE], 0, keepdims=True), (SIZE, ROWS)),
            jnp.broadcast_to(jnp.mean(along[SIZE:], 0, keepdims=True), (SIZE, ROWS)),
        ],
        0,
    )
    d_query = inverse[...] * (d_query - wide_query * along)
    grad = dot_nt(embed_turned[...], d_query.astype(BF16))
    payload[:, :TILE] = (grad * SCALE).astype(BF16)
    grad = dot(sets[0][0][...], d_table[0]) + dot(sets[1][0][...], d_table[1])
    payload[:, TILE : 3 * TILE] = (grad * SCALE).astype(BF16)
    high = loss[...].astype(BF16).astype(F32)
    lane = iota((WIDTH, TILE), 1)
    side = jnp.where(lane == VARS, high, jnp.where(lane == VARS + 1, loss[...] - high, 0.0))
    payload[:, 3 * TILE :] = side.astype(BF16)
    rows = pl.ds(pl.multiple_of(here * TILE, TILE), TILE)
    payload[rows, 3 * TILE :] = jnp.where(
        iota((TILE, TILE), 1) < VARS, d_head * SCALE, side[:TILE]
    ).astype(BF16)


def latent_kernel(
    d_own, weights, normed, table, normal, head, w_keyval,
    own, partner, other, d_table,
):
    tail = d_own[CARRY:, :].astype(F32)
    at = VARS + 2 - EDGE
    scale = tail[at : at + 1] + tail[at + 1 : at + 2]
    result = normed[...].astype(F32)
    d_normed = dot(head[...], d_own[...])
    level = jnp.mean(d_normed, 0, keepdims=True)
    along = jnp.mean(d_normed * result, 0, keepdims=True)
    d_mixed = (scale * (d_normed - level - result * along)).astype(BF16)
    for t in range(TILES):
        at = slice(t * TILE, (t + 1) * TILE)
        key, root = key_parts(table[:, at].astype(F32))
        value = table[:, WIDTH + t * TILE : WIDTH + (t + 1) * TILE]
        d_score, d_value, d_key = attention_back(
            weights[t], stack_heads(value), normal[at, :], d_mixed[at]
        )
        d_table[:, at] = key_back(d_key, key, root).astype(BF16)
        d_table[:, WIDTH + t * TILE : WIDTH + (t + 1) * TILE] = d_value.astype(BF16)
    total = dot_nt(d_table[...], w_keyval[...])
    own[...] = total[:NODES]
    partner[...] = total[NODES : 2 * NODES].astype(BF16)
    other[...] = total[2 * NODES :].astype(BF16)


def sum_kernel(me, pieces, stay, leave):
    low = jnp.sum(pieces[:, :NODES, :].astype(F32), 0)
    high = jnp.sum(pieces[:, NODES:, :].astype(F32), 0)
    even = jnp.bitwise_and(me[1], 1) == 0
    stay[...] = jnp.where(even, low, high)
    leave[...] = jnp.where(even, high, low).astype(BF16)


def merge_kernel(stay, came, total, loss):
    value = stay[...] + came[...].astype(F32)
    total[...] = value.astype(BF16)
    at = 3 * TILE + VARS
    loss[...] = value[0:1, at : at + 1] + value[0:1, at + 1 : at + 2]


def place_kernel(me, mine, theirs, latent, near, far, query, keyval, head, d_latent):
    here = me[0]
    total = jnp.zeros((NODES, TILE), F32)
    for k in range(MEMBERS):
        part = (mine, theirs)[k % 2][k // 2]
        at = pl.multiple_of(jnp.bitwise_xor(here, k) * TILE, TILE)
        query[:, pl.ds(at, TILE)] = part[:, :TILE].astype(F32)
        keyval[:, pl.ds(at, TILE)] = part[:, TILE : 2 * TILE].astype(F32)
        keyval[:, pl.ds(pl.multiple_of(WIDTH + at, TILE), TILE)] = part[
            :, 2 * TILE : 3 * TILE
        ].astype(F32)
        total = total + part[:, 3 * TILE :].astype(F32)
    head[...] = total[:, :VARS]
    d_latent[...] = latent[...] + near[...].astype(F32) + far[...].astype(F32)


def swap(array, axis, bits):
    count = lax.axis_size(axis)
    return lax.ppermute(array, axis, [(i, i ^ bits) for i in range(count)])


def beyond(array):
    step = lambda i: -1 if i % 2 == 0 else 1
    return lax.ppermute(array, "shard", [(i, (i + step(i)) % SHARDS) for i in range(SHARDS)])


def chips(array):
    return [array] + [swap(array, "member", k) for k in (2, 4, 6)]


def cores(*blocks):
    parts = [part for block in blocks for part in block]
    rows = sum(block[0].shape[0] for block in blocks)
    (mine,) = call(
        stack_kernel,
        [shape(HALF, rows, parts[0].shape[1])],
        [VMEM] * len(parts),
        size=1 << 20,
    )(*parts)
    return mine, swap(mine, "member", 1)


def shape(*dims, kind=BF16):
    return jax.ShapeDtypeStruct(dims, kind)


def on_device(latent, grid_embed, edge_src, area, target, w_query, w_keyval, w_head):
    member = lax.axis_index("member").astype(jnp.int32)
    shard = lax.axis_index("shard").astype(jnp.int32)
    me = jnp.stack([member, shard])
    own = latent[0]
    edges, head_turned = edge_src.T, w_head.T
    partner = swap(own, "shard", 1)
    other = beyond(own)
    own_far = chips(own)
    prepared = call(
        prepare_kernel,
        [
            shape(WIDTH, ROWS),
            shape(TILE, ROWS),
            shape(TILE, ROWS, kind=F32),
            shape(WIDTH, ROWS),
            shape(TILE, ROWS),
        ],
        [SMEM, VMEM, VMEM],
        flops=20 << 30,
        size=4 << 20,
    )(me, grid_embed, w_query)
    prepared, other, partner = lax.optimization_barrier((prepared, other, partner))
    normal, normal_tile, inverse, embed_turned, embed_tile = prepared
    partner_far = chips(partner)
    bundle, weights, normed, table = call(
        forward_kernel,
        [
            shape(2 * NODES, WIDTH),
            shape(TILES, BOTH, ROWS),
            shape(WIDTH, ROWS),
            shape(WIDE, 2 * WIDTH),
        ],
        [SMEM] + [VMEM] * 8,
        [pltpu.VMEM((WIDTH, ROWS), F32)],
    )(me, own, partner, other, w_keyval, normal, embed_turned, edges, head_turned)
    bundle, own_far = lax.optimization_barrier((bundle, own_far))
    stacks = cores(own_far, partner_far, chips(bundle))
    d_pred, d_own, loss = call(
        crps_kernel,
        [shape(TILE, MEMBERS * ROWS), shape(TILE, ROWS), shape(1, 1, kind=F32)],
        [VMEM] * 4,
    )(*stacks, target.T, area.reshape(1, ROWS))
    head, head_tile, head_sum = call(
        head_kernel,
        [shape(WIDTH, TILE), shape(TILE, TILE), shape(TILE, 1, kind=F32)],
        [SMEM, VMEM],
    )(me, head_turned)
    tables = [
        call(
            tables_kernel,
            [
                shape(WIDTH, HALF * WIDE),
                shape(HALF * BOTH, ROWS),
                shape(HALF * BOTH, TILE),
                shape(HALF * WIDE, TILE, kind=F32),
                shape(HALF * BOTH, TILE),
                shape(HALF, TILE, ROWS, kind=F32),
            ],
            [SMEM] + [VMEM] * 5,
            flops=1 << 30,
            size=4 << 20,
        )(me, stack, w_keyval, normal_tile, embed_tile, edges)
        for stack in stacks
    ]
    (grads,) = call(
        backward_kernel,
        [shape(WIDTH, 4 * TILE)],
        [SMEM] + [VMEM] * 21,
        [
            pltpu.VMEM((2, HALF * WIDE, 2 * TILE), BF16),
            pltpu.VMEM((TILE, MEMBERS * ROWS), BF16),
            pltpu.VMEM((TILE, MEMBERS * ROWS), BF16),
            pltpu.VMEM((2, HALF * BOTH, ROWS), BF16),
        ],
        flops=2 << 30,
        size=8 << 20,
    )(
        me, *tables[0], *tables[1], normal_tile, inverse, embed_turned, head_tile, head_sum,
        d_pred, loss, *stacks,
    )
    pieces = lax.all_to_all(
        grads.reshape(SHARDS // 2, 2 * NODES, 4 * TILE),
        "shard",
        0,
        0,
        axis_index_groups=[[2 * pair + side for pair in range(SHARDS // 2)] for side in range(2)],
    )
    mine, near, far = call(
        latent_kernel,
        [
            shape(NODES, WIDTH, kind=F32),
            shape(NODES, WIDTH),
            shape(NODES, WIDTH),
        ],
        [VMEM] * 7,
        [pltpu.VMEM((WIDE, 2 * WIDTH), BF16)],
        flops=16 << 30,
        size=8 << 20,
    )(d_own, weights, normed, table, normal, head, w_keyval)
    near = swap(near, "shard", 1)
    far = beyond(far)
    pieces, mine = lax.optimization_barrier((pieces, mine))
    stay, leave = call(
        sum_kernel,
        [shape(NODES, 4 * TILE, kind=F32), shape(NODES, 4 * TILE)],
        [SMEM, VMEM],
        flops=1 << 20,
        size=1 << 20,
    )(me, pieces)
    came = swap(leave, "shard", 1)
    came, near, far = lax.optimization_barrier((came, near, far))
    total, loss = call(
        merge_kernel,
        [shape(NODES, 4 * TILE), shape(1, 1, kind=F32)],
        [VMEM] * 2,
        flops=1 << 16,
        size=1 << 18,
    )(stay, came)
    parts = cores(chips(total))
    grad_query, grad_keyval, grad_head, d_latent = call(
        place_kernel,
        [
            shape(NODES, WIDTH, kind=F32),
            shape(NODES, 2 * WIDTH, kind=F32),
            shape(NODES, VARS, kind=F32),
            shape(NODES, WIDTH, kind=F32),
        ],
        [SMEM] + [VMEM] * 5,
        size=1 << 20,
    )(me, *parts, mine, near, far)
    return (loss.reshape(1), d_latent[None], grad_query, grad_keyval, grad_head)


def solution(mesh):
    placed = (
        P("member", "shard", None),
        P("shard", None),
        P("shard", None),
        P("shard"),
        P("shard", None),
        P(),
        P(),
        P(),
    )
    return jax.shard_map(
        on_device,
        mesh=mesh,
        in_specs=placed,
        out_specs=(
            P("member"),
            P("member", "shard", None),
            P("shard", None),
            P("shard", None),
            P("shard", None),
        ),
        check_vma=False,
    )
```

time: 119 us -> 101 us (0.85)
  starting transfers between devices: 71.5 us -> 47 us
  waiting for transfers between devices: 6.93 us -> 22.6 us
  local copies, waits for them, and re-layouts: 15.9 us -> 6.48 us
  Pallas kernels: 21.9 us -> 23.8 us
  other arithmetic: 1.67 us -> 0.07 us
    ppermute x37 -> x17, starting transfers between devices: 56.4 us -> 31.6 us  [swap(): return lax.ppermute(array, axis, [(i, i ^ bits) for i in range(count)])]
    ppermute x37 -> x17, waiting for transfers between devices: 4.89 us -> 15.9 us  [swap(): return lax.ppermute(array, axis, [(i, i ^ bits) for i in range(count)])]
    unnamed x42 -> x22, local copies, waits for them, and re-layouts: 15.9 us -> 6.48 us
    ppermute x2, starting transfers between devices: 6.01 us -> 11.8 us  [beyond(): lax.ppermute(array, 'shard', [(i, (i + step(i)) % SHARDS) for i in range(...]
    all_to_all x1, starting transfers between devices: 9.13 us -> 3.65 us  [on_device(): lax.all_to_all(grads.reshape(SHARDS // 2, 2 * NODES, 4 * TILE), 'shard',...]
    ppermute x2, waiting for transfers between devices: 1.33 us -> 6.67 us  [beyond(): lax.ppermute(array, 'shard', [(i, (i + step(i)) % SHARDS) for i in range(...]
    pallas_call x5 -> x11, Pallas kernels: 19 us -> 21 us  [the longest x1 5.24 us: on_device(): call(latent_kernel, [shape(NODES, WIDTH, kind=F32), shape(NODES, WIDTH),...]
    broadcast_in_dim x1 -> x0, other arithmetic: 1.57 us -> none  [on_device(): return (loss.reshape(1), d_latent[None], grad_query, grad_keyval, grad_head)]
  transfers between devices with their start and end apart: 40 -> 20, of which waited for: 4 -> 7; matrix products, arithmetic and copies ran while one was open for 1% -> 0% of each run, Pallas kernels for 11% -> 13%
where the time goes in v3:
time: 101 us
  starting transfers between devices  47 us (47%)
  Pallas kernels  23.8 us (24%)
  waiting for transfers between devices  22.6 us (22%)
  local copies, waits for them, and re-layouts  6.48 us (6%)
    ppermute x17, starting transfers between devices, swap(): return lax.ppermute(array, axis, [(i, i ^ bits) for i in range(count)])  31.6 us
    ppermute x17, waiting for transfers between devices, swap(): return lax.ppermute(array, axis, [(i, i ^ bits) for i in range(count)])  15.9 us
    ppermute x2, starting transfers between devices, beyond(): lax.ppermute(array, 'shard', [(i, (i + step(i)) % SHARDS) for i in range(...  11.8 us
    ppermute x2, waiting for transfers between devices, beyond(): lax.ppermute(array, 'shard', [(i, (i + step(i)) % SHARDS) for i in range(...  6.67 us
    unnamed x22, local copies, waits for them, and re-layouts  6.48 us
    pallas_call x1, Pallas kernels, on_device(): call(latent_kernel, [shape(NODES, WIDTH, kind=F32), shape(NODES, WIDTH),...  5.24 us
    pallas_call x1, Pallas kernels, on_device(): call(backward_kernel, [shape(WIDTH, 4 * TILE)], [SMEM] + [VMEM] * 21, [pl...  5.21 us
    pallas_call x2, Pallas kernels, on_device(): call(tables_kernel, [shape(WIDTH, HALF * WIDE), shape(HALF * BOTH, ROWS),...  3.91 us
  transfers between devices with their start and end apart: 20, of which 7 were waited for; matrix products, arithmetic and copies ran while one was open for 0% of the time, Pallas kernels for 13%

profile of v3, /device:TPU:1, one launch (start us, length us, event | category | flops | bytes accessed | tf_op | source)
XLA Modules:
  0.0 100.9 jit_solution(16498671018857283691)
XLA Ops:
  0.6 5.3 %collective-permute-start.4 = (bf16[32,1024]{1,0:T(8,128)(2,1)}, bf16[32,1024]{1,0:T(8,128)(2,1)S(1)}, u32[]{:S(2)}, u32[]{:S(2)}) collective-permute-start(bf16[32,1024]{1,0:T(8,128)(2,1)} %bitcast.12), channel_id=1, source_target_pairs={{0,192},{32,224},{64,128},{96,160},{128,64},{160,96},{192,0},{224,... | collective-permute-start | bytes 196616 | tf_op jit(solution)/shard_map/ppermute | solution.py:421
  6.3 5.7 %collective-permute-start.1 = (bf16[32,1024]{1,0:T(8,128)(2,1)}, bf16[32,1024]{1,0:T(8,128)(2,1)S(1)}, u32[]{:S(2)}, u32[]{:S(2)}) collective-permute-start(bf16[32,1024]{1,0:T(8,128)(2,1)} %bitcast.15), channel_id=1, source_target_pairs={{0,1},{1,0},{2,3},{3,2},{4,5},{5,4},{6,7},{7,6},{8,9},{9,8},{10,11... | collective-permute-start | bytes 196616 | tf_op jit(solution)/shard_map/ppermute | solution.py:421
  12.0 4.6 %collective-permute-start = (bf16[32,1024]{1,0:T(8,128)(2,1)}, bf16[32,1024]{1,0:T(8,128)(2,1)S(1)}, u32[]{:S(2)}, u32[]{:S(2)}) collective-permute-start(bf16[32,1024]{1,0:T(8,128)(2,1)} %bitcast.16), channel_id=1, source_target_pairs={{0,31},{1,2},{2,1},{3,4},{4,3},{5,6},{6,5},{7,8},{8,7},{9,10},{10,... | collective-permute-start | bytes 196616 | tf_op jit(solution)/shard_map/ppermute | solution.py:426
  16.7 1.6 %copy-done.7 = bf16[1024,1024]{1,0:T(8,128)(2,1)S(1)} copy-done((bf16[1024,1024]{1,0:T(8,128)(2,1)S(1)}, bf16[1024,1024]{1,0:T(8,128)(2,1)}, u32[]{:S(2)}) %copy-start.7) | copy-done | bytes 2097176
  20.8 3.1 %collective-permute-done.other = bf16[32,1024]{1,0:T(8,128)(2,1)S(1)} collective-permute-done((bf16[32,1024]{1,0:T(8,128)(2,1)}, bf16[32,1024]{1,0:T(8,128)(2,1)S(1)}, u32[]{:S(2)}, u32[]{:S(2)}) %collective-permute-start) | collective-permute-done | bytes 65568 | tf_op jit(solution)/shard_map/ppermute | solution.py:426
  23.9 2.1 %collective-permute-start.7 = (bf16[32,1024]{1,0:T(8,128)(2,1)S(1)}, bf16[32,1024]{1,0:T(8,128)(2,1)S(1)}, u32[]{:S(2)}, u32[]{:S(2)}) collective-permute-start(bf16[32,1024]{1,0:T(8,128)(2,1)S(1)} %collective-permute-done.1.partner.refs_4_), channel_id=1, source_target_pairs={{0,192},{32,224},{64,128},{96,160},{128,64},{160,96},{192,0},{224,... | collective-permute-start | bytes 196616 | tf_op jit(solution)/shard_map/ppermute | solution.py:421
  26.1 2.7 %shard_map.120 = (bf16[64,1024]{1,0:T(8,128)(2,1)S(1)}, bf16[8,192,256]{2,1,0:T(8,128)(2,1)S(1)}, bf16[1024,256]{1,0:T(8,128)(2,1)S(1)}, bf16[96,2048]{1,0:T(8,128)(2,1)S(1)}) custom-call(s32[2]{0:T(128)S(1)} %pad_add_fusion.me.refs_0_, bf16[32,1024]{1,0:T(8,128)(2,1)S(1)} %bitcast.17, bf16[32,1024]{1,0:T(8,128)(2,1)S(1)} %collective-permute-done.1.partner.refs_4_, ...), custom_call_target="tpu_custom_call" | custom-call | tf_op jit(solution)/shard_map/pallas_call | solution.py:474
  30.8 1.7 %collective-permute-start.8 = (bf16[64,1024]{1,0:T(8,128)(2,1)S(1)}, bf16[64,1024]{1,0:T(8,128)(2,1)S(1)}, u32[]{:S(2)}, u32[]{:S(2)}) collective-permute-start(bf16[64,1024]{1,0:T(8,128)(2,1)S(1)} %get-tuple-element.74.refs_8_), channel_id=1, source_target_pairs={{0,64},{32,96},{64,0},{96,32},{128,192},{160,224},{192,128},{224,1... | collective-permute-start | bytes 393224 | tf_op jit(solution)/shard_map/ppermute | solution.py:421
  33.9 11.4 %collective-permute-done.6.refs_6_ = bf16[32,1024]{1,0:T(8,128)(2,1)S(1)} collective-permute-done((bf16[32,1024]{1,0:T(8,128)(2,1)S(1)}, bf16[32,1024]{1,0:T(8,128)(2,1)S(1)}, u32[]{:S(2)}, u32[]{:S(2)}) %collective-permute-start.6) | collective-permute-done | bytes 65568 | tf_op jit(solution)/shard_map/ppermute | solution.py:421
  45.4 1.8 %collective-permute-start.11 = (bf16[4,128,1024]{2,1,0:T(8,128)(2,1)S(1)}, bf16[4,128,1024]{2,1,0:T(8,128)(2,1)S(1)}, u32[]{:S(2)}, u32[]{:S(2)}) collective-permute-start(bf16[4,128,1024]{2,1,0:T(8,128)(2,1)S(1)} %shard_map.121.stack.mine.refs_20_), channel_id=1, source_target_pairs={{0,32},{32,0},{64,96},{96,64},{128,160},{160,128},{192,224},{224,1... | collective-permute-start | bytes 3145736 | tf_op jit(solution)/shard_map/ppermute | solution.py:421
  48.7 2.0 %shard_map.122 = (bf16[1024,384]{1,0:T(8,128)(2,1)S(1)}, bf16[768,256]{1,0:T(8,128)(2,1)S(1)}, bf16[768,128]{1,0:T(8,128)(2,1)S(1)}, f32[384,128]{1,0:T(8,128)S(...) custom-call(s32[2]{0:T(128)S(1)} %pad_add_fusion.me.refs_0_, ...), custom_call_target="tpu_custom_call" | custom-call | flops 1073741824 | bytes 4194304 | tf_op jit(solution)/shard_map/pallas_call | solution.py:498
  50.7 2.0 %shard_map.123 = (bf16[1024,384]{1,0:T(8,128)(2,1)S(1)}, bf16[768,256]{1,0:T(8,128)(2,1)S(1)}, bf16[768,128]{1,0:T(8,128)(2,1)S(1)}, f32[384,128]{1,0:T(8,128)S(...) custom-call(s32[2]{0:T(128)S(1)} %pad_add_fusion.me.refs_0_, ...), custom_call_target="tpu_custom_call" | custom-call | flops 1073741824 | bytes 4194304 | tf_op jit(solution)/shard_map/pallas_call | solution.py:498
  52.6 1.8 %shard_map.125 = (bf16[128,2048]{1,0:T(8,128)(2,1)S(1)}, bf16[128,256]{1,0:T(8,128)(2,1)S(1)}, f32[1,1]{1,0:T(1,128)}) custom-call(bf16[4,128,1024]{2,1,0:T(8,128)(2,1)S(1)} %shard_map.121.stack.mine.refs_20_, bf16[4,128,1024]{2,1,0:T(8,128)(2,1)S(1)} %collective-permute-done.11.stack.theirs.refs_21_, f32[100,256]{1,0:T(8,128)S(1)} %bitcast.19, ...), custom_call_target="tpu_custom_call" | custom-call | tf_op jit(solution)/shard_map/pallas_call | solution.py:487
  54.4 5.2 %shard_map.126 = bf16[1024,512]{1,0:T(8,128)(2,1)} custom-call(s32[2]{0:T(128)S(1)} %pad_add_fusion.me.refs_0_, bf16[1024,384]{1,0:T(8,128)(2,1)S(1)} %get-tuple-element.77.refs_1_, bf16[768,256]{1,0:T(8,128)(2,1)S(1)} %get-tuple-element.78.refs_2_, bf16[768,128]{1,0:T(8,128)(2,1)S(1)} %get-tuple-element.79.refs_3_, ...), custom_call_target="tpu_custom_call" | custom-call | flops 2147483648 | bytes 8388608 | tf_op jit(solution)/shard_map/pallas_call | solution.py:514
  59.6 3.7 %all-to-all-start = ((bf16[16,64,512]{2,1,0:T(8,128)(2,1)}), bf16[16,64,512]{2,1,0:T(8,128)(2,1)S(1)}, u32[]{:S(2)}, u32[]{:S(2)}) async-start(bf16[16,64,512]{2,1,0:T(8,128)(2,1)} %bitcast.7), calls=%async_computation | async-start | bytes 2097152 | tf_op jit(solution)/shard_map/all_to_all | solution.py:530
  63.3 2.2 %copy-done.1 = bf16[1024,2048]{1,0:T(8,128)(2,1)S(1)} copy-done((bf16[1024,2048]{1,0:T(8,128)(2,1)S(1)}, bf16[1024,2048]{1,0:T(8,128)(2,1)}, u32[]{:S(2)}) %copy-start.1) | copy-done | bytes 4194328
  66.4 5.2 %shard_map.127 = (f32[32,1024]{1,0:T(8,128)S(1)}, bf16[32,1024]{1,0:T(8,128)(2,1)}, bf16[32,1024]{1,0:T(8,128)(2,1)S(1)}) custom-call(bf16[128,256]{1,0:T(8,128)(2,1)S(1)} %get-tuple-element.94.d_own, bf16[8,192,256]{2,1,0:T(8,128)(2,1)S(1)} %get-tuple-element.95.weights, bf16[1024,256]{1,0:T(8,128)(2,1)S(1)} %get-tuple-element.96.normed, ...), custom_call_target="tpu_custom_call" | custom-call | flops 17179869184 | bytes 8388608 | tf_op jit(solution)/shard_map/pallas_call | solution.py:537
  71.7 2.6 %collective-permute-start.13 = (bf16[32,1024]{1,0:T(8,128)(2,1)}, bf16[32,1024]{1,0:T(8,128)(2,1)S(1)}, u32[]{:S(2)}, u32[]{:S(2)}) collective-permute-start(bf16[32,1024]{1,0:T(8,128)(2,1)} %get-tuple-element.103), channel_id=1, source_target_pairs={{0,1},{1,0},{2,3},{3,2},{4,5},{5,4},{6,7},{7,6},{8,9},{9,8},{10,11... | collective-permute-start | bytes 196616 | tf_op jit(solution)/shard_map/ppermute | solution.py:421
  74.2 7.2 %collective-permute-start.14 = (bf16[32,1024]{1,0:T(8,128)(2,1)S(1)}, bf16[32,1024]{1,0:T(8,128)(2,1)S(1)}, u32[]{:S(2)}, u32[]{:S(2)}) collective-permute-start(bf16[32,1024]{1,0:T(8,128)(2,1)S(1)} %get-tuple-element.104), channel_id=1, source_target_pairs={{0,31},{1,2},{2,1},{3,4},{4,3},{5,6},{6,5},{7,8},{8,7},{9,10},{10,... | collective-permute-start | bytes 196616 | tf_op jit(solution)/shard_map/ppermute | solution.py:426
  83.6 3.6 %collective-permute-done.14.far = bf16[32,1024]{1,0:T(8,128)(2,1)S(1)} collective-permute-done((bf16[32,1024]{1,0:T(8,128)(2,1)S(1)}, bf16[32,1024]{1,0:T(8,128)(2,1)S(1)}, u32[]{:S(2)}, u32[]{:S(2)}) %collective-permute-start.14) | collective-permute-done | bytes 65568 | tf_op jit(solution)/shard_map/ppermute | solution.py:426
  87.2 1.7 %collective-permute-done.12.came = bf16[32,512]{1,0:T(8,128)(2,1)S(1)} collective-permute-done((bf16[32,512]{1,0:T(8,128)(2,1)S(1)}, bf16[32,512]{1,0:T(8,128)(2,1)S(1)}, u32[]{:S(2)}, u32[]{:S(2)}) %collective-permute-start.12) | collective-permute-done | bytes 32800 | tf_op jit(solution)/shard_map/ppermute | solution.py:421
  89.5 1.7 %collective-permute-start.17 = (bf16[32,512]{1,0:T(8,128)(2,1)S(1)}, bf16[32,512]{1,0:T(8,128)(2,1)S(1)}, u32[]{:S(2)}, u32[]{:S(2)}) collective-permute-start(bf16[32,512]{1,0:T(8,128)(2,1)S(1)} %get-tuple-element.107.refs_0_), channel_id=1, source_target_pairs={{0,192},{32,224},{64,128},{96,160},{128,64},{160,96},{192,0},{224,... | collective-permute-start | bytes 98312 | tf_op jit(solution)/shard_map/ppermute | solution.py:421
  91.2 1.9 %collective-permute-start.15 = (bf16[32,512]{1,0:T(8,128)(2,1)S(1)}, bf16[32,512]{1,0:T(8,128)(2,1)S(1)}, u32[]{:S(2)}, u32[]{:S(2)}) collective-permute-start(bf16[32,512]{1,0:T(8,128)(2,1)S(1)} %get-tuple-element.107.refs_0_), channel_id=1, source_target_pairs={{0,64},{32,96},{64,0},{96,32},{128,192},{160,224},{192,128},{224,1... | collective-permute-start | bytes 98312 | tf_op jit(solution)/shard_map/ppermute | solution.py:421
  94.9 3.6 %collective-permute-start.18 = (bf16[4,32,512]{2,1,0:T(8,128)(2,1)S(1)}, bf16[4,32,512]{2,1,0:T(8,128)(2,1)S(1)}, u32[]{:S(2)}, u32[]{:S(2)}) collective-permute-start(bf16[4,32,512]{2,1,0:T(8,128)(2,1)S(1)} %shard_map.130.mine), channel_id=1, source_target_pairs={{0,32},{32,0},{64,96},{96,64},{128,160},{160,128},{192,224},{224,1... | collective-permute-start | bytes 393224 | tf_op jit(solution)/shard_map/ppermute | solution.py:421
  (52 shorter events, 15.8 us)
Async XLA Ops:
  0.6 28.2 %collective-permute-start.4 = (bf16[32,1024]{1,0:T(8,128)(2,1)}, bf16[32,1024]{1,0:T(8,128)(2,1)S(1)}, u32[]{:S(2)}, u32[]{:S(2)}) collective-permute-start(bf16[32,1024]{1,0:T(8,128)(2,1)} %bitcast.12), channel_id=1, source_target_pairs={{0,192},{32,224},{64,128},{96,160},{128,64},{160,96},{192,0},{224,... | collective-permute-start | bytes 196616 | tf_op jit(solution)/shard_map/ppermute | solution.py:421
  5.9 22.9 %collective-permute-start.3 = (bf16[32,1024]{1,0:T(8,128)(2,1)}, bf16[32,1024]{1,0:T(8,128)(2,1)S(1)}, u32[]{:S(2)}, u32[]{:S(2)}) collective-permute-start(bf16[32,1024]{1,0:T(8,128)(2,1)} %bitcast.13), channel_id=1, source_target_pairs={{0,128},{32,160},{64,192},{96,224},{128,0},{160,32},{192,64},{224,... | collective-permute-start | bytes 196616 | tf_op jit(solution)/shard_map/ppermute | solution.py:421
  5.9 22.9 %collective-permute-start.2 = (bf16[32,1024]{1,0:T(8,128)(2,1)}, bf16[32,1024]{1,0:T(8,128)(2,1)S(1)}, u32[]{:S(2)}, u32[]{:S(2)}) collective-permute-start(bf16[32,1024]{1,0:T(8,128)(2,1)} %bitcast.14), channel_id=1, source_target_pairs={{0,64},{32,96},{64,0},{96,32},{128,192},{160,224},{192,128},{224,1... | collective-permute-start | bytes 196616 | tf_op jit(solution)/shard_map/ppermute | solution.py:421
  6.3 14.5 %collective-permute-start.1 = (bf16[32,1024]{1,0:T(8,128)(2,1)}, bf16[32,1024]{1,0:T(8,128)(2,1)S(1)}, u32[]{:S(2)}, u32[]{:S(2)}) collective-permute-start(bf16[32,1024]{1,0:T(8,128)(2,1)} %bitcast.15), channel_id=1, source_target_pairs={{0,1},{1,0},{2,3},{3,2},{4,5},{5,4},{6,7},{7,6},{8,9},{9,8},{10,11... | collective-permute-start | bytes 196616 | tf_op jit(solution)/shard_map/ppermute | solution.py:421
  12.0 11.9 %collective-permute-start = (bf16[32,1024]{1,0:T(8,128)(2,1)}, bf16[32,1024]{1,0:T(8,128)(2,1)S(1)}, u32[]{:S(2)}, u32[]{:S(2)}) collective-permute-start(bf16[32,1024]{1,0:T(8,128)(2,1)} %bitcast.16), channel_id=1, source_target_pairs={{0,31},{1,2},{2,1},{3,4},{4,3},{5,6},{6,5},{7,8},{8,7},{9,10},{10,... | collective-permute-start | bytes 196616 | tf_op jit(solution)/shard_map/ppermute | solution.py:426
  19.4 6.7 %copy-start = (bf16[1024,2048]{1,0:T(8,128)(2,1)S(1)}, bf16[1024,2048]{1,0:T(8,128)(2,1)}, u32[]{:S(2)}) copy-start(bf16[1024,2048]{1,0:T(8,128)(2,1)} %w_keyval.7) | copy-start | bytes 12582916
  19.4 6.7 %copy-start.2 = (bf16[1024,100]{0,1:T(8,128)(2,1)S(1)}, bf16[1024,100]{0,1:T(8,128)(2,1)}, u32[]{:S(2)}) copy-start(bf16[1024,100]{0,1:T(8,128)(2,1)} %param.15) | copy-start | bytes 614404
  19.4 6.7 %copy-start.3 = (bf16[1,32,1024]{2,1,0:T(8,128)(2,1)S(1)}, bf16[1,32,1024]{2,1,0:T(8,128)(2,1)}, u32[]{:S(2)}) copy-start(bf16[1,32,1024]{2,1,0:T(8,128)(2,1)} %param.8) | copy-start | bytes 196612
  19.4 6.7 %copy-start.5 = (s32[256,3]{0,1:T(4,128)S(1)}, s32[256,3]{0,1:T(4,128)}, u32[]{:S(2)}) copy-start(s32[256,3]{0,1:T(4,128)} %param.10) | copy-start | bytes 9220
  23.9 8.5 %collective-permute-start.7 = (bf16[32,1024]{1,0:T(8,128)(2,1)S(1)}, bf16[32,1024]{1,0:T(8,128)(2,1)S(1)}, u32[]{:S(2)}, u32[]{:S(2)}) collective-permute-start(bf16[32,1024]{1,0:T(8,128)(2,1)S(1)} %collective-permute-done.1.partner.refs_4_), channel_id=1, source_target_pairs={{0,192},{32,224},{64,128},{96,160},{128,64},{160,96},{192,0},{224,... | collective-permute-start | bytes 196616 | tf_op jit(solution)/shard_map/ppermute | solution.py:421
  28.8 16.5 %collective-permute-start.10 = (bf16[64,1024]{1,0:T(8,128)(2,1)S(1)}, bf16[64,1024]{1,0:T(8,128)(2,1)S(1)}, u32[]{:S(2)}, u32[]{:S(2)}) collective-permute-start(bf16[64,1024]{1,0:T(8,128)(2,1)S(1)} %get-tuple-element.74.refs_8_), channel_id=1, source_target_pairs={{0,192},{32,224},{64,128},{96,160},{128,64},{160,96},{192,0},{224,... | collective-permute-start | bytes 393224 | tf_op jit(solution)/shard_map/ppermute | solution.py:421
  30.1 15.3 %collective-permute-start.9 = (bf16[64,1024]{1,0:T(8,128)(2,1)S(1)}, bf16[64,1024]{1,0:T(8,128)(2,1)S(1)}, u32[]{:S(2)}, u32[]{:S(2)}) collective-permute-start(bf16[64,1024]{1,0:T(8,128)(2,1)S(1)} %get-tuple-element.74.refs_8_), channel_id=1, source_target_pairs={{0,128},{32,160},{64,192},{96,224},{128,0},{160,32},{192,64},{224,... | collective-permute-start | bytes 393224 | tf_op jit(solution)/shard_map/ppermute | solution.py:421
  30.8 14.6 %collective-permute-start.8 = (bf16[64,1024]{1,0:T(8,128)(2,1)S(1)}, bf16[64,1024]{1,0:T(8,128)(2,1)S(1)}, u32[]{:S(2)}, u32[]{:S(2)}) collective-permute-start(bf16[64,1024]{1,0:T(8,128)(2,1)S(1)} %get-tuple-element.74.refs_8_), channel_id=1, source_target_pairs={{0,64},{32,96},{64,0},{96,32},{128,192},{160,224},{192,128},{224,1... | collective-permute-start | bytes 393224 | tf_op jit(solution)/shard_map/ppermute | solution.py:421
  32.5 12.9 %collective-permute-start.6 = (bf16[32,1024]{1,0:T(8,128)(2,1)S(1)}, bf16[32,1024]{1,0:T(8,128)(2,1)S(1)}, u32[]{:S(2)}, u32[]{:S(2)}) collective-permute-start(bf16[32,1024]{1,0:T(8,128)(2,1)S(1)} %collective-permute-done.1.partner.refs_4_), channel_id=1, source_target_pairs={{0,128},{32,160},{64,192},{96,224},{128,0},{160,32},{192,64},{224,... | collective-permute-start | bytes 196616 | tf_op jit(solution)/shard_map/ppermute | solution.py:421
  32.5 12.8 %collective-permute-start.5 = (bf16[32,1024]{1,0:T(8,128)(2,1)S(1)}, bf16[32,1024]{1,0:T(8,128)(2,1)S(1)}, u32[]{:S(2)}, u32[]{:S(2)}) collective-permute-start(bf16[32,1024]{1,0:T(8,128)(2,1)S(1)} %collective-permute-done.1.partner.refs_4_), channel_id=1, source_target_pairs={{0,64},{32,96},{64,0},{96,32},{128,192},{160,224},{192,128},{224,1... | collective-permute-start | bytes 196616 | tf_op jit(solution)/shard_map/ppermute | solution.py:421
  45.4 5.2 %collective-permute-start.11 = (bf16[4,128,1024]{2,1,0:T(8,128)(2,1)S(1)}, bf16[4,128,1024]{2,1,0:T(8,128)(2,1)S(1)}, u32[]{:S(2)}, u32[]{:S(2)}) collective-permute-start(bf16[4,128,1024]{2,1,0:T(8,128)(2,1)S(1)} %shard_map.121.stack.mine.refs_20_), channel_id=1, source_target_pairs={{0,32},{32,0},{64,96},{96,64},{128,160},{160,128},{192,224},{224,1... | collective-permute-start | bytes 3145736 | tf_op jit(solution)/shard_map/ppermute | solution.py:421
  59.6 21.8 %all-to-all-start = ((bf16[16,64,512]{2,1,0:T(8,128)(2,1)}), bf16[16,64,512]{2,1,0:T(8,128)(2,1)S(1)}, u32[]{:S(2)}, u32[]{:S(2)}) async-start(bf16[16,64,512]{2,1,0:T(8,128)(2,1)} %bitcast.7), calls=%async_computation | async-start | bytes 2097152 | tf_op jit(solution)/shard_map/all_to_all | solution.py:530
  71.7 11.9 %collective-permute-start.13 = (bf16[32,1024]{1,0:T(8,128)(2,1)}, bf16[32,1024]{1,0:T(8,128)(2,1)S(1)}, u32[]{:S(2)}, u32[]{:S(2)}) collective-permute-start(bf16[32,1024]{1,0:T(8,128)(2,1)} %get-tuple-element.103), channel_id=1, source_target_pairs={{0,1},{1,0},{2,3},{3,2},{4,5},{5,4},{6,7},{7,6},{8,9},{9,8},{10,11... | collective-permute-start | bytes 196616 | tf_op jit(solution)/shard_map/ppermute | solution.py:421
  74.2 12.9 %collective-permute-start.14 = (bf16[32,1024]{1,0:T(8,128)(2,1)S(1)}, bf16[32,1024]{1,0:T(8,128)(2,1)S(1)}, u32[]{:S(2)}, u32[]{:S(2)}) collective-permute-start(bf16[32,1024]{1,0:T(8,128)(2,1)S(1)} %get-tuple-element.104), channel_id=1, source_target_pairs={{0,31},{1,2},{2,1},{3,4},{4,3},{5,6},{6,5},{7,8},{8,7},{9,10},{10,... | collective-permute-start | bytes 196616 | tf_op jit(solution)/shard_map/ppermute | solution.py:426
  82.1 6.8 %collective-permute-start.12 = (bf16[32,512]{1,0:T(8,128)(2,1)S(1)}, bf16[32,512]{1,0:T(8,128)(2,1)S(1)}, u32[]{:S(2)}, u32[]{:S(2)}) collective-permute-start(bf16[32,512]{1,0:T(8,128)(2,1)S(1)} %get-tuple-element.102), channel_id=1, source_target_pairs={{0,1},{1,0},{2,3},{3,2},{4,5},{5,4},{6,7},{7,6},{8,9},{9,8},{10,11... | collective-permute-start | bytes 98312 | tf_op jit(solution)/shard_map/ppermute | solution.py:421
  89.5 4.6 %collective-permute-start.17 = (bf16[32,512]{1,0:T(8,128)(2,1)S(1)}, bf16[32,512]{1,0:T(8,128)(2,1)S(1)}, u32[]{:S(2)}, u32[]{:S(2)}) collective-permute-start(bf16[32,512]{1,0:T(8,128)(2,1)S(1)} %get-tuple-element.107.refs_0_), channel_id=1, source_target_pairs={{0,192},{32,224},{64,128},{96,160},{128,64},{160,96},{192,0},{224,... | collective-permute-start | bytes 98312 | tf_op jit(solution)/shard_map/ppermute | solution.py:421
  91.2 3.7 %collective-permute-start.16 = (bf16[32,512]{1,0:T(8,128)(2,1)S(1)}, bf16[32,512]{1,0:T(8,128)(2,1)S(1)}, u32[]{:S(2)}, u32[]{:S(2)}) collective-permute-start(bf16[32,512]{1,0:T(8,128)(2,1)S(1)} %get-tuple-element.107.refs_0_), channel_id=1, source_target_pairs={{0,128},{32,160},{64,192},{96,224},{128,0},{160,32},{192,64},{224,... | collective-permute-start | bytes 98312 | tf_op jit(solution)/shard_map/ppermute | solution.py:421
  91.2 3.7 %collective-permute-start.15 = (bf16[32,512]{1,0:T(8,128)(2,1)S(1)}, bf16[32,512]{1,0:T(8,128)(2,1)S(1)}, u32[]{:S(2)}, u32[]{:S(2)}) collective-permute-start(bf16[32,512]{1,0:T(8,128)(2,1)S(1)} %get-tuple-element.107.refs_0_), channel_id=1, source_target_pairs={{0,64},{32,96},{64,0},{96,32},{128,192},{160,224},{192,128},{224,1... | collective-permute-start | bytes 98312 | tf_op jit(solution)/shard_map/ppermute | solution.py:421
  94.9 4.6 %collective-permute-start.18 = (bf16[4,32,512]{2,1,0:T(8,128)(2,1)S(1)}, bf16[4,32,512]{2,1,0:T(8,128)(2,1)S(1)}, u32[]{:S(2)}, u32[]{:S(2)}) collective-permute-start(bf16[4,32,512]{2,1,0:T(8,128)(2,1)S(1)} %shard_map.130.mine), channel_id=1, source_target_pairs={{0,32},{32,0},{64,96},{96,64},{128,160},{160,128},{192,224},{224,1... | collective-permute-start | bytes 393224 | tf_op jit(solution)/shard_map/ppermute | solution.py:421
  (7 other events, 14.4 us)

commit v4 on v3

--- a/solution.py
+++ b/solution.py
@@ -138,7 +138,7 @@
 
 def weigh(scores, count):
     groups = scores.shape[0] // WIDE
-    expon = jnp.exp(scores * SIZE**-0.5).reshape(groups, WIDE, ROWS) * count[None]
+    expon = jnp.exp(scores).reshape(groups, WIDE, ROWS) * count[None]
     weight = expon * (1.0 / jnp.sum(expon, 1, keepdims=True))
     return weight.astype(BF16).reshape(groups * WIDE, ROWS)
 
@@ -154,7 +154,7 @@
     table[...] = low
     tiles = [slice(t * TILE, (t + 1) * TILE) for t in range(TILES)]
     raw = jnp.concatenate([low[:, at] for at in tiles], 0).astype(F32)
-    keys = key_parts(raw)[0].astype(BF16)
+    keys = key_parts(raw)[0].astype(BF16) * BF16(SIZE**-0.5)
     scores = [
         dot(stack_heads(keys[t * WIDE : (t + 1) * WIDE]), normal[at, :])
         for t, at in enumerate(tiles)
@@ -203,7 +203,7 @@
     at = pl.multiple_of(WIDTH + at, TILE)
     value = dot(flat, w_keyval[:, pl.ds(at, TILE)]).astype(BF16)
     key_roots[...] = root
-    key = key.astype(BF16)
+    key = key.astype(BF16) * BF16(SIZE**-0.5)
     members = [slice(i * WIDE, (i + 1) * WIDE) for i in range(HALF)]
     key = jnp.concatenate([stack_heads(key[rows]) for rows in members], 0)
     value = jnp.concatenate([stack_heads(value[rows]) for rows in members], 0)
@@ -215,14 +215,6 @@
     for i in range(HALF):
         rows = slice(i * BOTH, (i + 1) * BOTH)
         hidden[i] = base + dot_tn(value[rows], weight[rows])
-
-
-def head_kernel(me, w_head, head, head_tile, head_sum):
-    at = pl.multiple_of(me[0] * TILE, TILE)
-    rows = jnp.concatenate([w_head[...], jnp.zeros((TILE - VARS, WIDTH), BF16)], 0)
-    head[...] = rows.T
-    head_tile[...] = head[pl.ds(at, TILE), :]
-    head_sum[...] = jnp.sum(rows.astype(F32), 1, keepdims=True)
 
 
 def payload_rows(stack, i, start, size):
@@ -285,17 +277,18 @@
     me = refs[0]
     sets = (refs[1:7], refs[7:13])
     (
-        normal_tile, inverse, embed_turned, head_tile, head_sum, d_pred, loss, mine, theirs,
+        normal_tile, inverse, embed_turned, w_head, d_pred, loss, mine, theirs,
         payload, d_table, normed_all, d_mixed_all, d_score_all,
     ) = refs[13:]
     stacks = (mine, theirs)
     here = me[0]
     query = normal_tile[...]
-    sums = head_sum[...]
     out = d_pred[...]
     wide = out.astype(F32)
-    d_normed = dot(head_tile[...], out)
-    levels = jnp.sum(wide * sums, 0, keepdims=True) / WIDTH
+    sums = jnp.sum(w_head[...].astype(F32), 1, keepdims=True)
+    at = pl.multiple_of(here * TILE, TILE)
+    d_normed = dot_tn(w_head[:, pl.ds(at, TILE)], out[:VARS])
+    levels = jnp.sum(wide[:VARS] * sums, 0, keepdims=True) / WIDTH
     for k in range(MEMBERS):
         side, i = k % 2, k // 2
         cols = slice(k * ROWS, (k + 1) * ROWS)
@@ -317,23 +310,24 @@
         weight = sets[side][1][rows, :].astype(F32).reshape(2, WIDE, ROWS)
         d_weight = d_weight.reshape(2, WIDE, ROWS)
         d_score = weight * (d_weight - jnp.sum(weight * d_weight, 1, keepdims=True))
-        d_score_all[side, rows, :] = (
-            (d_score * SIZE**-0.5).astype(BF16).reshape(BOTH, ROWS)
-        )
+        d_score_all[side, rows, :] = d_score.astype(BF16).reshape(BOTH, ROWS)
     d_query = jnp.zeros((TILE, ROWS), F32)
     for side in range(2):
         turned, weights, keys, key_roots, values, hidden = sets[side]
         d_score = d_score_all[side]
         d_query = d_query + dot_tn(keys[...], d_score)
-        d_both = dot_nt(d_score, query)
+        d_both = dot_nt(d_score, query * BF16(SIZE**-0.5))
         parts = [slice(i * BOTH, (i + 1) * BOTH) for i in range(HALF)]
         d_key = jnp.concatenate([unstack_heads(d_both[rows]) for rows in parts], 0)
-        key = jnp.concatenate([unstack_heads(keys[rows, :]) for rows in parts], 0).astype(F32)
-        d_table[side, :, :TILE] = key_back(d_key, key, key_roots[...]).astype(BF16)
+        key = jnp.concatenate([unstack_heads(keys[rows, :]) for rows in parts], 0)
+        key = key.astype(F32) * SIZE**0.5
+        d_table[side, :, :TILE] = key_back(d_key, key, key_roots[...] * SCALE).astype(BF16)
         for i, rows in enumerate(parts):
             k = 2 * i + side
             d_value = dot_nt(weights[rows, :], d_mixed_all[:, k * ROWS : (k + 1) * ROWS])
-            d_table[side, i * WIDE : (i + 1) * WIDE, TILE:] = unstack_heads(d_value).astype(BF16)
+            d_table[side, i * WIDE : (i + 1) * WIDE, TILE:] = (
+                unstack_heads(d_value) * SCALE
+            ).astype(BF16)
     wide_query = query.astype(F32)
     along = d_query * wide_query
     along = jnp.concatenate(
@@ -343,11 +337,11 @@
         ],
         0,
     )
-    d_query = inverse[...] * (d_query - wide_query * along)
+    d_query = inverse[...] * SCALE * (d_query - wide_query * along)
     grad = dot_nt(embed_turned[...], d_query.astype(BF16))
-    payload[:, :TILE] = (grad * SCALE).astype(BF16)
+    payload[:, :TILE] = grad.astype(BF16)
     grad = dot(sets[0][0][...], d_table[0]) + dot(sets[1][0][...], d_table[1])
-    payload[:, TILE : 3 * TILE] = (grad * SCALE).astype(BF16)
+    payload[:, TILE : 3 * TILE] = grad.astype(BF16)
     high = loss[...].astype(BF16).astype(F32)
     lane = iota((WIDTH, TILE), 1)
     side = jnp.where(lane == VARS, high, jnp.where(lane == VARS + 1, loss[...] - high, 0.0))
@@ -359,14 +353,14 @@
 
 
 def latent_kernel(
-    d_own, weights, normed, table, normal, head, w_keyval,
+    d_own, weights, normed, table, normal, w_head, w_keyval,
     own, partner, other, d_table,
 ):
     tail = d_own[CARRY:, :].astype(F32)
     at = VARS + 2 - EDGE
     scale = tail[at : at + 1] + tail[at + 1 : at + 2]
     result = normed[...].astype(F32)
-    d_normed = dot(head[...], d_own[...])
+    d_normed = dot_tn(w_head[...], d_own[:VARS, :])
     level = jnp.mean(d_normed, 0, keepdims=True)
     along = jnp.mean(d_normed * result, 0, keepdims=True)
     d_mixed = (scale * (d_normed - level - result * along)).astype(BF16)
@@ -454,7 +448,6 @@
     edges, head_turned = edge_src.T, w_head.T
     partner = swap(own, "shard", 1)
     other = beyond(own)
-    own_far = chips(own)
     prepared = call(
         prepare_kernel,
         [
@@ -468,6 +461,8 @@
         flops=20 << 30,
         size=4 << 20,
     )(me, grid_embed, w_query)
+    early, prepared = lax.optimization_barrier((own, prepared))
+    own_far = chips(early)
     prepared, other, partner = lax.optimization_barrier((prepared, other, partner))
     normal, normal_tile, inverse, embed_turned, embed_tile = prepared
     partner_far = chips(partner)
@@ -489,11 +484,6 @@
         [shape(TILE, MEMBERS * ROWS), shape(TILE, ROWS), shape(1, 1, kind=F32)],
         [VMEM] * 4,
     )(*stacks, target.T, area.reshape(1, ROWS))
-    head, head_tile, head_sum = call(
-        head_kernel,
-        [shape(WIDTH, TILE), shape(TILE, TILE), shape(TILE, 1, kind=F32)],
-        [SMEM, VMEM],
-    )(me, head_turned)
     tables = [
         call(
             tables_kernel,
@@ -514,7 +504,7 @@
     (grads,) = call(
         backward_kernel,
         [shape(WIDTH, 4 * TILE)],
-        [SMEM] + [VMEM] * 21,
+        [SMEM] + [VMEM] * 20,
         [
             pltpu.VMEM((2, HALF * WIDE, 2 * TILE), BF16),
             pltpu.VMEM((TILE, MEMBERS * ROWS), BF16),
@@ -524,7 +514,7 @@
         flops=2 << 30,
         size=8 << 20,
     )(
-        me, *tables[0], *tables[1], normal_tile, inverse, embed_turned, head_tile, head_sum,
+        me, *tables[0], *tables[1], normal_tile, inverse, embed_turned, head_turned,
         d_pred, loss, *stacks,
     )
     pieces = lax.all_to_all(
@@ -545,7 +535,7 @@
         [pltpu.VMEM((WIDE, 2 * WIDTH), BF16)],
         flops=16 << 30,
         size=8 << 20,
-    )(d_own, weights, normed, table, normal, head, w_keyval)
+    )(d_own, weights, normed, table, normal, head_turned, w_keyval)
     near = swap(near, "shard", 1)
     far = beyond(far)
     pieces, mine = lax.optimization_barrier((pieces, mine))

time: 101 us -> 97.8 us (0.968)
  waiting for transfers between devices: 22.6 us -> 19.3 us
  starting transfers between devices: 47 us -> 48.9 us
  Pallas kernels: 23.8 us -> 22.6 us
    ppermute x17, starting transfers between devices: 31.6 us -> 35.2 us  [swap(): return lax.ppermute(array, axis, [(i, i ^ bits) for i in range(count)])]
    ppermute x2, waiting for transfers between devices: 6.67 us -> 3.42 us  [beyond(): lax.ppermute(array, 'shard', [(i, (i + step(i)) % SHARDS) for i in range(...]
    ppermute x2, starting transfers between devices: 11.8 us -> 10 us  [beyond(): lax.ppermute(array, 'shard', [(i, (i + step(i)) % SHARDS) for i in range(...]
    pallas_call x2 -> x1, Pallas kernels: 5.94 us -> 5.27 us  [on_device(): call(backward_kernel, [shape(WIDTH, 4 * TILE)], [SMEM] + [VMEM] * 20, [pl...]
  transfers between devices with their start and end apart: 20 -> 20, of which waited for: 7 -> 8; matrix products, arithmetic and copies ran while one was open for 0% -> 0% of each run, Pallas kernels for 13% -> 12%
where the time goes in v4:
time: 97.8 us; the launch traced here: 97.5 us
  starting transfers between devices  48.9 us (50%)
  Pallas kernels  22.6 us (23%)
  waiting for transfers between devices  19.3 us (20%)
  local copies, waits for them, and re-layouts  5.84 us (6%)
    ppermute x17, starting transfers between devices, swap(): return lax.ppermute(array, axis, [(i, i ^ bits) for i in range(count)])  35.2 us
    ppermute x17, waiting for transfers between devices, swap(): return lax.ppermute(array, axis, [(i, i ^ bits) for i in range(count)])  15.8 us
    ppermute x2, starting transfers between devices, beyond(): lax.ppermute(array, 'shard', [(i, (i + step(i)) % SHARDS) for i in range(...  10 us
    unnamed x22, local copies, waits for them, and re-layouts  5.84 us
    pallas_call x1, Pallas kernels, on_device(): call(backward_kernel, [shape(WIDTH, 4 * TILE)], [SMEM] + [VMEM] * 20, [pl...  5.27 us
    pallas_call x1, Pallas kernels, on_device(): call(latent_kernel, [shape(NODES, WIDTH, kind=F32), shape(NODES, WIDTH),...  4.66 us
    pallas_call x2, Pallas kernels, on_device(): call(tables_kernel, [shape(WIDTH, HALF * WIDE), shape(HALF * BOTH, ROWS),...  3.9 us
    all_to_all x1, starting transfers between devices, on_device(): lax.all_to_all(grads.reshape(SHARDS // 2, 2 * NODES, 4 * TILE), 'shard',...  3.65 us
  transfers between devices with their start and end apart: 20, of which 8 were waited for; matrix products, arithmetic and copies ran while one was open for 0% of the time, Pallas kernels for 12%

profile of v4, /device:TPU:1, one launch (start us, length us, event | category | flops | bytes accessed | tf_op | source)
XLA Modules:
  0.0 97.5 jit_solution(7508392303203140290)
XLA Ops:
  0.6 7.8 %collective-permute-start.1 = (bf16[32,1024]{1,0:T(8,128)(2,1)}, bf16[32,1024]{1,0:T(8,128)(2,1)S(1)}, u32[]{:S(2)}, u32[]{:S(2)}) collective-permute-start(bf16[32,1024]{1,0:T(8,128)(2,1)} %bitcast.13), channel_id=1, source_target_pairs={{0,1},{1,0},{2,3},{3,2},{4,5},{5,4},{6,7},{7,6},{8,9},{9,8},{10,11... | collective-permute-start | bytes 196616 | tf_op jit(solution)/shard_map/ppermute | solution.py:415
  8.5 4.7 %collective-permute-start = (bf16[32,1024]{1,0:T(8,128)(2,1)}, bf16[32,1024]{1,0:T(8,128)(2,1)S(1)}, u32[]{:S(2)}, u32[]{:S(2)}) collective-permute-start(bf16[32,1024]{1,0:T(8,128)(2,1)} %bitcast.14), channel_id=1, source_target_pairs={{0,31},{1,2},{2,1},{3,4},{4,3},{5,6},{6,5},{7,8},{8,7},{9,10},{10,... | collective-permute-start | bytes 196616 | tf_op jit(solution)/shard_map/ppermute | solution.py:420
  13.3 1.6 %copy-done.7 = bf16[1024,1024]{1,0:T(8,128)(2,1)S(1)} copy-done((bf16[1024,1024]{1,0:T(8,128)(2,1)S(1)}, bf16[1024,1024]{1,0:T(8,128)(2,1)}, u32[]{:S(2)}) %copy-start.7) | copy-done | bytes 2097176
  17.4 2.8 %collective-permute-start.4 = (bf16[32,1024]{1,0:T(8,128)(2,1)S(1)}, bf16[32,1024]{1,0:T(8,128)(2,1)S(1)}, u32[]{:S(2)}, u32[]{:S(2)}) collective-permute-start(bf16[32,1024]{1,0:T(8,128)(2,1)S(1)} %bitcast.15), channel_id=1, source_target_pairs={{0,192},{32,224},{64,128},{96,160},{128,64},{160,96},{192,0},{224,... | collective-permute-start | bytes 196616 | tf_op jit(solution)/shard_map/ppermute | solution.py:415
  21.0 2.7 %collective-permute-start.7 = (bf16[32,1024]{1,0:T(8,128)(2,1)S(1)}, bf16[32,1024]{1,0:T(8,128)(2,1)S(1)}, u32[]{:S(2)}, u32[]{:S(2)}) collective-permute-start(bf16[32,1024]{1,0:T(8,128)(2,1)S(1)} %collective-permute-done.1.partner.refs_4_), channel_id=1, source_target_pairs={{0,192},{32,224},{64,128},{96,160},{128,64},{160,96},{192,0},{224,... | collective-permute-start | bytes 196616 | tf_op jit(solution)/shard_map/ppermute | solution.py:415
  23.7 2.7 %shard_map.120 = (bf16[64,1024]{1,0:T(8,128)(2,1)S(1)}, bf16[8,192,256]{2,1,0:T(8,128)(2,1)S(1)}, bf16[1024,256]{1,0:T(8,128)(2,1)S(1)}, bf16[96,2048]{1,0:T(8,128)(2,1)S(1)}) custom-call(s32[2]{0:T(128)S(1)} %pad_add_fusion.me.refs_0_, bf16[32,1024]{1,0:T(8,128)(2,1)S(1)} %bitcast.18, bf16[32,1024]{1,0:T(8,128)(2,1)S(1)} %collective-permute-done.1.partner.refs_4_, ...), custom_call_target="tpu_custom_call" | custom-call | tf_op jit(solution)/shard_map/pallas_call | solution.py:469
  27.0 1.8 %collective-permute-start.10 = (bf16[64,1024]{1,0:T(8,128)(2,1)S(1)}, bf16[64,1024]{1,0:T(8,128)(2,1)S(1)}, u32[]{:S(2)}, u32[]{:S(2)}) collective-permute-start(bf16[64,1024]{1,0:T(8,128)(2,1)S(1)} %get-tuple-element.83.refs_8_), channel_id=1, source_target_pairs={{0,192},{32,224},{64,128},{96,160},{128,64},{160,96},{192,0},{224,... | collective-permute-start | bytes 393224 | tf_op jit(solution)/shard_map/ppermute | solution.py:415
  28.8 1.7 %collective-permute-start.8 = (bf16[64,1024]{1,0:T(8,128)(2,1)S(1)}, bf16[64,1024]{1,0:T(8,128)(2,1)S(1)}, u32[]{:S(2)}, u32[]{:S(2)}) collective-permute-start(bf16[64,1024]{1,0:T(8,128)(2,1)S(1)} %get-tuple-element.83.refs_8_), channel_id=1, source_target_pairs={{0,64},{32,96},{64,0},{96,32},{128,192},{160,224},{192,128},{224,1... | collective-permute-start | bytes 393224 | tf_op jit(solution)/shard_map/ppermute | solution.py:415
  32.6 10.2 %collective-permute-done.6.refs_6_ = bf16[32,1024]{1,0:T(8,128)(2,1)S(1)} collective-permute-done((bf16[32,1024]{1,0:T(8,128)(2,1)S(1)}, bf16[32,1024]{1,0:T(8,128)(2,1)S(1)}, u32[]{:S(2)}, u32[]{:S(2)}) %collective-permute-start.6) | collective-permute-done | bytes 65568 | tf_op jit(solution)/shard_map/ppermute | solution.py:415
  44.5 2.0 %shard_map.122 = (bf16[1024,384]{1,0:T(8,128)(2,1)S(1)}, bf16[768,256]{1,0:T(8,128)(2,1)S(1)}, bf16[768,128]{1,0:T(8,128)(2,1)S(1)}, f32[384,128]{1,0:T(8,128)S(...) custom-call(s32[2]{0:T(128)S(1)} %pad_add_fusion.me.refs_0_, ...), custom_call_target="tpu_custom_call" | custom-call | flops 1073741824 | bytes 4194304 | tf_op jit(solution)/shard_map/pallas_call | solution.py:488
  46.8 2.0 %shard_map.123 = (bf16[1024,384]{1,0:T(8,128)(2,1)S(1)}, bf16[768,256]{1,0:T(8,128)(2,1)S(1)}, bf16[768,128]{1,0:T(8,128)(2,1)S(1)}, f32[384,128]{1,0:T(8,128)S(...) custom-call(s32[2]{0:T(128)S(1)} %pad_add_fusion.me.refs_0_, ...), custom_call_target="tpu_custom_call" | custom-call | flops 1073741824 | bytes 4194304 | tf_op jit(solution)/shard_map/pallas_call | solution.py:488
  48.8 1.8 %shard_map.124 = (bf16[128,2048]{1,0:T(8,128)(2,1)S(1)}, bf16[128,256]{1,0:T(8,128)(2,1)S(1)}, f32[1,1]{1,0:T(1,128)}) custom-call(bf16[4,128,1024]{2,1,0:T(8,128)(2,1)S(1)} %shard_map.121.stack.mine.refs_19_, bf16[4,128,1024]{2,1,0:T(8,128)(2,1)S(1)} %collective-permute-done.11.stack.theirs.refs_20_, f32[100,256]{1,0:T(8,128)S(1)} %bitcast.20, ...), custom_call_target="tpu_custom_call" | custom-call | tf_op jit(solution)/shard_map/pallas_call | solution.py:482
  50.6 5.3 %shard_map.125 = bf16[1024,512]{1,0:T(8,128)(2,1)} custom-call(s32[2]{0:T(128)S(1)} %pad_add_fusion.me.refs_0_, bf16[1024,384]{1,0:T(8,128)(2,1)S(1)} %get-tuple-element.86.refs_1_, bf16[768,256]{1,0:T(8,128)(2,1)S(1)} %get-tuple-element.87.refs_2_, bf16[768,128]{1,0:T(8,128)(2,1)S(1)} %get-tuple-element.88.refs_3_, ...), custom_call_target="tpu_custom_call" | custom-call | flops 2147483648 | bytes 8388608 | tf_op jit(solution)/shard_map/pallas_call | solution.py:504
  55.8 3.7 %all-to-all-start = ((bf16[16,64,512]{2,1,0:T(8,128)(2,1)}), bf16[16,64,512]{2,1,0:T(8,128)(2,1)S(1)}, u32[]{:S(2)}, u32[]{:S(2)}) async-start(bf16[16,64,512]{2,1,0:T(8,128)(2,1)} %bitcast.7), calls=%async_computation | async-start | bytes 2097152 | tf_op jit(solution)/shard_map/all_to_all | solution.py:520
  59.5 2.2 %copy-done.1 = bf16[1024,2048]{1,0:T(8,128)(2,1)S(1)} copy-done((bf16[1024,2048]{1,0:T(8,128)(2,1)S(1)}, bf16[1024,2048]{1,0:T(8,128)(2,1)}, u32[]{:S(2)}) %copy-start.1) | copy-done | bytes 4194328
  62.7 4.7 %shard_map.126 = (f32[32,1024]{1,0:T(8,128)S(1)}, bf16[32,1024]{1,0:T(8,128)(2,1)S(1)}, bf16[32,1024]{1,0:T(8,128)(2,1)S(1)}) custom-call(bf16[128,256]{1,0:T(8,128)(2,1)S(1)} %get-tuple-element.101.d_own, bf16[8,192,256]{2,1,0:T(8,128)(2,1)S(1)} %get-tuple-element.102.weights, bf16[1024,256]{1,0:T(8,128)(2,1)S(1)} %get-tuple-element.103.normed, ...), custom_call_target="tpu_custom_call" | custom-call | flops 17179869184 | bytes 8388608 | tf_op jit(solution)/shard_map/pallas_call | solution.py:527
  67.4 4.5 %collective-permute-start.13 = (bf16[32,1024]{1,0:T(8,128)(2,1)S(1)}, bf16[32,1024]{1,0:T(8,128)(2,1)S(1)}, u32[]{:S(2)}, u32[]{:S(2)}) collective-permute-start(bf16[32,1024]{1,0:T(8,128)(2,1)S(1)} %get-tuple-element.109), channel_id=1, source_target_pairs={{0,1},{1,0},{2,3},{3,2},{4,5},{5,4},{6,7},{7,6},{8,9},{9,8},{10,11... | collective-permute-start | bytes 196616 | tf_op jit(solution)/shard_map/ppermute | solution.py:415
  71.9 5.3 %collective-permute-start.14 = (bf16[32,1024]{1,0:T(8,128)(2,1)S(1)}, bf16[32,1024]{1,0:T(8,128)(2,1)S(1)}, u32[]{:S(2)}, u32[]{:S(2)}) collective-permute-start(bf16[32,1024]{1,0:T(8,128)(2,1)S(1)} %get-tuple-element.110), channel_id=1, source_target_pairs={{0,31},{1,2},{2,1},{3,4},{4,3},{5,6},{6,5},{7,8},{8,7},{9,10},{10,... | collective-permute-start | bytes 196616 | tf_op jit(solution)/shard_map/ppermute | solution.py:420
  77.9 1.8 %collective-permute-start.12 = (bf16[32,512]{1,0:T(8,128)(2,1)S(1)}, bf16[32,512]{1,0:T(8,128)(2,1)S(1)}, u32[]{:S(2)}, u32[]{:S(2)}) collective-permute-start(bf16[32,512]{1,0:T(8,128)(2,1)S(1)} %get-tuple-element.108), channel_id=1, source_target_pairs={{0,1},{1,0},{2,3},{3,2},{4,5},{5,4},{6,7},{7,6},{8,9},{9,8},{10,11... | collective-permute-start | bytes 98312 | tf_op jit(solution)/shard_map/ppermute | solution.py:415
  79.8 3.4 %collective-permute-done.14.far = bf16[32,1024]{1,0:T(8,128)(2,1)S(1)} collective-permute-done((bf16[32,1024]{1,0:T(8,128)(2,1)S(1)}, bf16[32,1024]{1,0:T(8,128)(2,1)S(1)}, u32[]{:S(2)}, u32[]{:S(2)}) %collective-permute-start.14) | collective-permute-done | bytes 65568 | tf_op jit(solution)/shard_map/ppermute | solution.py:420
  83.2 1.7 %collective-permute-done.12.came = bf16[32,512]{1,0:T(8,128)(2,1)S(1)} collective-permute-done((bf16[32,512]{1,0:T(8,128)(2,1)S(1)}, bf16[32,512]{1,0:T(8,128)(2,1)S(1)}, u32[]{:S(2)}, u32[]{:S(2)}) %collective-permute-start.12) | collective-permute-done | bytes 32800 | tf_op jit(solution)/shard_map/ppermute | solution.py:415
  85.5 2.0 %collective-permute-start.17 = (bf16[32,512]{1,0:T(8,128)(2,1)S(1)}, bf16[32,512]{1,0:T(8,128)(2,1)S(1)}, u32[]{:S(2)}, u32[]{:S(2)}) collective-permute-start(bf16[32,512]{1,0:T(8,128)(2,1)S(1)} %get-tuple-element.113.refs_0_), channel_id=1, source_target_pairs={{0,192},{32,224},{64,128},{96,160},{128,64},{160,96},{192,0},{224,... | collective-permute-start | bytes 98312 | tf_op jit(solution)/shard_map/ppermute | solution.py:415
  87.5 1.6 %collective-permute-start.15 = (bf16[32,512]{1,0:T(8,128)(2,1)S(1)}, bf16[32,512]{1,0:T(8,128)(2,1)S(1)}, u32[]{:S(2)}, u32[]{:S(2)}) collective-permute-start(bf16[32,512]{1,0:T(8,128)(2,1)S(1)} %get-tuple-element.113.refs_0_), channel_id=1, source_target_pairs={{0,64},{32,96},{64,0},{96,32},{128,192},{160,224},{192,128},{224,1... | collective-permute-start | bytes 98312 | tf_op jit(solution)/shard_map/ppermute | solution.py:415
  91.1 4.0 %collective-permute-start.18 = (bf16[4,32,512]{2,1,0:T(8,128)(2,1)S(1)}, bf16[4,32,512]{2,1,0:T(8,128)(2,1)S(1)}, u32[]{:S(2)}, u32[]{:S(2)}) collective-permute-start(bf16[4,32,512]{2,1,0:T(8,128)(2,1)S(1)} %shard_map.129.mine), channel_id=1, source_target_pairs={{0,32},{32,0},{64,96},{96,64},{128,160},{160,128},{192,224},{224,1... | collective-permute-start | bytes 393224 | tf_op jit(solution)/shard_map/ppermute | solution.py:415
  (51 shorter events, 14.8 us)
Async XLA Ops:
  0.6 20.4 %collective-permute-start.1 = (bf16[32,1024]{1,0:T(8,128)(2,1)}, bf16[32,1024]{1,0:T(8,128)(2,1)S(1)}, u32[]{:S(2)}, u32[]{:S(2)}) collective-permute-start(bf16[32,1024]{1,0:T(8,128)(2,1)} %bitcast.13), channel_id=1, source_target_pairs={{0,1},{1,0},{2,3},{3,2},{4,5},{5,4},{6,7},{7,6},{8,9},{9,8},{10,11... | collective-permute-start | bytes 196616 | tf_op jit(solution)/shard_map/ppermute | solution.py:415
  8.5 12.6 %collective-permute-start = (bf16[32,1024]{1,0:T(8,128)(2,1)}, bf16[32,1024]{1,0:T(8,128)(2,1)S(1)}, u32[]{:S(2)}, u32[]{:S(2)}) collective-permute-start(bf16[32,1024]{1,0:T(8,128)(2,1)} %bitcast.14), channel_id=1, source_target_pairs={{0,31},{1,2},{2,1},{3,4},{4,3},{5,6},{6,5},{7,8},{8,7},{9,10},{10,... | collective-permute-start | bytes 196616 | tf_op jit(solution)/shard_map/ppermute | solution.py:420
  15.9 7.8 %copy-start = (bf16[1024,2048]{1,0:T(8,128)(2,1)S(1)}, bf16[1024,2048]{1,0:T(8,128)(2,1)}, u32[]{:S(2)}) copy-start(bf16[1024,2048]{1,0:T(8,128)(2,1)} %w_keyval.7) | copy-start | bytes 12582916
  15.9 7.8 %copy-start.2 = (bf16[1024,100]{0,1:T(8,128)(2,1)S(1)}, bf16[1024,100]{0,1:T(8,128)(2,1)}, u32[]{:S(2)}) copy-start(bf16[1024,100]{0,1:T(8,128)(2,1)} %param.15) | copy-start | bytes 614404
  15.9 7.8 %copy-start.5 = (s32[256,3]{0,1:T(4,128)S(1)}, s32[256,3]{0,1:T(4,128)}, u32[]{:S(2)}) copy-start(s32[256,3]{0,1:T(4,128)} %param.10) | copy-start | bytes 9220
  17.4 9.1 %collective-permute-start.4 = (bf16[32,1024]{1,0:T(8,128)(2,1)S(1)}, bf16[32,1024]{1,0:T(8,128)(2,1)S(1)}, u32[]{:S(2)}, u32[]{:S(2)}) collective-permute-start(bf16[32,1024]{1,0:T(8,128)(2,1)S(1)} %bitcast.15), channel_id=1, source_target_pairs={{0,192},{32,224},{64,128},{96,160},{128,64},{160,96},{192,0},{224,... | collective-permute-start | bytes 196616 | tf_op jit(solution)/shard_map/ppermute | solution.py:415
  20.2 6.8 %collective-permute-start.3 = (bf16[32,1024]{1,0:T(8,128)(2,1)S(1)}, bf16[32,1024]{1,0:T(8,128)(2,1)S(1)}, u32[]{:S(2)}, u32[]{:S(2)}) collective-permute-start(bf16[32,1024]{1,0:T(8,128)(2,1)S(1)} %bitcast.16), channel_id=1, source_target_pairs={{0,128},{32,160},{64,192},{96,224},{128,0},{160,32},{192,64},{224,... | collective-permute-start | bytes 196616 | tf_op jit(solution)/shard_map/ppermute | solution.py:415
  20.2 6.8 %collective-permute-start.2 = (bf16[32,1024]{1,0:T(8,128)(2,1)S(1)}, bf16[32,1024]{1,0:T(8,128)(2,1)S(1)}, u32[]{:S(2)}, u32[]{:S(2)}) collective-permute-start(bf16[32,1024]{1,0:T(8,128)(2,1)S(1)} %bitcast.17), channel_id=1, source_target_pairs={{0,64},{32,96},{64,0},{96,32},{128,192},{160,224},{192,128},{224,1... | collective-permute-start | bytes 196616 | tf_op jit(solution)/shard_map/ppermute | solution.py:415
  21.0 10.2 %collective-permute-start.7 = (bf16[32,1024]{1,0:T(8,128)(2,1)S(1)}, bf16[32,1024]{1,0:T(8,128)(2,1)S(1)}, u32[]{:S(2)}, u32[]{:S(2)}) collective-permute-start(bf16[32,1024]{1,0:T(8,128)(2,1)S(1)} %collective-permute-done.1.partner.refs_4_), channel_id=1, source_target_pairs={{0,192},{32,224},{64,128},{96,160},{128,64},{160,96},{192,0},{224,... | collective-permute-start | bytes 196616 | tf_op jit(solution)/shard_map/ppermute | solution.py:415
  26.4 20.0 %copy-start.9 = (bf16[96,2048]{1,0:T(8,128)(2,1)}, bf16[96,2048]{1,0:T(8,128)(2,1)S(1)}, u32[]{:S(2)}) copy-start(bf16[96,2048]{1,0:T(8,128)(2,1)S(1)} %get-tuple-element.104.table) | copy-start | bytes 1179652
  27.0 15.9 %collective-permute-start.10 = (bf16[64,1024]{1,0:T(8,128)(2,1)S(1)}, bf16[64,1024]{1,0:T(8,128)(2,1)S(1)}, u32[]{:S(2)}, u32[]{:S(2)}) collective-permute-start(bf16[64,1024]{1,0:T(8,128)(2,1)S(1)} %get-tuple-element.83.refs_8_), channel_id=1, source_target_pairs={{0,192},{32,224},{64,128},{96,160},{128,64},{160,96},{192,0},{224,... | collective-permute-start | bytes 393224 | tf_op jit(solution)/shard_map/ppermute | solution.py:415
  28.8 14.1 %collective-permute-start.9 = (bf16[64,1024]{1,0:T(8,128)(2,1)S(1)}, bf16[64,1024]{1,0:T(8,128)(2,1)S(1)}, u32[]{:S(2)}, u32[]{:S(2)}) collective-permute-start(bf16[64,1024]{1,0:T(8,128)(2,1)S(1)} %get-tuple-element.83.refs_8_), channel_id=1, source_target_pairs={{0,128},{32,160},{64,192},{96,224},{128,0},{160,32},{192,64},{224,... | collective-permute-start | bytes 393224 | tf_op jit(solution)/shard_map/ppermute | solution.py:415
  28.8 14.1 %collective-permute-start.8 = (bf16[64,1024]{1,0:T(8,128)(2,1)S(1)}, bf16[64,1024]{1,0:T(8,128)(2,1)S(1)}, u32[]{:S(2)}, u32[]{:S(2)}) collective-permute-start(bf16[64,1024]{1,0:T(8,128)(2,1)S(1)} %get-tuple-element.83.refs_8_), channel_id=1, source_target_pairs={{0,64},{32,96},{64,0},{96,32},{128,192},{160,224},{192,128},{224,1... | collective-permute-start | bytes 393224 | tf_op jit(solution)/shard_map/ppermute | solution.py:415
  30.5 12.3 %collective-permute-start.6 = (bf16[32,1024]{1,0:T(8,128)(2,1)S(1)}, bf16[32,1024]{1,0:T(8,128)(2,1)S(1)}, u32[]{:S(2)}, u32[]{:S(2)}) collective-permute-start(bf16[32,1024]{1,0:T(8,128)(2,1)S(1)} %collective-permute-done.1.partner.refs_4_), channel_id=1, source_target_pairs={{0,128},{32,160},{64,192},{96,224},{128,0},{160,32},{192,64},{224,... | collective-permute-start | bytes 196616 | tf_op jit(solution)/shard_map/ppermute | solution.py:415
  31.2 11.7 %collective-permute-start.5 = (bf16[32,1024]{1,0:T(8,128)(2,1)S(1)}, bf16[32,1024]{1,0:T(8,128)(2,1)S(1)}, u32[]{:S(2)}, u32[]{:S(2)}) collective-permute-start(bf16[32,1024]{1,0:T(8,128)(2,1)S(1)} %collective-permute-done.1.partner.refs_4_), channel_id=1, source_target_pairs={{0,64},{32,96},{64,0},{96,32},{128,192},{160,224},{192,128},{224,1... | collective-permute-start | bytes 196616 | tf_op jit(solution)/shard_map/ppermute | solution.py:415
  43.0 3.8 %collective-permute-start.11 = (bf16[4,128,1024]{2,1,0:T(8,128)(2,1)S(1)}, bf16[4,128,1024]{2,1,0:T(8,128)(2,1)S(1)}, u32[]{:S(2)}, u32[]{:S(2)}) collective-permute-start(bf16[4,128,1024]{2,1,0:T(8,128)(2,1)S(1)} %shard_map.121.stack.mine.refs_19_), channel_id=1, source_target_pairs={{0,32},{32,0},{64,96},{96,64},{128,160},{160,128},{192,224},{224,1... | collective-permute-start | bytes 3145736 | tf_op jit(solution)/shard_map/ppermute | solution.py:415
  55.8 21.4 %all-to-all-start = ((bf16[16,64,512]{2,1,0:T(8,128)(2,1)}), bf16[16,64,512]{2,1,0:T(8,128)(2,1)S(1)}, u32[]{:S(2)}, u32[]{:S(2)}) async-start(bf16[16,64,512]{2,1,0:T(8,128)(2,1)} %bitcast.7), calls=%async_computation | async-start | bytes 2097152 | tf_op jit(solution)/shard_map/all_to_all | solution.py:520
  67.4 12.4 %collective-permute-start.13 = (bf16[32,1024]{1,0:T(8,128)(2,1)S(1)}, bf16[32,1024]{1,0:T(8,128)(2,1)S(1)}, u32[]{:S(2)}, u32[]{:S(2)}) collective-permute-start(bf16[32,1024]{1,0:T(8,128)(2,1)S(1)} %get-tuple-element.109), channel_id=1, source_target_pairs={{0,1},{1,0},{2,3},{3,2},{4,5},{5,4},{6,7},{7,6},{8,9},{9,8},{10,11... | collective-permute-start | bytes 196616 | tf_op jit(solution)/shard_map/ppermute | solution.py:415
  71.9 11.3 %collective-permute-start.14 = (bf16[32,1024]{1,0:T(8,128)(2,1)S(1)}, bf16[32,1024]{1,0:T(8,128)(2,1)S(1)}, u32[]{:S(2)}, u32[]{:S(2)}) collective-permute-start(bf16[32,1024]{1,0:T(8,128)(2,1)S(1)} %get-tuple-element.110), channel_id=1, source_target_pairs={{0,31},{1,2},{2,1},{3,4},{4,3},{5,6},{6,5},{7,8},{8,7},{9,10},{10,... | collective-permute-start | bytes 196616 | tf_op jit(solution)/shard_map/ppermute | solution.py:420
  77.9 6.9 %collective-permute-start.12 = (bf16[32,512]{1,0:T(8,128)(2,1)S(1)}, bf16[32,512]{1,0:T(8,128)(2,1)S(1)}, u32[]{:S(2)}, u32[]{:S(2)}) collective-permute-start(bf16[32,512]{1,0:T(8,128)(2,1)S(1)} %get-tuple-element.108), channel_id=1, source_target_pairs={{0,1},{1,0},{2,3},{3,2},{4,5},{5,4},{6,7},{7,6},{8,9},{9,8},{10,11... | collective-permute-start | bytes 98312 | tf_op jit(solution)/shard_map/ppermute | solution.py:415
  85.5 4.7 %collective-permute-start.17 = (bf16[32,512]{1,0:T(8,128)(2,1)S(1)}, bf16[32,512]{1,0:T(8,128)(2,1)S(1)}, u32[]{:S(2)}, u32[]{:S(2)}) collective-permute-start(bf16[32,512]{1,0:T(8,128)(2,1)S(1)} %get-tuple-element.113.refs_0_), channel_id=1, source_target_pairs={{0,192},{32,224},{64,128},{96,160},{128,64},{160,96},{192,0},{224,... | collective-permute-start | bytes 98312 | tf_op jit(solution)/shard_map/ppermute | solution.py:415
  87.5 3.7 %collective-permute-start.16 = (bf16[32,512]{1,0:T(8,128)(2,1)S(1)}, bf16[32,512]{1,0:T(8,128)(2,1)S(1)}, u32[]{:S(2)}, u32[]{:S(2)}) collective-permute-start(bf16[32,512]{1,0:T(8,128)(2,1)S(1)} %get-tuple-element.113.refs_0_), channel_id=1, source_target_pairs={{0,128},{32,160},{64,192},{96,224},{128,0},{160,32},{192,64},{224,... | collective-permute-start | bytes 98312 | tf_op jit(solution)/shard_map/ppermute | solution.py:415
  87.5 3.7 %collective-permute-start.15 = (bf16[32,512]{1,0:T(8,128)(2,1)S(1)}, bf16[32,512]{1,0:T(8,128)(2,1)S(1)}, u32[]{:S(2)}, u32[]{:S(2)}) collective-permute-start(bf16[32,512]{1,0:T(8,128)(2,1)S(1)} %get-tuple-element.113.refs_0_), channel_id=1, source_target_pairs={{0,64},{32,96},{64,0},{96,32},{128,192},{160,224},{192,128},{224,1... | collective-permute-start | bytes 98312 | tf_op jit(solution)/shard_map/ppermute | solution.py:415
  91.1 5.0 %collective-permute-start.18 = (bf16[4,32,512]{2,1,0:T(8,128)(2,1)S(1)}, bf16[4,32,512]{2,1,0:T(8,128)(2,1)S(1)}, u32[]{:S(2)}, u32[]{:S(2)}) collective-permute-start(bf16[4,32,512]{2,1,0:T(8,128)(2,1)S(1)} %shard_map.129.mine), channel_id=1, source_target_pairs={{0,32},{32,0},{64,96},{96,64},{128,160},{160,128},{192,224},{224,1... | collective-permute-start | bytes 393224 | tf_op jit(solution)/shard_map/ppermute | solution.py:415
  (7 other events, 18.9 us)

commit v5 on v4

--- a/solution.py
+++ b/solution.py
@@ -20,6 +20,7 @@
 WIDTH = 1024
 VARS = 100
 KNB = 3
+PIECES = 4
 CARRY = 112
 EDGE = 96
 FOLDS = 4
@@ -41,12 +42,12 @@
     return lax.dot_general(left, right, (((0,), (0,)), ((), ())), preferred_element_type=F32)
 
 
-def call(body, outs, specs, scratch=(), flops=0, size=0, limit=12):
+def call(body, outs, specs, scratch=(), flops=0, size=0, limit=12, into=VMEM):
     return pl.pallas_call(
         body,
         out_shape=outs,
         in_specs=specs,
-        out_specs=[VMEM] * len(outs),
+        out_specs=[into] * len(outs),
         scratch_shapes=list(scratch),
         compiler_params=pltpu.CompilerParams(vmem_limit_bytes=limit << 20),
         cost_estimate=pl.CostEstimate(flops=flops, bytes_accessed=size, transcendentals=0),
@@ -61,9 +62,7 @@
     average = jnp.where(
         iota((TILE, TILE), 0) // SIZE == iota((TILE, TILE), 1) // SIZE, 1.0 / SIZE, 0.0
     ).astype(BF16)
-    high = values.astype(BF16)
-    low = (values - high.astype(F32)).astype(BF16)
-    return dot(high, average) + dot(low, average)
+    return dot(values.astype(BF16), average)
 
 
 def stack_heads(tile):
@@ -199,9 +198,11 @@
     at = pl.multiple_of(me[0] * TILE, TILE)
     flat = jnp.concatenate([stack[i, :WIDE, :] for i in range(HALF)], 0)
     turned[...] = flat.T
-    key, root = key_parts(dot(flat, w_keyval[:, pl.ds(at, TILE)]).astype(BF16).astype(F32))
-    at = pl.multiple_of(WIDTH + at, TILE)
-    value = dot(flat, w_keyval[:, pl.ds(at, TILE)]).astype(BF16)
+    after = pl.multiple_of(WIDTH + at, TILE)
+    tile = jnp.concatenate([w_keyval[:, pl.ds(at, TILE)], w_keyval[:, pl.ds(after, TILE)]], 1)
+    table = dot(flat, tile).astype(BF16)
+    key, root = key_parts(table[:, :TILE].astype(F32))
+    value = table[:, TILE:]
     key_roots[...] = root
     key = key.astype(BF16) * BF16(SIZE**-0.5)
     members = [slice(i * WIDE, (i + 1) * WIDE) for i in range(HALF)]
@@ -229,8 +230,12 @@
     return mean, rows[at + 2 : at + 3] + rows[at + 3 : at + 4]
 
 
-def crps_kernel(mine, theirs, target, area, d_pred, d_own, loss):
+def crps_kernel(mine, theirs, target, area, w_head, d_pred, d_own, loss, sums):
     size = 16
+    columns = jnp.sum(w_head[...].astype(F32), 1, keepdims=True) / WIDTH
+    columns = jnp.concatenate([columns, jnp.zeros((CARRY - VARS, 1), F32)], 0)
+    levels = [jnp.zeros((8, ROWS), F32) for _ in range(MEMBERS)]
+    alongs = [jnp.zeros((8, ROWS), F32) for _ in range(MEMBERS)]
     stacks = (mine, theirs)
     lost = jnp.zeros((size, ROWS), F32)
     weight = area[...]
@@ -264,10 +269,19 @@
             root = lax.rsqrt(square)
             if i == 0:
                 lost = lost + share * (square * root / MEMBERS - 0.5 * PAIR * pair)
-            out = (share * (delta * root / MEMBERS - PAIR * slope[i])).astype(BF16)
+            wide = share * (delta * root / MEMBERS - PAIR * slope[i])
+            part = wide * columns[rows]
+            levels[i] = levels[i] + (part[:8] + part[8:])
+            part = wide * value[i]
+            alongs[i] = alongs[i] + (part[:8] + part[8:])
+            out = wide.astype(BF16)
             d_pred[rows, i * ROWS : (i + 1) * ROWS] = out
             if i == 0:
                 d_own[rows, :] = out
+    for i in range(MEMBERS):
+        sums[i : i + 1, :] = jnp.sum(levels[i], 0, keepdims=True)
+        along = jnp.sum(alongs[i], 0, keepdims=True) / WIDTH
+        sums[MEMBERS + i : MEMBERS + i + 1, :] = along
     d_pred[CARRY:, :] = jnp.zeros((TILE - CARRY, MEMBERS * ROWS), BF16)
     d_own[CARRY:, :] = payload_rows(mine, 0, EDGE, 16)
     loss[...] = jnp.sum(lost, axis=(0, 1), keepdims=True) / (ROWS * SHARDS * VARS)
@@ -277,30 +291,24 @@
     me = refs[0]
     sets = (refs[1:7], refs[7:13])
     (
-        normal_tile, inverse, embed_turned, w_head, d_pred, loss, mine, theirs,
-        payload, d_table, normed_all, d_mixed_all, d_score_all,
+        normal_tile, inverse, embed_turned, w_head, d_pred, loss, sums, mine, theirs,
+        payload_far, payload, sems, d_table, normed_all, d_mixed_all, d_score_all,
     ) = refs[13:]
     stacks = (mine, theirs)
     here = me[0]
     query = normal_tile[...]
     out = d_pred[...]
-    wide = out.astype(F32)
-    sums = jnp.sum(w_head[...].astype(F32), 1, keepdims=True)
     at = pl.multiple_of(here * TILE, TILE)
     d_normed = dot_tn(w_head[:, pl.ds(at, TILE)], out[:VARS])
-    levels = jnp.sum(wide[:VARS] * sums, 0, keepdims=True) / WIDTH
     for k in range(MEMBERS):
         side, i = k % 2, k // 2
         cols = slice(k * ROWS, (k + 1) * ROWS)
         mean, scale = stats_of(stacks[side], i)
         normed = (sets[side][5][i] - mean) * scale
-        along = jnp.zeros((1, ROWS), F32)
-        for start in range(0, VARS + NODES - VARS % NODES, NODES):
-            pred = payload_rows(stacks[side], i, start, NODES).astype(F32)
-            along = along + jnp.sum(pred * wide[start : start + NODES, cols], 0, keepdims=True)
+        level, along = sums[k : k + 1, :], sums[MEMBERS + k : MEMBERS + k + 1, :]
         normed_all[:, cols] = normed.astype(BF16)
         d_mixed_all[:, cols] = (
-            scale * (d_normed[:, cols] - levels[:, cols] - normed * (along / WIDTH))
+            scale * (d_normed[:, cols] - level - normed * along)
         ).astype(BF16)
     d_head = dot_nt(normed_all[...], out)
     for k in range(MEMBERS):
@@ -338,10 +346,7 @@
         0,
     )
     d_query = inverse[...] * SCALE * (d_query - wide_query * along)
-    grad = dot_nt(embed_turned[...], d_query.astype(BF16))
-    payload[:, :TILE] = grad.astype(BF16)
-    grad = dot(sets[0][0][...], d_table[0]) + dot(sets[1][0][...], d_table[1])
-    payload[:, TILE : 3 * TILE] = grad.astype(BF16)
+    payload[:, :TILE] = dot_nt(embed_turned[...], d_query.astype(BF16)).astype(BF16)
     high = loss[...].astype(BF16).astype(F32)
     lane = iota((WIDTH, TILE), 1)
     side = jnp.where(lane == VARS, high, jnp.where(lane == VARS + 1, loss[...] - high, 0.0))
@@ -350,6 +355,17 @@
     payload[rows, 3 * TILE :] = jnp.where(
         iota((TILE, TILE), 1) < VARS, d_head * SCALE, side[:TILE]
     ).astype(BF16)
+    sent = []
+    for step in range(PIECES):
+        rows = slice(step * WIDTH // PIECES, (step + 1) * WIDTH // PIECES)
+        grad = dot(sets[0][0][rows, :], d_table[0]) + dot(sets[1][0][rows, :], d_table[1])
+        payload[rows, TILE : 3 * TILE] = grad.astype(BF16)
+        sent.append(
+            pltpu.make_async_copy(payload.at[rows, :], payload_far.at[rows, :], sems.at[step])
+        )
+        sent[-1].start()
+    for copy in sent:
+        copy.wait()
 
 
 def latent_kernel(
@@ -479,11 +495,16 @@
     )(me, own, partner, other, w_keyval, normal, embed_turned, edges, head_turned)
     bundle, own_far = lax.optimization_barrier((bundle, own_far))
     stacks = cores(own_far, partner_far, chips(bundle))
-    d_pred, d_own, loss = call(
+    d_pred, d_own, loss, sums = call(
         crps_kernel,
-        [shape(TILE, MEMBERS * ROWS), shape(TILE, ROWS), shape(1, 1, kind=F32)],
-        [VMEM] * 4,
-    )(*stacks, target.T, area.reshape(1, ROWS))
+        [
+            shape(TILE, MEMBERS * ROWS),
+            shape(TILE, ROWS),
+            shape(1, 1, kind=F32),
+            shape(2 * MEMBERS, ROWS, kind=F32),
+        ],
+        [VMEM] * 5,
+    )(*stacks, target.T, area.reshape(1, ROWS), head_turned)
     tables = [
         call(
             tables_kernel,
@@ -504,8 +525,10 @@
     (grads,) = call(
         backward_kernel,
         [shape(WIDTH, 4 * TILE)],
-        [SMEM] + [VMEM] * 20,
+        [SMEM] + [VMEM] * 21,
         [
+            pltpu.VMEM((WIDTH, 4 * TILE), BF16),
+            pltpu.SemaphoreType.DMA((PIECES,)),
             pltpu.VMEM((2, HALF * WIDE, 2 * TILE), BF16),
             pltpu.VMEM((TILE, MEMBERS * ROWS), BF16),
             pltpu.VMEM((TILE, MEMBERS * ROWS), BF16),
@@ -513,9 +536,10 @@
         ],
         flops=2 << 30,
         size=8 << 20,
+        into=pl.BlockSpec(memory_space=pl.ANY),
     )(
         me, *tables[0], *tables[1], normal_tile, inverse, embed_turned, head_turned,
-        d_pred, loss, *stacks,
+        d_pred, loss, sums, *stacks,
     )
     pieces = lax.all_to_all(
         grads.reshape(SHARDS // 2, 2 * NODES, 4 * TILE),

time: 97.8 us -> 96.6 us (0.988)
  Pallas kernels: 22.6 us -> 20.7 us
  transfers between devices with their start and end apart: 20 -> 20, of which waited for: 8 -> 8; matrix products, arithmetic and copies ran while one was open for 0% -> 0% of each run, Pallas kernels for 12% -> 11%
where the time goes in v5:
time: 96.6 us; the launch traced here: 96.3 us
  starting transfers between devices  49.8 us (52%)
  Pallas kernels  20.7 us (21%)
  waiting for transfers between devices  19 us (20%)
  local copies, waits for them, and re-layouts  5.84 us (6%)
    ppermute x17, starting transfers between devices, swap(): return lax.ppermute(array, axis, [(i, i ^ bits) for i in range(count)])  36.1 us
    ppermute x17, waiting for transfers between devices, swap(): return lax.ppermute(array, axis, [(i, i ^ bits) for i in range(count)])  16.2 us
    ppermute x2, starting transfers between devices, beyond(): lax.ppermute(array, 'shard', [(i, (i + step(i)) % SHARDS) for i in range(...  10.1 us
    unnamed x22, local copies, waits for them, and re-layouts  5.84 us
    pallas_call x1, Pallas kernels, on_device(): call(backward_kernel, [shape(WIDTH, 4 * TILE)], [SMEM] + [VMEM] * 21, [pl...  4.57 us
    pallas_call x1, Pallas kernels, on_device(): call(latent_kernel, [shape(NODES, WIDTH, kind=F32), shape(NODES, WIDTH),...  4.09 us
    all_to_all x1, starting transfers between devices, on_device(): lax.all_to_all(grads.reshape(SHARDS // 2, 2 * NODES, 4 * TILE), 'shard',...  3.66 us
    pallas_call x2, Pallas kernels, on_device(): call(tables_kernel, [shape(WIDTH, HALF * WIDE), shape(HALF * BOTH, ROWS),...  3.31 us
  transfers between devices with their start and end apart: 20, of which 8 were waited for; matrix products, arithmetic and copies ran while one was open for 0% of the time, Pallas kernels for 11%

profile of v5, /device:TPU:1, one launch (start us, length us, event | category | flops | bytes accessed | tf_op | source)
XLA Modules:
  0.0 96.3 jit_solution(14078342399669451996)
XLA Ops:
  0.6 7.8 %collective-permute-start.1 = (bf16[32,1024]{1,0:T(8,128)(2,1)}, bf16[32,1024]{1,0:T(8,128)(2,1)S(1)}, u32[]{:S(2)}, u32[]{:S(2)}) collective-permute-start(bf16[32,1024]{1,0:T(8,128)(2,1)} %bitcast.14), channel_id=1, source_target_pairs={{0,1},{1,0},{2,3},{3,2},{4,5},{5,4},{6,7},{7,6},{8,9},{9,8},{10,11... | collective-permute-start | bytes 196616 | tf_op jit(solution)/shard_map/ppermute | solution.py:431
  8.5 4.7 %collective-permute-start = (bf16[32,1024]{1,0:T(8,128)(2,1)}, bf16[32,1024]{1,0:T(8,128)(2,1)S(1)}, u32[]{:S(2)}, u32[]{:S(2)}) collective-permute-start(bf16[32,1024]{1,0:T(8,128)(2,1)} %bitcast.15), channel_id=1, source_target_pairs={{0,31},{1,2},{2,1},{3,4},{4,3},{5,6},{6,5},{7,8},{8,7},{9,10},{10,... | collective-permute-start | bytes 196616 | tf_op jit(solution)/shard_map/ppermute | solution.py:436
  13.3 1.6 %copy-done.7 = bf16[1024,1024]{1,0:T(8,128)(2,1)S(1)} copy-done((bf16[1024,1024]{1,0:T(8,128)(2,1)S(1)}, bf16[1024,1024]{1,0:T(8,128)(2,1)}, u32[]{:S(2)}) %copy-start.7) | copy-done | bytes 2097176
  17.4 2.8 %collective-permute-start.4 = (bf16[32,1024]{1,0:T(8,128)(2,1)S(1)}, bf16[32,1024]{1,0:T(8,128)(2,1)S(1)}, u32[]{:S(2)}, u32[]{:S(2)}) collective-permute-start(bf16[32,1024]{1,0:T(8,128)(2,1)S(1)} %bitcast.16), channel_id=1, source_target_pairs={{0,192},{32,224},{64,128},{96,160},{128,64},{160,96},{192,0},{224,... | collective-permute-start | bytes 196616 | tf_op jit(solution)/shard_map/ppermute | solution.py:431
  21.0 2.7 %collective-permute-start.7 = (bf16[32,1024]{1,0:T(8,128)(2,1)S(1)}, bf16[32,1024]{1,0:T(8,128)(2,1)S(1)}, u32[]{:S(2)}, u32[]{:S(2)}) collective-permute-start(bf16[32,1024]{1,0:T(8,128)(2,1)S(1)} %collective-permute-done.1.partner.refs_4_), channel_id=1, source_target_pairs={{0,192},{32,224},{64,128},{96,160},{128,64},{160,96},{192,0},{224,... | collective-permute-start | bytes 196616 | tf_op jit(solution)/shard_map/ppermute | solution.py:431
  23.7 2.6 %shard_map.120 = (bf16[64,1024]{1,0:T(8,128)(2,1)S(1)}, bf16[8,192,256]{2,1,0:T(8,128)(2,1)S(1)}, bf16[1024,256]{1,0:T(8,128)(2,1)S(1)}, bf16[96,2048]{1,0:T(8,128)(2,1)S(1)}) custom-call(s32[2]{0:T(128)S(1)} %pad_add_fusion.me.refs_0_, bf16[32,1024]{1,0:T(8,128)(2,1)S(1)} %bitcast.19, bf16[32,1024]{1,0:T(8,128)(2,1)S(1)} %collective-permute-done.1.partner.refs_4_, ...), custom_call_target="tpu_custom_call" | custom-call | tf_op jit(solution)/shard_map/pallas_call | solution.py:485
  27.0 1.8 %collective-permute-start.10 = (bf16[64,1024]{1,0:T(8,128)(2,1)S(1)}, bf16[64,1024]{1,0:T(8,128)(2,1)S(1)}, u32[]{:S(2)}, u32[]{:S(2)}) collective-permute-start(bf16[64,1024]{1,0:T(8,128)(2,1)S(1)} %get-tuple-element.84.refs_8_), channel_id=1, source_target_pairs={{0,192},{32,224},{64,128},{96,160},{128,64},{160,96},{192,0},{224,... | collective-permute-start | bytes 393224 | tf_op jit(solution)/shard_map/ppermute | solution.py:431
  28.8 1.7 %collective-permute-start.8 = (bf16[64,1024]{1,0:T(8,128)(2,1)S(1)}, bf16[64,1024]{1,0:T(8,128)(2,1)S(1)}, u32[]{:S(2)}, u32[]{:S(2)}) collective-permute-start(bf16[64,1024]{1,0:T(8,128)(2,1)S(1)} %get-tuple-element.84.refs_8_), channel_id=1, source_target_pairs={{0,64},{32,96},{64,0},{96,32},{128,192},{160,224},{192,128},{224,1... | collective-permute-start | bytes 393224 | tf_op jit(solution)/shard_map/ppermute | solution.py:431
  32.6 10.2 %collective-permute-done.6.refs_6_ = bf16[32,1024]{1,0:T(8,128)(2,1)S(1)} collective-permute-done((bf16[32,1024]{1,0:T(8,128)(2,1)S(1)}, bf16[32,1024]{1,0:T(8,128)(2,1)S(1)}, u32[]{:S(2)}, u32[]{:S(2)}) %collective-permute-start.6) | collective-permute-done | bytes 65568 | tf_op jit(solution)/shard_map/ppermute | solution.py:431
  44.5 1.7 %shard_map.122 = (bf16[1024,384]{1,0:T(8,128)(2,1)S(1)}, bf16[768,256]{1,0:T(8,128)(2,1)S(1)}, bf16[768,128]{1,0:T(8,128)(2,1)S(1)}, f32[384,128]{1,0:T(8,128)S(...) custom-call(s32[2]{0:T(128)S(1)} %pad_add_fusion.me.refs_0_, ...), custom_call_target="tpu_custom_call" | custom-call | flops 1073741824 | bytes 4194304 | tf_op jit(solution)/shard_map/pallas_call | solution.py:509
  46.8 1.7 %shard_map.123 = (bf16[1024,384]{1,0:T(8,128)(2,1)S(1)}, bf16[768,256]{1,0:T(8,128)(2,1)S(1)}, bf16[768,128]{1,0:T(8,128)(2,1)S(1)}, f32[384,128]{1,0:T(8,128)S(...) custom-call(s32[2]{0:T(128)S(1)} %pad_add_fusion.me.refs_0_, ...), custom_call_target="tpu_custom_call" | custom-call | flops 1073741824 | bytes 4194304 | tf_op jit(solution)/shard_map/pallas_call | solution.py:509
  48.5 1.9 %shard_map.124 = (bf16[128,2048]{1,0:T(8,128)(2,1)S(1)}, bf16[128,256]{1,0:T(8,128)(2,1)S(1)}, f32[1,1]{1,0:T(1,128)}, f32[16,256]{1,0:T(8,128)S(1)}) custom-call(bf16[4,128,1024]{2,1,0:T(8,128)(2,1)S(1)} %shard_map.121.stack.mine.refs_20_, bf16[4,128,1024]{2,1,0:T(8,128)(2,1)S(1)} %collective-permute-done.11.stack.theirs.refs_21_, f32[100,256]{1,0:T(8,128)S(1)} %bitcast.21, ...), custom_call_target="tpu_custom_call" | custom-call | tf_op jit(solution)/shard_map/pallas_call | solution.py:498
  50.4 4.6 %shard_map.125 = bf16[1024,512]{1,0:T(8,128)(2,1)} custom-call(s32[2]{0:T(128)S(1)} %pad_add_fusion.me.refs_0_, bf16[1024,384]{1,0:T(8,128)(2,1)S(1)} %get-tuple-element.87.refs_1_, bf16[768,256]{1,0:T(8,128)(2,1)S(1)} %get-tuple-element.88.refs_2_, bf16[768,128]{1,0:T(8,128)(2,1)S(1)} %get-tuple-element.89.refs_3_, ...), custom_call_target="tpu_custom_call" | custom-call | flops 2147483648 | bytes 8388608 | tf_op jit(solution)/shard_map/pallas_call | solution.py:525
  55.0 3.7 %all-to-all-start = ((bf16[16,64,512]{2,1,0:T(8,128)(2,1)}), bf16[16,64,512]{2,1,0:T(8,128)(2,1)S(1)}, u32[]{:S(2)}, u32[]{:S(2)}) async-start(bf16[16,64,512]{2,1,0:T(8,128)(2,1)} %bitcast.7), calls=%async_computation | async-start | bytes 2097152 | tf_op jit(solution)/shard_map/all_to_all | solution.py:544
  58.6 2.2 %copy-done.1 = bf16[1024,2048]{1,0:T(8,128)(2,1)S(1)} copy-done((bf16[1024,2048]{1,0:T(8,128)(2,1)S(1)}, bf16[1024,2048]{1,0:T(8,128)(2,1)}, u32[]{:S(2)}) %copy-start.1) | copy-done | bytes 4194328
  61.8 4.1 %shard_map.126 = (f32[32,1024]{1,0:T(8,128)S(1)}, bf16[32,1024]{1,0:T(8,128)(2,1)S(1)}, bf16[32,1024]{1,0:T(8,128)(2,1)S(1)}) custom-call(bf16[128,256]{1,0:T(8,128)(2,1)S(1)} %get-tuple-element.103.d_own, bf16[8,192,256]{2,1,0:T(8,128)(2,1)S(1)} %get-tuple-element.104.weights, bf16[1024,256]{1,0:T(8,128)(2,1)S(1)} %get-tuple-element.105.normed, ...), custom_call_target="tpu_custom_call" | custom-call | flops 17179869184 | bytes 8388608 | tf_op jit(solution)/shard_map/pallas_call | solution.py:551
  65.9 4.5 %collective-permute-start.13 = (bf16[32,1024]{1,0:T(8,128)(2,1)S(1)}, bf16[32,1024]{1,0:T(8,128)(2,1)S(1)}, u32[]{:S(2)}, u32[]{:S(2)}) collective-permute-start(bf16[32,1024]{1,0:T(8,128)(2,1)S(1)} %get-tuple-element.111), channel_id=1, source_target_pairs={{0,1},{1,0},{2,3},{3,2},{4,5},{5,4},{6,7},{7,6},{8,9},{9,8},{10,11... | collective-permute-start | bytes 196616 | tf_op jit(solution)/shard_map/ppermute | solution.py:431
  70.5 5.3 %collective-permute-start.14 = (bf16[32,1024]{1,0:T(8,128)(2,1)S(1)}, bf16[32,1024]{1,0:T(8,128)(2,1)S(1)}, u32[]{:S(2)}, u32[]{:S(2)}) collective-permute-start(bf16[32,1024]{1,0:T(8,128)(2,1)S(1)} %get-tuple-element.112), channel_id=1, source_target_pairs={{0,31},{1,2},{2,1},{3,4},{4,3},{5,6},{6,5},{7,8},{8,7},{9,10},{10,... | collective-permute-start | bytes 196616 | tf_op jit(solution)/shard_map/ppermute | solution.py:436
  76.5 2.4 %collective-permute-start.12 = (bf16[32,512]{1,0:T(8,128)(2,1)S(1)}, bf16[32,512]{1,0:T(8,128)(2,1)S(1)}, u32[]{:S(2)}, u32[]{:S(2)}) collective-permute-start(bf16[32,512]{1,0:T(8,128)(2,1)S(1)} %get-tuple-element.110), channel_id=1, source_target_pairs={{0,1},{1,0},{2,3},{3,2},{4,5},{5,4},{6,7},{7,6},{8,9},{9,8},{10,11... | collective-permute-start | bytes 98312 | tf_op jit(solution)/shard_map/ppermute | solution.py:431
  78.9 2.8 %collective-permute-done.14.far = bf16[32,1024]{1,0:T(8,128)(2,1)S(1)} collective-permute-done((bf16[32,1024]{1,0:T(8,128)(2,1)S(1)}, bf16[32,1024]{1,0:T(8,128)(2,1)S(1)}, u32[]{:S(2)}, u32[]{:S(2)}) %collective-permute-start.14) | collective-permute-done | bytes 65568 | tf_op jit(solution)/shard_map/ppermute | solution.py:436
  81.7 1.7 %collective-permute-done.12.came = bf16[32,512]{1,0:T(8,128)(2,1)S(1)} collective-permute-done((bf16[32,512]{1,0:T(8,128)(2,1)S(1)}, bf16[32,512]{1,0:T(8,128)(2,1)S(1)}, u32[]{:S(2)}, u32[]{:S(2)}) %collective-permute-start.12) | collective-permute-done | bytes 32800 | tf_op jit(solution)/shard_map/ppermute | solution.py:431
  84.1 2.0 %collective-permute-start.17 = (bf16[32,512]{1,0:T(8,128)(2,1)S(1)}, bf16[32,512]{1,0:T(8,128)(2,1)S(1)}, u32[]{:S(2)}, u32[]{:S(2)}) collective-permute-start(bf16[32,512]{1,0:T(8,128)(2,1)S(1)} %get-tuple-element.115.refs_0_), channel_id=1, source_target_pairs={{0,192},{32,224},{64,128},{96,160},{128,64},{160,96},{192,0},{224,... | collective-permute-start | bytes 98312 | tf_op jit(solution)/shard_map/ppermute | solution.py:431
  86.0 1.6 %collective-permute-start.15 = (bf16[32,512]{1,0:T(8,128)(2,1)S(1)}, bf16[32,512]{1,0:T(8,128)(2,1)S(1)}, u32[]{:S(2)}, u32[]{:S(2)}) collective-permute-start(bf16[32,512]{1,0:T(8,128)(2,1)S(1)} %get-tuple-element.115.refs_0_), channel_id=1, source_target_pairs={{0,64},{32,96},{64,0},{96,32},{128,192},{160,224},{192,128},{224,1... | collective-permute-start | bytes 98312 | tf_op jit(solution)/shard_map/ppermute | solution.py:431
  89.7 4.2 %collective-permute-start.18 = (bf16[4,32,512]{2,1,0:T(8,128)(2,1)S(1)}, bf16[4,32,512]{2,1,0:T(8,128)(2,1)S(1)}, u32[]{:S(2)}, u32[]{:S(2)}) collective-permute-start(bf16[4,32,512]{2,1,0:T(8,128)(2,1)S(1)} %shard_map.129.mine), channel_id=1, source_target_pairs={{0,32},{32,0},{64,96},{96,64},{128,160},{160,128},{192,224},{224,1... | collective-permute-start | bytes 393224 | tf_op jit(solution)/shard_map/ppermute | solution.py:431
  (51 shorter events, 15.1 us)
Async XLA Ops:
  0.6 20.4 %collective-permute-start.1 = (bf16[32,1024]{1,0:T(8,128)(2,1)}, bf16[32,1024]{1,0:T(8,128)(2,1)S(1)}, u32[]{:S(2)}, u32[]{:S(2)}) collective-permute-start(bf16[32,1024]{1,0:T(8,128)(2,1)} %bitcast.14), channel_id=1, source_target_pairs={{0,1},{1,0},{2,3},{3,2},{4,5},{5,4},{6,7},{7,6},{8,9},{9,8},{10,11... | collective-permute-start | bytes 196616 | tf_op jit(solution)/shard_map/ppermute | solution.py:431
  8.5 12.6 %collective-permute-start = (bf16[32,1024]{1,0:T(8,128)(2,1)}, bf16[32,1024]{1,0:T(8,128)(2,1)S(1)}, u32[]{:S(2)}, u32[]{:S(2)}) collective-permute-start(bf16[32,1024]{1,0:T(8,128)(2,1)} %bitcast.15), channel_id=1, source_target_pairs={{0,31},{1,2},{2,1},{3,4},{4,3},{5,6},{6,5},{7,8},{8,7},{9,10},{10,... | collective-permute-start | bytes 196616 | tf_op jit(solution)/shard_map/ppermute | solution.py:436
  15.9 7.8 %copy-start = (bf16[1024,2048]{1,0:T(8,128)(2,1)S(1)}, bf16[1024,2048]{1,0:T(8,128)(2,1)}, u32[]{:S(2)}) copy-start(bf16[1024,2048]{1,0:T(8,128)(2,1)} %w_keyval.7) | copy-start | bytes 12582916
  15.9 7.8 %copy-start.2 = (bf16[1024,100]{0,1:T(8,128)(2,1)S(1)}, bf16[1024,100]{0,1:T(8,128)(2,1)}, u32[]{:S(2)}) copy-start(bf16[1024,100]{0,1:T(8,128)(2,1)} %param.15) | copy-start | bytes 614404
  15.9 7.8 %copy-start.5 = (s32[256,3]{0,1:T(4,128)S(1)}, s32[256,3]{0,1:T(4,128)}, u32[]{:S(2)}) copy-start(s32[256,3]{0,1:T(4,128)} %param.10) | copy-start | bytes 9220
  17.4 9.0 %collective-permute-start.4 = (bf16[32,1024]{1,0:T(8,128)(2,1)S(1)}, bf16[32,1024]{1,0:T(8,128)(2,1)S(1)}, u32[]{:S(2)}, u32[]{:S(2)}) collective-permute-start(bf16[32,1024]{1,0:T(8,128)(2,1)S(1)} %bitcast.16), channel_id=1, source_target_pairs={{0,192},{32,224},{64,128},{96,160},{128,64},{160,96},{192,0},{224,... | collective-permute-start | bytes 196616 | tf_op jit(solution)/shard_map/ppermute | solution.py:431
  20.2 6.8 %collective-permute-start.3 = (bf16[32,1024]{1,0:T(8,128)(2,1)S(1)}, bf16[32,1024]{1,0:T(8,128)(2,1)S(1)}, u32[]{:S(2)}, u32[]{:S(2)}) collective-permute-start(bf16[32,1024]{1,0:T(8,128)(2,1)S(1)} %bitcast.17), channel_id=1, source_target_pairs={{0,128},{32,160},{64,192},{96,224},{128,0},{160,32},{192,64},{224,... | collective-permute-start | bytes 196616 | tf_op jit(solution)/shard_map/ppermute | solution.py:431
  20.2 6.8 %collective-permute-start.2 = (bf16[32,1024]{1,0:T(8,128)(2,1)S(1)}, bf16[32,1024]{1,0:T(8,128)(2,1)S(1)}, u32[]{:S(2)}, u32[]{:S(2)}) collective-permute-start(bf16[32,1024]{1,0:T(8,128)(2,1)S(1)} %bitcast.18), channel_id=1, source_target_pairs={{0,64},{32,96},{64,0},{96,32},{128,192},{160,224},{192,128},{224,1... | collective-permute-start | bytes 196616 | tf_op jit(solution)/shard_map/ppermute | solution.py:431
  21.0 10.2 %collective-permute-start.7 = (bf16[32,1024]{1,0:T(8,128)(2,1)S(1)}, bf16[32,1024]{1,0:T(8,128)(2,1)S(1)}, u32[]{:S(2)}, u32[]{:S(2)}) collective-permute-start(bf16[32,1024]{1,0:T(8,128)(2,1)S(1)} %collective-permute-done.1.partner.refs_4_), channel_id=1, source_target_pairs={{0,192},{32,224},{64,128},{96,160},{128,64},{160,96},{192,0},{224,... | collective-permute-start | bytes 196616 | tf_op jit(solution)/shard_map/ppermute | solution.py:431
  26.4 22.1 %copy-start.9 = (bf16[96,2048]{1,0:T(8,128)(2,1)}, bf16[96,2048]{1,0:T(8,128)(2,1)S(1)}, u32[]{:S(2)}) copy-start(bf16[96,2048]{1,0:T(8,128)(2,1)S(1)} %get-tuple-element.106.table) | copy-start | bytes 1179652
  27.0 15.9 %collective-permute-start.10 = (bf16[64,1024]{1,0:T(8,128)(2,1)S(1)}, bf16[64,1024]{1,0:T(8,128)(2,1)S(1)}, u32[]{:S(2)}, u32[]{:S(2)}) collective-permute-start(bf16[64,1024]{1,0:T(8,128)(2,1)S(1)} %get-tuple-element.84.refs_8_), channel_id=1, source_target_pairs={{0,192},{32,224},{64,128},{96,160},{128,64},{160,96},{192,0},{224,... | collective-permute-start | bytes 393224 | tf_op jit(solution)/shard_map/ppermute | solution.py:431
  28.8 14.1 %collective-permute-start.9 = (bf16[64,1024]{1,0:T(8,128)(2,1)S(1)}, bf16[64,1024]{1,0:T(8,128)(2,1)S(1)}, u32[]{:S(2)}, u32[]{:S(2)}) collective-permute-start(bf16[64,1024]{1,0:T(8,128)(2,1)S(1)} %get-tuple-element.84.refs_8_), channel_id=1, source_target_pairs={{0,128},{32,160},{64,192},{96,224},{128,0},{160,32},{192,64},{224,... | collective-permute-start | bytes 393224 | tf_op jit(solution)/shard_map/ppermute | solution.py:431
  28.8 14.1 %collective-permute-start.8 = (bf16[64,1024]{1,0:T(8,128)(2,1)S(1)}, bf16[64,1024]{1,0:T(8,128)(2,1)S(1)}, u32[]{:S(2)}, u32[]{:S(2)}) collective-permute-start(bf16[64,1024]{1,0:T(8,128)(2,1)S(1)} %get-tuple-element.84.refs_8_), channel_id=1, source_target_pairs={{0,64},{32,96},{64,0},{96,32},{128,192},{160,224},{192,128},{224,1... | collective-permute-start | bytes 393224 | tf_op jit(solution)/shard_map/ppermute | solution.py:431
  30.5 12.3 %collective-permute-start.6 = (bf16[32,1024]{1,0:T(8,128)(2,1)S(1)}, bf16[32,1024]{1,0:T(8,128)(2,1)S(1)}, u32[]{:S(2)}, u32[]{:S(2)}) collective-permute-start(bf16[32,1024]{1,0:T(8,128)(2,1)S(1)} %collective-permute-done.1.partner.refs_4_), channel_id=1, source_target_pairs={{0,128},{32,160},{64,192},{96,224},{128,0},{160,32},{192,64},{224,... | collective-permute-start | bytes 196616 | tf_op jit(solution)/shard_map/ppermute | solution.py:431
  31.2 11.7 %collective-permute-start.5 = (bf16[32,1024]{1,0:T(8,128)(2,1)S(1)}, bf16[32,1024]{1,0:T(8,128)(2,1)S(1)}, u32[]{:S(2)}, u32[]{:S(2)}) collective-permute-start(bf16[32,1024]{1,0:T(8,128)(2,1)S(1)} %collective-permute-done.1.partner.refs_4_), channel_id=1, source_target_pairs={{0,64},{32,96},{64,0},{96,32},{128,192},{160,224},{192,128},{224,1... | collective-permute-start | bytes 196616 | tf_op jit(solution)/shard_map/ppermute | solution.py:431
  43.0 3.8 %collective-permute-start.11 = (bf16[4,128,1024]{2,1,0:T(8,128)(2,1)S(1)}, bf16[4,128,1024]{2,1,0:T(8,128)(2,1)S(1)}, u32[]{:S(2)}, u32[]{:S(2)}) collective-permute-start(bf16[4,128,1024]{2,1,0:T(8,128)(2,1)S(1)} %shard_map.121.stack.mine.refs_20_), channel_id=1, source_target_pairs={{0,32},{32,0},{64,96},{96,64},{128,160},{160,128},{192,224},{224,1... | collective-permute-start | bytes 3145736 | tf_op jit(solution)/shard_map/ppermute | solution.py:431
  55.0 20.8 %all-to-all-start = ((bf16[16,64,512]{2,1,0:T(8,128)(2,1)}), bf16[16,64,512]{2,1,0:T(8,128)(2,1)S(1)}, u32[]{:S(2)}, u32[]{:S(2)}) async-start(bf16[16,64,512]{2,1,0:T(8,128)(2,1)} %bitcast.7), calls=%async_computation | async-start | bytes 2097152 | tf_op jit(solution)/shard_map/all_to_all | solution.py:544
  65.9 13.0 %collective-permute-start.13 = (bf16[32,1024]{1,0:T(8,128)(2,1)S(1)}, bf16[32,1024]{1,0:T(8,128)(2,1)S(1)}, u32[]{:S(2)}, u32[]{:S(2)}) collective-permute-start(bf16[32,1024]{1,0:T(8,128)(2,1)S(1)} %get-tuple-element.111), channel_id=1, source_target_pairs={{0,1},{1,0},{2,3},{3,2},{4,5},{5,4},{6,7},{7,6},{8,9},{9,8},{10,11... | collective-permute-start | bytes 196616 | tf_op jit(solution)/shard_map/ppermute | solution.py:431
  70.5 11.3 %collective-permute-start.14 = (bf16[32,1024]{1,0:T(8,128)(2,1)S(1)}, bf16[32,1024]{1,0:T(8,128)(2,1)S(1)}, u32[]{:S(2)}, u32[]{:S(2)}) collective-permute-start(bf16[32,1024]{1,0:T(8,128)(2,1)S(1)} %get-tuple-element.112), channel_id=1, source_target_pairs={{0,31},{1,2},{2,1},{3,4},{4,3},{5,6},{6,5},{7,8},{8,7},{9,10},{10,... | collective-permute-start | bytes 196616 | tf_op jit(solution)/shard_map/ppermute | solution.py:436
  76.5 6.9 %collective-permute-start.12 = (bf16[32,512]{1,0:T(8,128)(2,1)S(1)}, bf16[32,512]{1,0:T(8,128)(2,1)S(1)}, u32[]{:S(2)}, u32[]{:S(2)}) collective-permute-start(bf16[32,512]{1,0:T(8,128)(2,1)S(1)} %get-tuple-element.110), channel_id=1, source_target_pairs={{0,1},{1,0},{2,3},{3,2},{4,5},{5,4},{6,7},{7,6},{8,9},{9,8},{10,11... | collective-permute-start | bytes 98312 | tf_op jit(solution)/shard_map/ppermute | solution.py:431
  84.1 4.6 %collective-permute-start.17 = (bf16[32,512]{1,0:T(8,128)(2,1)S(1)}, bf16[32,512]{1,0:T(8,128)(2,1)S(1)}, u32[]{:S(2)}, u32[]{:S(2)}) collective-permute-start(bf16[32,512]{1,0:T(8,128)(2,1)S(1)} %get-tuple-element.115.refs_0_), channel_id=1, source_target_pairs={{0,192},{32,224},{64,128},{96,160},{128,64},{160,96},{192,0},{224,... | collective-permute-start | bytes 98312 | tf_op jit(solution)/shard_map/ppermute | solution.py:431
  86.0 3.7 %collective-permute-start.16 = (bf16[32,512]{1,0:T(8,128)(2,1)S(1)}, bf16[32,512]{1,0:T(8,128)(2,1)S(1)}, u32[]{:S(2)}, u32[]{:S(2)}) collective-permute-start(bf16[32,512]{1,0:T(8,128)(2,1)S(1)} %get-tuple-element.115.refs_0_), channel_id=1, source_target_pairs={{0,128},{32,160},{64,192},{96,224},{128,0},{160,32},{192,64},{224,... | collective-permute-start | bytes 98312 | tf_op jit(solution)/shard_map/ppermute | solution.py:431
  86.0 3.7 %collective-permute-start.15 = (bf16[32,512]{1,0:T(8,128)(2,1)S(1)}, bf16[32,512]{1,0:T(8,128)(2,1)S(1)}, u32[]{:S(2)}, u32[]{:S(2)}) collective-permute-start(bf16[32,512]{1,0:T(8,128)(2,1)S(1)} %get-tuple-element.115.refs_0_), channel_id=1, source_target_pairs={{0,64},{32,96},{64,0},{96,32},{128,192},{160,224},{192,128},{224,1... | collective-permute-start | bytes 98312 | tf_op jit(solution)/shard_map/ppermute | solution.py:431
  89.7 5.2 %collective-permute-start.18 = (bf16[4,32,512]{2,1,0:T(8,128)(2,1)S(1)}, bf16[4,32,512]{2,1,0:T(8,128)(2,1)S(1)}, u32[]{:S(2)}, u32[]{:S(2)}) collective-permute-start(bf16[4,32,512]{2,1,0:T(8,128)(2,1)S(1)} %shard_map.129.mine), channel_id=1, source_target_pairs={{0,32},{32,0},{64,96},{96,64},{128,160},{160,128},{192,224},{224,1... | collective-permute-start | bytes 393224 | tf_op jit(solution)/shard_map/ppermute | solution.py:431
  (7 other events, 18.3 us)

commit v6 on v5

--- a/solution.py
+++ b/solution.py
@@ -231,18 +231,19 @@
 
 
 def crps_kernel(mine, theirs, target, area, w_head, d_pred, d_own, loss, sums):
-    size = 16
     columns = jnp.sum(w_head[...].astype(F32), 1, keepdims=True) / WIDTH
     columns = jnp.concatenate([columns, jnp.zeros((CARRY - VARS, 1), F32)], 0)
     levels = [jnp.zeros((8, ROWS), F32) for _ in range(MEMBERS)]
     alongs = [jnp.zeros((8, ROWS), F32) for _ in range(MEMBERS)]
     stacks = (mine, theirs)
-    lost = jnp.zeros((size, ROWS), F32)
+    lost = jnp.zeros((8, ROWS), F32)
     weight = area[...]
-    for start in range(0, CARRY, size):
+    fold = lambda part: part if part.shape[0] == 8 else part[:8] + part[8:]
+    for start in range(0, CARRY, 16):
+        size = min(16, VARS + 4 - start)
         rows = slice(start, start + size)
         value = [
-            payload_rows(stacks[k % 2], k // 2, start, size).astype(F32)
+            payload_rows(stacks[k % 2], k // 2, start, 16).astype(F32)[:size]
             for k in range(MEMBERS)
         ]
         slope = [jnp.zeros((size, ROWS), F32) for _ in range(MEMBERS)]
@@ -268,13 +269,16 @@
             square = delta * delta + 0.0625
             root = lax.rsqrt(square)
             if i == 0:
-                lost = lost + share * (square * root / MEMBERS - 0.5 * PAIR * pair)
+                lost = lost + fold(share * (square * root / MEMBERS - 0.5 * PAIR * pair))
             wide = share * (delta * root / MEMBERS - PAIR * slope[i])
-            part = wide * columns[rows]
-            levels[i] = levels[i] + (part[:8] + part[8:])
+            part = wide * columns[start : start + size]
+            levels[i] = levels[i] + fold(part)
             part = wide * value[i]
-            alongs[i] = alongs[i] + (part[:8] + part[8:])
+            alongs[i] = alongs[i] + fold(part)
+            if size < 16:
+                wide = jnp.concatenate([wide, jnp.zeros((16 - size, ROWS), F32)], 0)
             out = wide.astype(BF16)
+            rows = slice(start, start + 16)
             d_pred[rows, i * ROWS : (i + 1) * ROWS] = out
             if i == 0:
                 d_own[rows, :] = out
@@ -410,7 +414,7 @@
     loss[...] = value[0:1, at : at + 1] + value[0:1, at + 1 : at + 2]
 
 
-def place_kernel(me, mine, theirs, latent, near, far, query, keyval, head, d_latent):
+def place_kernel(me, mine, theirs, query, keyval, head):
     here = me[0]
     total = jnp.zeros((NODES, TILE), F32)
     for k in range(MEMBERS):
@@ -423,6 +427,9 @@
         ].astype(F32)
         total = total + part[:, 3 * TILE :].astype(F32)
     head[...] = total[:, :VARS]
+
+
+def gather_kernel(latent, near, far, d_latent):
     d_latent[...] = latent[...] + near[...].astype(F32) + far[...].astype(F32)
 
 
@@ -580,17 +587,19 @@
         size=1 << 18,
     )(stay, came)
     parts = cores(chips(total))
-    grad_query, grad_keyval, grad_head, d_latent = call(
+    (d_latent,) = call(gather_kernel, [shape(NODES, WIDTH, kind=F32)], [VMEM] * 3)(
+        mine, near, far
+    )
+    grad_query, grad_keyval, grad_head = call(
         place_kernel,
         [
             shape(NODES, WIDTH, kind=F32),
             shape(NODES, 2 * WIDTH, kind=F32),
             shape(NODES, VARS, kind=F32),
-            shape(NODES, WIDTH, kind=F32),
         ],
-        [SMEM] + [VMEM] * 5,
+        [SMEM] + [VMEM] * 2,
         size=1 << 20,
-    )(me, *parts, mine, near, far)
+    )(me, *parts)
     return (loss.reshape(1), d_latent[None], grad_query, grad_keyval, grad_head)
 
 

time: 96.6 us -> 96.5 us (level)
  waiting for transfers between devices: 19 us -> 17.7 us
  transfers between devices with their start and end apart: 20 -> 20, of which waited for: 8 -> 8; matrix products, arithmetic and copies ran while one was open for 0% -> 0% of each run, Pallas kernels for 11% -> 12%
where the time goes in v6:
time: 96.5 us; the launch traced here: 96.2 us
  starting transfers between devices  50.5 us (52%)
  Pallas kernels  21.3 us (22%)
  waiting for transfers between devices  17.7 us (18%)
  local copies, waits for them, and re-layouts  5.84 us (6%)
    ppermute x17, starting transfers between devices, swap(): return lax.ppermute(array, axis, [(i, i ^ bits) for i in range(count)])  36.8 us
    ppermute x17, waiting for transfers between devices, swap(): return lax.ppermute(array, axis, [(i, i ^ bits) for i in range(count)])  15.5 us
    ppermute x2, starting transfers between devices, beyond(): lax.ppermute(array, 'shard', [(i, (i + step(i)) % SHARDS) for i in range(...  10 us
    unnamed x22, local copies, waits for them, and re-layouts  5.84 us
    pallas_call x1, Pallas kernels, on_device(): call(backward_kernel, [shape(WIDTH, 4 * TILE)], [SMEM] + [VMEM] * 21, [pl...  4.58 us
    pallas_call x1, Pallas kernels, on_device(): call(latent_kernel, [shape(NODES, WIDTH, kind=F32), shape(NODES, WIDTH),...  4.09 us
    all_to_all x1, starting transfers between devices, on_device(): lax.all_to_all(grads.reshape(SHARDS // 2, 2 * NODES, 4 * TILE), 'shard',...  3.66 us
    pallas_call x2, Pallas kernels, on_device(): call(tables_kernel, [shape(WIDTH, HALF * WIDE), shape(HALF * BOTH, ROWS),...  3.31 us
  transfers between devices with their start and end apart: 20, of which 8 were waited for; matrix products, arithmetic and copies ran while one was open for 0% of the time, Pallas kernels for 12%

profile of v6, /device:TPU:1, one launch (start us, length us, event | category | flops | bytes accessed | tf_op | source)
XLA Modules:
  0.0 96.2 jit_solution(6185660387966876269)
XLA Ops:
  0.6 7.8 %collective-permute-start.1 = (bf16[32,1024]{1,0:T(8,128)(2,1)}, bf16[32,1024]{1,0:T(8,128)(2,1)S(1)}, u32[]{:S(2)}, u32[]{:S(2)}) collective-permute-start(bf16[32,1024]{1,0:T(8,128)(2,1)} %bitcast.14), channel_id=1, source_target_pairs={{0,1},{1,0},{2,3},{3,2},{4,5},{5,4},{6,7},{7,6},{8,9},{9,8},{10,11... | collective-permute-start | bytes 196616 | tf_op jit(solution)/shard_map/ppermute | solution.py:438
  8.5 4.7 %collective-permute-start = (bf16[32,1024]{1,0:T(8,128)(2,1)}, bf16[32,1024]{1,0:T(8,128)(2,1)S(1)}, u32[]{:S(2)}, u32[]{:S(2)}) collective-permute-start(bf16[32,1024]{1,0:T(8,128)(2,1)} %bitcast.15), channel_id=1, source_target_pairs={{0,31},{1,2},{2,1},{3,4},{4,3},{5,6},{6,5},{7,8},{8,7},{9,10},{10,... | collective-permute-start | bytes 196616 | tf_op jit(solution)/shard_map/ppermute | solution.py:443
  13.3 1.6 %copy-done.7 = bf16[1024,1024]{1,0:T(8,128)(2,1)S(1)} copy-done((bf16[1024,1024]{1,0:T(8,128)(2,1)S(1)}, bf16[1024,1024]{1,0:T(8,128)(2,1)}, u32[]{:S(2)}) %copy-start.7) | copy-done | bytes 2097176
  17.4 2.8 %collective-permute-start.4 = (bf16[32,1024]{1,0:T(8,128)(2,1)S(1)}, bf16[32,1024]{1,0:T(8,128)(2,1)S(1)}, u32[]{:S(2)}, u32[]{:S(2)}) collective-permute-start(bf16[32,1024]{1,0:T(8,128)(2,1)S(1)} %bitcast.16), channel_id=1, source_target_pairs={{0,192},{32,224},{64,128},{96,160},{128,64},{160,96},{192,0},{224,... | collective-permute-start | bytes 196616 | tf_op jit(solution)/shard_map/ppermute | solution.py:438
  21.0 2.7 %collective-permute-start.7 = (bf16[32,1024]{1,0:T(8,128)(2,1)S(1)}, bf16[32,1024]{1,0:T(8,128)(2,1)S(1)}, u32[]{:S(2)}, u32[]{:S(2)}) collective-permute-start(bf16[32,1024]{1,0:T(8,128)(2,1)S(1)} %collective-permute-done.1.partner.refs_4_), channel_id=1, source_target_pairs={{0,192},{32,224},{64,128},{96,160},{128,64},{160,96},{192,0},{224,... | collective-permute-start | bytes 196616 | tf_op jit(solution)/shard_map/ppermute | solution.py:438
  23.7 2.6 %shard_map.120 = (bf16[64,1024]{1,0:T(8,128)(2,1)S(1)}, bf16[8,192,256]{2,1,0:T(8,128)(2,1)S(1)}, bf16[1024,256]{1,0:T(8,128)(2,1)S(1)}, bf16[96,2048]{1,0:T(8,128)(2,1)S(1)}) custom-call(s32[2]{0:T(128)S(1)} %pad_add_fusion.me.refs_0_, bf16[32,1024]{1,0:T(8,128)(2,1)S(1)} %bitcast.19, bf16[32,1024]{1,0:T(8,128)(2,1)S(1)} %collective-permute-done.1.partner.refs_4_, ...), custom_call_target="tpu_custom_call" | custom-call | tf_op jit(solution)/shard_map/pallas_call | solution.py:492
  27.0 1.8 %collective-permute-start.10 = (bf16[64,1024]{1,0:T(8,128)(2,1)S(1)}, bf16[64,1024]{1,0:T(8,128)(2,1)S(1)}, u32[]{:S(2)}, u32[]{:S(2)}) collective-permute-start(bf16[64,1024]{1,0:T(8,128)(2,1)S(1)} %get-tuple-element.83.refs_8_), channel_id=1, source_target_pairs={{0,192},{32,224},{64,128},{96,160},{128,64},{160,96},{192,0},{224,... | collective-permute-start | bytes 393224 | tf_op jit(solution)/shard_map/ppermute | solution.py:438
  28.8 1.7 %collective-permute-start.8 = (bf16[64,1024]{1,0:T(8,128)(2,1)S(1)}, bf16[64,1024]{1,0:T(8,128)(2,1)S(1)}, u32[]{:S(2)}, u32[]{:S(2)}) collective-permute-start(bf16[64,1024]{1,0:T(8,128)(2,1)S(1)} %get-tuple-element.83.refs_8_), channel_id=1, source_target_pairs={{0,64},{32,96},{64,0},{96,32},{128,192},{160,224},{192,128},{224,1... | collective-permute-start | bytes 393224 | tf_op jit(solution)/shard_map/ppermute | solution.py:438
  32.6 10.2 %collective-permute-done.6.refs_6_ = bf16[32,1024]{1,0:T(8,128)(2,1)S(1)} collective-permute-done((bf16[32,1024]{1,0:T(8,128)(2,1)S(1)}, bf16[32,1024]{1,0:T(8,128)(2,1)S(1)}, u32[]{:S(2)}, u32[]{:S(2)}) %collective-permute-start.6) | collective-permute-done | bytes 65568 | tf_op jit(solution)/shard_map/ppermute | solution.py:438
  44.5 1.7 %shard_map.122 = (bf16[1024,384]{1,0:T(8,128)(2,1)S(1)}, bf16[768,256]{1,0:T(8,128)(2,1)S(1)}, bf16[768,128]{1,0:T(8,128)(2,1)S(1)}, f32[384,128]{1,0:T(8,128)S(...) custom-call(s32[2]{0:T(128)S(1)} %pad_add_fusion.me.refs_0_, ...), custom_call_target="tpu_custom_call" | custom-call | flops 1073741824 | bytes 4194304 | tf_op jit(solution)/shard_map/pallas_call | solution.py:516
  46.8 1.7 %shard_map.123 = (bf16[1024,384]{1,0:T(8,128)(2,1)S(1)}, bf16[768,256]{1,0:T(8,128)(2,1)S(1)}, bf16[768,128]{1,0:T(8,128)(2,1)S(1)}, f32[384,128]{1,0:T(8,128)S(...) custom-call(s32[2]{0:T(128)S(1)} %pad_add_fusion.me.refs_0_, ...), custom_call_target="tpu_custom_call" | custom-call | flops 1073741824 | bytes 4194304 | tf_op jit(solution)/shard_map/pallas_call | solution.py:516
  48.5 1.8 %shard_map.124 = (bf16[128,2048]{1,0:T(8,128)(2,1)S(1)}, bf16[128,256]{1,0:T(8,128)(2,1)S(1)}, f32[1,1]{1,0:T(1,128)}, f32[16,256]{1,0:T(8,128)S(1)}) custom-call(bf16[4,128,1024]{2,1,0:T(8,128)(2,1)S(1)} %shard_map.121.stack.mine.refs_20_, bf16[4,128,1024]{2,1,0:T(8,128)(2,1)S(1)} %collective-permute-done.11.stack.theirs.refs_21_, f32[100,256]{1,0:T(8,128)S(1)} %bitcast.21, ...), custom_call_target="tpu_custom_call" | custom-call | tf_op jit(solution)/shard_map/pallas_call | solution.py:505
  50.3 4.6 %shard_map.125 = bf16[1024,512]{1,0:T(8,128)(2,1)} custom-call(s32[2]{0:T(128)S(1)} %pad_add_fusion.me.refs_0_, bf16[1024,384]{1,0:T(8,128)(2,1)S(1)} %get-tuple-element.86.refs_1_, bf16[768,256]{1,0:T(8,128)(2,1)S(1)} %get-tuple-element.87.refs_2_, bf16[768,128]{1,0:T(8,128)(2,1)S(1)} %get-tuple-element.88.refs_3_, ...), custom_call_target="tpu_custom_call" | custom-call | flops 2147483648 | bytes 8388608 | tf_op jit(solution)/shard_map/pallas_call | solution.py:532
  54.9 3.7 %all-to-all-start = ((bf16[16,64,512]{2,1,0:T(8,128)(2,1)}), bf16[16,64,512]{2,1,0:T(8,128)(2,1)S(1)}, u32[]{:S(2)}, u32[]{:S(2)}) async-start(bf16[16,64,512]{2,1,0:T(8,128)(2,1)} %bitcast.7), calls=%async_computation | async-start | bytes 2097152 | tf_op jit(solution)/shard_map/all_to_all | solution.py:551
  58.6 2.2 %copy-done.1 = bf16[1024,2048]{1,0:T(8,128)(2,1)S(1)} copy-done((bf16[1024,2048]{1,0:T(8,128)(2,1)S(1)}, bf16[1024,2048]{1,0:T(8,128)(2,1)}, u32[]{:S(2)}) %copy-start.1) | copy-done | bytes 4194328
  61.7 4.1 %shard_map.126 = (f32[32,1024]{1,0:T(8,128)S(1)}, bf16[32,1024]{1,0:T(8,128)(2,1)S(1)}, bf16[32,1024]{1,0:T(8,128)(2,1)S(1)}) custom-call(bf16[128,256]{1,0:T(8,128)(2,1)S(1)} %get-tuple-element.102.d_own, bf16[8,192,256]{2,1,0:T(8,128)(2,1)S(1)} %get-tuple-element.103.weights, bf16[1024,256]{1,0:T(8,128)(2,1)S(1)} %get-tuple-element.104.normed, ...), custom_call_target="tpu_custom_call" | custom-call | flops 17179869184 | bytes 8388608 | tf_op jit(solution)/shard_map/pallas_call | solution.py:558
  65.8 4.5 %collective-permute-start.13 = (bf16[32,1024]{1,0:T(8,128)(2,1)S(1)}, bf16[32,1024]{1,0:T(8,128)(2,1)S(1)}, u32[]{:S(2)}, u32[]{:S(2)}) collective-permute-start(bf16[32,1024]{1,0:T(8,128)(2,1)S(1)} %get-tuple-element.110), channel_id=1, source_target_pairs={{0,1},{1,0},{2,3},{3,2},{4,5},{5,4},{6,7},{7,6},{8,9},{9,8},{10,11... | collective-permute-start | bytes 196616 | tf_op jit(solution)/shard_map/ppermute | solution.py:438
  70.4 5.3 %collective-permute-start.14 = (bf16[32,1024]{1,0:T(8,128)(2,1)S(1)}, bf16[32,1024]{1,0:T(8,128)(2,1)S(1)}, u32[]{:S(2)}, u32[]{:S(2)}) collective-permute-start(bf16[32,1024]{1,0:T(8,128)(2,1)S(1)} %get-tuple-element.111), channel_id=1, source_target_pairs={{0,31},{1,2},{2,1},{3,4},{4,3},{5,6},{6,5},{7,8},{8,7},{9,10},{10,... | collective-permute-start | bytes 196616 | tf_op jit(solution)/shard_map/ppermute | solution.py:443
  76.4 3.1 %collective-permute-start.12 = (bf16[32,512]{1,0:T(8,128)(2,1)S(1)}, bf16[32,512]{1,0:T(8,128)(2,1)S(1)}, u32[]{:S(2)}, u32[]{:S(2)}) collective-permute-start(bf16[32,512]{1,0:T(8,128)(2,1)S(1)} %get-tuple-element.109), channel_id=1, source_target_pairs={{0,1},{1,0},{2,3},{3,2},{4,5},{5,4},{6,7},{7,6},{8,9},{9,8},{10,11... | collective-permute-start | bytes 98312 | tf_op jit(solution)/shard_map/ppermute | solution.py:438
  79.5 2.2 %collective-permute-done.14.far = bf16[32,1024]{1,0:T(8,128)(2,1)S(1)} collective-permute-done((bf16[32,1024]{1,0:T(8,128)(2,1)S(1)}, bf16[32,1024]{1,0:T(8,128)(2,1)S(1)}, u32[]{:S(2)}, u32[]{:S(2)}) %collective-permute-start.14) | collective-permute-done | bytes 65568 | tf_op jit(solution)/shard_map/ppermute | solution.py:443
  81.6 1.7 %collective-permute-done.12.came = bf16[32,512]{1,0:T(8,128)(2,1)S(1)} collective-permute-done((bf16[32,512]{1,0:T(8,128)(2,1)S(1)}, bf16[32,512]{1,0:T(8,128)(2,1)S(1)}, u32[]{:S(2)}, u32[]{:S(2)}) %collective-permute-start.12) | collective-permute-done | bytes 32800 | tf_op jit(solution)/shard_map/ppermute | solution.py:438
  83.9 2.0 %collective-permute-start.17 = (bf16[32,512]{1,0:T(8,128)(2,1)S(1)}, bf16[32,512]{1,0:T(8,128)(2,1)S(1)}, u32[]{:S(2)}, u32[]{:S(2)}) collective-permute-start(bf16[32,512]{1,0:T(8,128)(2,1)S(1)} %get-tuple-element.117.refs_0_), channel_id=1, source_target_pairs={{0,192},{32,224},{64,128},{96,160},{128,64},{160,96},{192,0},{224,... | collective-permute-start | bytes 98312 | tf_op jit(solution)/shard_map/ppermute | solution.py:438
  85.9 1.6 %collective-permute-start.15 = (bf16[32,512]{1,0:T(8,128)(2,1)S(1)}, bf16[32,512]{1,0:T(8,128)(2,1)S(1)}, u32[]{:S(2)}, u32[]{:S(2)}) collective-permute-start(bf16[32,512]{1,0:T(8,128)(2,1)S(1)} %get-tuple-element.117.refs_0_), channel_id=1, source_target_pairs={{0,64},{32,96},{64,0},{96,32},{128,192},{160,224},{192,128},{224,1... | collective-permute-start | bytes 98312 | tf_op jit(solution)/shard_map/ppermute | solution.py:438
  89.6 4.3 %collective-permute-start.18 = (bf16[4,32,512]{2,1,0:T(8,128)(2,1)S(1)}, bf16[4,32,512]{2,1,0:T(8,128)(2,1)S(1)}, u32[]{:S(2)}, u32[]{:S(2)}) collective-permute-start(bf16[4,32,512]{2,1,0:T(8,128)(2,1)S(1)} %shard_map.130.mine), channel_id=1, source_target_pairs={{0,32},{32,0},{64,96},{96,64},{128,160},{160,128},{192,224},{224,1... | collective-permute-start | bytes 393224 | tf_op jit(solution)/shard_map/ppermute | solution.py:438
  (52 shorter events, 15.1 us)
Async XLA Ops:
  0.6 20.4 %collective-permute-start.1 = (bf16[32,1024]{1,0:T(8,128)(2,1)}, bf16[32,1024]{1,0:T(8,128)(2,1)S(1)}, u32[]{:S(2)}, u32[]{:S(2)}) collective-permute-start(bf16[32,1024]{1,0:T(8,128)(2,1)} %bitcast.14), channel_id=1, source_target_pairs={{0,1},{1,0},{2,3},{3,2},{4,5},{5,4},{6,7},{7,6},{8,9},{9,8},{10,11... | collective-permute-start | bytes 196616 | tf_op jit(solution)/shard_map/ppermute | solution.py:438
  8.5 12.6 %collective-permute-start = (bf16[32,1024]{1,0:T(8,128)(2,1)}, bf16[32,1024]{1,0:T(8,128)(2,1)S(1)}, u32[]{:S(2)}, u32[]{:S(2)}) collective-permute-start(bf16[32,1024]{1,0:T(8,128)(2,1)} %bitcast.15), channel_id=1, source_target_pairs={{0,31},{1,2},{2,1},{3,4},{4,3},{5,6},{6,5},{7,8},{8,7},{9,10},{10,... | collective-permute-start | bytes 196616 | tf_op jit(solution)/shard_map/ppermute | solution.py:443
  15.9 7.8 %copy-start = (bf16[1024,2048]{1,0:T(8,128)(2,1)S(1)}, bf16[1024,2048]{1,0:T(8,128)(2,1)}, u32[]{:S(2)}) copy-start(bf16[1024,2048]{1,0:T(8,128)(2,1)} %w_keyval.7) | copy-start | bytes 12582916
  15.9 7.8 %copy-start.2 = (bf16[1024,100]{0,1:T(8,128)(2,1)S(1)}, bf16[1024,100]{0,1:T(8,128)(2,1)}, u32[]{:S(2)}) copy-start(bf16[1024,100]{0,1:T(8,128)(2,1)} %param.15) | copy-start | bytes 614404
  15.9 7.8 %copy-start.5 = (s32[256,3]{0,1:T(4,128)S(1)}, s32[256,3]{0,1:T(4,128)}, u32[]{:S(2)}) copy-start(s32[256,3]{0,1:T(4,128)} %param.10) | copy-start | bytes 9220
  17.4 9.0 %collective-permute-start.4 = (bf16[32,1024]{1,0:T(8,128)(2,1)S(1)}, bf16[32,1024]{1,0:T(8,128)(2,1)S(1)}, u32[]{:S(2)}, u32[]{:S(2)}) collective-permute-start(bf16[32,1024]{1,0:T(8,128)(2,1)S(1)} %bitcast.16), channel_id=1, source_target_pairs={{0,192},{32,224},{64,128},{96,160},{128,64},{160,96},{192,0},{224,... | collective-permute-start | bytes 196616 | tf_op jit(solution)/shard_map/ppermute | solution.py:438
  20.2 6.8 %collective-permute-start.3 = (bf16[32,1024]{1,0:T(8,128)(2,1)S(1)}, bf16[32,1024]{1,0:T(8,128)(2,1)S(1)}, u32[]{:S(2)}, u32[]{:S(2)}) collective-permute-start(bf16[32,1024]{1,0:T(8,128)(2,1)S(1)} %bitcast.17), channel_id=1, source_target_pairs={{0,128},{32,160},{64,192},{96,224},{128,0},{160,32},{192,64},{224,... | collective-permute-start | bytes 196616 | tf_op jit(solution)/shard_map/ppermute | solution.py:438
  20.2 6.8 %collective-permute-start.2 = (bf16[32,1024]{1,0:T(8,128)(2,1)S(1)}, bf16[32,1024]{1,0:T(8,128)(2,1)S(1)}, u32[]{:S(2)}, u32[]{:S(2)}) collective-permute-start(bf16[32,1024]{1,0:T(8,128)(2,1)S(1)} %bitcast.18), channel_id=1, source_target_pairs={{0,64},{32,96},{64,0},{96,32},{128,192},{160,224},{192,128},{224,1... | collective-permute-start | bytes 196616 | tf_op jit(solution)/shard_map/ppermute | solution.py:438
  21.0 10.2 %collective-permute-start.7 = (bf16[32,1024]{1,0:T(8,128)(2,1)S(1)}, bf16[32,1024]{1,0:T(8,128)(2,1)S(1)}, u32[]{:S(2)}, u32[]{:S(2)}) collective-permute-start(bf16[32,1024]{1,0:T(8,128)(2,1)S(1)} %collective-permute-done.1.partner.refs_4_), channel_id=1, source_target_pairs={{0,192},{32,224},{64,128},{96,160},{128,64},{160,96},{192,0},{224,... | collective-permute-start | bytes 196616 | tf_op jit(solution)/shard_map/ppermute | solution.py:438
  26.4 22.1 %copy-start.9 = (bf16[96,2048]{1,0:T(8,128)(2,1)}, bf16[96,2048]{1,0:T(8,128)(2,1)S(1)}, u32[]{:S(2)}) copy-start(bf16[96,2048]{1,0:T(8,128)(2,1)S(1)} %get-tuple-element.105.table) | copy-start | bytes 1179652
  27.0 15.9 %collective-permute-start.10 = (bf16[64,1024]{1,0:T(8,128)(2,1)S(1)}, bf16[64,1024]{1,0:T(8,128)(2,1)S(1)}, u32[]{:S(2)}, u32[]{:S(2)}) collective-permute-start(bf16[64,1024]{1,0:T(8,128)(2,1)S(1)} %get-tuple-element.83.refs_8_), channel_id=1, source_target_pairs={{0,192},{32,224},{64,128},{96,160},{128,64},{160,96},{192,0},{224,... | collective-permute-start | bytes 393224 | tf_op jit(solution)/shard_map/ppermute | solution.py:438
  28.8 14.1 %collective-permute-start.9 = (bf16[64,1024]{1,0:T(8,128)(2,1)S(1)}, bf16[64,1024]{1,0:T(8,128)(2,1)S(1)}, u32[]{:S(2)}, u32[]{:S(2)}) collective-permute-start(bf16[64,1024]{1,0:T(8,128)(2,1)S(1)} %get-tuple-element.83.refs_8_), channel_id=1, source_target_pairs={{0,128},{32,160},{64,192},{96,224},{128,0},{160,32},{192,64},{224,... | collective-permute-start | bytes 393224 | tf_op jit(solution)/shard_map/ppermute | solution.py:438
  28.8 14.1 %collective-permute-start.8 = (bf16[64,1024]{1,0:T(8,128)(2,1)S(1)}, bf16[64,1024]{1,0:T(8,128)(2,1)S(1)}, u32[]{:S(2)}, u32[]{:S(2)}) collective-permute-start(bf16[64,1024]{1,0:T(8,128)(2,1)S(1)} %get-tuple-element.83.refs_8_), channel_id=1, source_target_pairs={{0,64},{32,96},{64,0},{96,32},{128,192},{160,224},{192,128},{224,1... | collective-permute-start | bytes 393224 | tf_op jit(solution)/shard_map/ppermute | solution.py:438
  30.5 12.3 %collective-permute-start.6 = (bf16[32,1024]{1,0:T(8,128)(2,1)S(1)}, bf16[32,1024]{1,0:T(8,128)(2,1)S(1)}, u32[]{:S(2)}, u32[]{:S(2)}) collective-permute-start(bf16[32,1024]{1,0:T(8,128)(2,1)S(1)} %collective-permute-done.1.partner.refs_4_), channel_id=1, source_target_pairs={{0,128},{32,160},{64,192},{96,224},{128,0},{160,32},{192,64},{224,... | collective-permute-start | bytes 196616 | tf_op jit(solution)/shard_map/ppermute | solution.py:438
  31.2 11.7 %collective-permute-start.5 = (bf16[32,1024]{1,0:T(8,128)(2,1)S(1)}, bf16[32,1024]{1,0:T(8,128)(2,1)S(1)}, u32[]{:S(2)}, u32[]{:S(2)}) collective-permute-start(bf16[32,1024]{1,0:T(8,128)(2,1)S(1)} %collective-permute-done.1.partner.refs_4_), channel_id=1, source_target_pairs={{0,64},{32,96},{64,0},{96,32},{128,192},{160,224},{192,128},{224,1... | collective-permute-start | bytes 196616 | tf_op jit(solution)/shard_map/ppermute | solution.py:438
  43.0 3.8 %collective-permute-start.11 = (bf16[4,128,1024]{2,1,0:T(8,128)(2,1)S(1)}, bf16[4,128,1024]{2,1,0:T(8,128)(2,1)S(1)}, u32[]{:S(2)}, u32[]{:S(2)}) collective-permute-start(bf16[4,128,1024]{2,1,0:T(8,128)(2,1)S(1)} %shard_map.121.stack.mine.refs_20_), channel_id=1, source_target_pairs={{0,32},{32,0},{64,96},{96,64},{128,160},{160,128},{192,224},{224,1... | collective-permute-start | bytes 3145736 | tf_op jit(solution)/shard_map/ppermute | solution.py:438
  54.9 20.8 %all-to-all-start = ((bf16[16,64,512]{2,1,0:T(8,128)(2,1)}), bf16[16,64,512]{2,1,0:T(8,128)(2,1)S(1)}, u32[]{:S(2)}, u32[]{:S(2)}) async-start(bf16[16,64,512]{2,1,0:T(8,128)(2,1)} %bitcast.7), calls=%async_computation | async-start | bytes 2097152 | tf_op jit(solution)/shard_map/all_to_all | solution.py:551
  65.8 13.6 %collective-permute-start.13 = (bf16[32,1024]{1,0:T(8,128)(2,1)S(1)}, bf16[32,1024]{1,0:T(8,128)(2,1)S(1)}, u32[]{:S(2)}, u32[]{:S(2)}) collective-permute-start(bf16[32,1024]{1,0:T(8,128)(2,1)S(1)} %get-tuple-element.110), channel_id=1, source_target_pairs={{0,1},{1,0},{2,3},{3,2},{4,5},{5,4},{6,7},{7,6},{8,9},{9,8},{10,11... | collective-permute-start | bytes 196616 | tf_op jit(solution)/shard_map/ppermute | solution.py:438
  70.4 11.3 %collective-permute-start.14 = (bf16[32,1024]{1,0:T(8,128)(2,1)S(1)}, bf16[32,1024]{1,0:T(8,128)(2,1)S(1)}, u32[]{:S(2)}, u32[]{:S(2)}) collective-permute-start(bf16[32,1024]{1,0:T(8,128)(2,1)S(1)} %get-tuple-element.111), channel_id=1, source_target_pairs={{0,31},{1,2},{2,1},{3,4},{4,3},{5,6},{6,5},{7,8},{8,7},{9,10},{10,... | collective-permute-start | bytes 196616 | tf_op jit(solution)/shard_map/ppermute | solution.py:443
  76.4 6.9 %collective-permute-start.12 = (bf16[32,512]{1,0:T(8,128)(2,1)S(1)}, bf16[32,512]{1,0:T(8,128)(2,1)S(1)}, u32[]{:S(2)}, u32[]{:S(2)}) collective-permute-start(bf16[32,512]{1,0:T(8,128)(2,1)S(1)} %get-tuple-element.109), channel_id=1, source_target_pairs={{0,1},{1,0},{2,3},{3,2},{4,5},{5,4},{6,7},{7,6},{8,9},{9,8},{10,11... | collective-permute-start | bytes 98312 | tf_op jit(solution)/shard_map/ppermute | solution.py:438
  83.9 4.6 %collective-permute-start.17 = (bf16[32,512]{1,0:T(8,128)(2,1)S(1)}, bf16[32,512]{1,0:T(8,128)(2,1)S(1)}, u32[]{:S(2)}, u32[]{:S(2)}) collective-permute-start(bf16[32,512]{1,0:T(8,128)(2,1)S(1)} %get-tuple-element.117.refs_0_), channel_id=1, source_target_pairs={{0,192},{32,224},{64,128},{96,160},{128,64},{160,96},{192,0},{224,... | collective-permute-start | bytes 98312 | tf_op jit(solution)/shard_map/ppermute | solution.py:438
  85.9 3.7 %collective-permute-start.16 = (bf16[32,512]{1,0:T(8,128)(2,1)S(1)}, bf16[32,512]{1,0:T(8,128)(2,1)S(1)}, u32[]{:S(2)}, u32[]{:S(2)}) collective-permute-start(bf16[32,512]{1,0:T(8,128)(2,1)S(1)} %get-tuple-element.117.refs_0_), channel_id=1, source_target_pairs={{0,128},{32,160},{64,192},{96,224},{128,0},{160,32},{192,64},{224,... | collective-permute-start | bytes 98312 | tf_op jit(solution)/shard_map/ppermute | solution.py:438
  85.9 3.7 %collective-permute-start.15 = (bf16[32,512]{1,0:T(8,128)(2,1)S(1)}, bf16[32,512]{1,0:T(8,128)(2,1)S(1)}, u32[]{:S(2)}, u32[]{:S(2)}) collective-permute-start(bf16[32,512]{1,0:T(8,128)(2,1)S(1)} %get-tuple-element.117.refs_0_), channel_id=1, source_target_pairs={{0,64},{32,96},{64,0},{96,32},{128,192},{160,224},{192,128},{224,1... | collective-permute-start | bytes 98312 | tf_op jit(solution)/shard_map/ppermute | solution.py:438
  89.6 5.2 %collective-permute-start.18 = (bf16[4,32,512]{2,1,0:T(8,128)(2,1)S(1)}, bf16[4,32,512]{2,1,0:T(8,128)(2,1)S(1)}, u32[]{:S(2)}, u32[]{:S(2)}) collective-permute-start(bf16[4,32,512]{2,1,0:T(8,128)(2,1)S(1)} %shard_map.130.mine), channel_id=1, source_target_pairs={{0,32},{32,0},{64,96},{96,64},{128,160},{160,128},{192,224},{224,1... | collective-permute-start | bytes 393224 | tf_op jit(solution)/shard_map/ppermute | solution.py:438
  (7 other events, 18.3 us)
